TPU v7x, 32 devices: a whole 2x2x4 slice. The times are simulated.
32 devices in a mesh: kv: 2 (over y), pb: 4 (over x, core), head: 4 (over z).
Axes of the slice: x: 2, y: 2, z: 4, core: 2. Of those that a mesh axis runs over, the one named last changes fastest.
Arguments:
- queries: bfloat16 [8192, 8192], P(('kv', 'pb', 'head')), may hold values from -20 to 20
- key_rows: bfloat16 [8192, 1024], P(('kv', 'pb', 'head')), may hold values from -5 to 5
- value_rows: bfloat16 [8192, 1024], P(('kv', 'pb', 'head')), may hold values from -6 to 6
- tile_lists: int32 [64, 8], P(('kv', 'pb')), may hold values from 0 to 63, as said below
Outputs:
- attended: bfloat16 [8192, 8192], P(('kv', 'pb', 'head'))
Inputs may be any that keep to these rules, and one draw needn't show every extreme that they name: `tile_lists`: row i names min(i + 1, 8) distinct tiles in its first slots, all at most i, the first of them i itself; its other slots hold 0.
All inputs are finite; a program needn't handle non-finite values.
Results may differ from a plain program's by a relative error of at most 0.0042.
Values may be sent and summed in bfloat16 or wider, within the bound.
No kernel may reach another device: no remote copies, remote signals or barrier semaphores. Data moves between devices by JAX's collectives and lax.ppermute only.
A program may use at most 128 MiB of HBM per device.

v0:
```python
import jax
import jax.numpy as jnp
from jax import lax
from jax.sharding import PartitionSpec as P

HEADS = 64
KV_HEADS = 8
HEAD_DIM = 128
TILE = 128
SLOTS = 8


NEG = -1e30


def tile_partial(query_tile, key_tiles, value_tiles, allowed, scaling):
    scores = (
        jnp.einsum("tkgd,jskd->tkgjs", query_tile, key_tiles, preferred_element_type=jnp.float32)
        * scaling
    )
    scores = jnp.where(allowed[:, None, None, :, :], scores, NEG)
    tile_max = jnp.max(scores, axis=-1)
    weights = jnp.exp(scores - tile_max[..., None])
    tile_sum = jnp.sum(weights, axis=-1)
    rounded = weights.astype(jnp.bfloat16)
    tile_out = jnp.einsum(
        "tkgjs,jskd->tkgjd", rounded, value_tiles, preferred_element_type=jnp.float32
    )
    return (tile_max, tile_sum, tile_out)


def combine_slots(tile_max, tile_sum, tile_out, usable):
    masked = jnp.where(usable, tile_max, NEG)
    overall = jnp.max(masked, axis=-1, keepdims=True)
    factor = jnp.exp(masked - overall)
    run_sum = jnp.sum(factor * tile_sum, axis=-1)
    run_out = jnp.sum(factor[..., None] * tile_out, axis=-2)
    return run_out / run_sum[..., None]


def per_device(queries, key_rows, value_rows, tile_lists):
    query_local, key_local, value_local = (
        lax.all_to_all(queries, "head", split_axis=1, concat_axis=0, tiled=True),
        lax.all_to_all(key_rows, "head", split_axis=1, concat_axis=0, tiled=True),
        lax.all_to_all(value_rows, "head", split_axis=1, concat_axis=0, tiled=True),
    )
    tokens = query_local.shape[0]
    key_heads = key_local.shape[1] // HEAD_DIM
    groups = HEADS // KV_HEADS
    tiles_here = tokens // TILE
    scaling = HEAD_DIM ** (-0.5)
    query_grid = query_local.reshape(tiles_here, TILE, key_heads, groups, HEAD_DIM)
    own_tile = lax.axis_index(("kv", "pb")) * tiles_here
    all_keys, all_values = (
        lax.all_gather(key_local, ("kv", "pb"), axis=0, tiled=True),
        lax.all_gather(value_local, ("kv", "pb"), axis=0, tiled=True),
    )
    key_grid = all_keys.reshape(-1, TILE, key_heads, HEAD_DIM)
    value_grid = all_values.reshape(-1, TILE, key_heads, HEAD_DIM)
    within = jnp.arange(TILE, dtype=jnp.int32)
    slot_order = jnp.arange(SLOTS, dtype=jnp.int32)

    def one_tile(local_index):
        listed = tile_lists[local_index]
        tile_index = own_tile + local_index
        key_tiles = jnp.take(key_grid, listed, axis=0)
        value_tiles = jnp.take(value_grid, listed, axis=0)
        query_position = tile_index * TILE + within
        key_position = listed[:, None] * TILE + within[None, :]
        allowed = key_position[None, :, :] <= query_position[:, None, None]
        usable = slot_order < jnp.minimum(tile_index + 1, SLOTS)
        tile_max, tile_sum, tile_out = tile_partial(
            query_grid[local_index], key_tiles, value_tiles, allowed, scaling
        )
        return combine_slots(tile_max, tile_sum, tile_out, usable).astype(jnp.bfloat16)

    result = lax.map(one_tile, jnp.arange(tiles_here, dtype=jnp.int32))
    result = result.reshape(tokens, key_heads * groups * HEAD_DIM)
    return lax.all_to_all(result, "head", split_axis=0, concat_axis=1, tiled=True)


def solution(mesh):
    in_specs = (
        P(("kv", "pb", "head"), None),
        P(("kv", "pb", "head"), None),
        P(("kv", "pb", "head"), None),
        P(("kv", "pb"), None),
    )
    out_specs = P(("kv", "pb", "head"), None)
    return jax.shard_map(
        per_device, mesh=mesh, in_specs=in_specs, out_specs=out_specs, check_vma=False
    )
```

profile of v0, /device:TPU:17, one launch (start us, length us, event | category | flops | bytes accessed | tf_op | source)
XLA Modules:
  0.0 475.4 jit_solution(11025487369437258014)
XLA Ops:
  8.0 16.1 %all_to_all.73 = bf16[256,4,256]{2,0,1:T(8,128)(2,1)} all-to-all(bf16[256,4,256]{2,0,1:T(8,128)(2,1)S(1)} %copy.29), channel_id=1, replica_groups=mesh['kv'=2,'pb'=4,'head'=4] {'head'}, dimensions={1} | all-to-all | bytes 1048576 | tf_op jit(solution)/shard_map/all_to_all | solution.py:44
  25.6 16.5 %all_to_all.74 = bf16[256,4,256]{2,0,1:T(8,128)(2,1)} all-to-all(bf16[256,4,256]{2,0,1:T(8,128)(2,1)S(1)} %copy.32), channel_id=1, replica_groups=mesh['kv'=2,'pb'=4,'head'=4] {'head'}, dimensions={1} | all-to-all | bytes 1048576 | tf_op jit(solution)/shard_map/all_to_all | solution.py:45
  42.1 4.7 copy.61
  46.8 7.1 %all-to-all-start.1 = ((bf16[256,4,2048]{2,0,1:T(8,128)(2,1)}), bf16[256,4,2048]{2,0,1:T(8,128)(2,1)}, u32[]{:S(2)}, u32[]{:S(2)}) async-start(bf16[256,4,2048]{2,0,1:T(8,128)(2,1)} %bitcast.79), calls=%async_computation.1 | async-start | bytes 8388608 | tf_op jit(solution)/shard_map/all_to_all | solution.py:43
  53.9 89.6 %all-to-all-done.1 = bf16[256,4,2048]{2,0,1:T(8,128)(2,1)} async-done(((bf16[256,4,2048]{2,0,1:T(8,128)(2,1)}), bf16[256,4,2048]{2,0,1:T(8,128)(2,1)}, u32[]{:S(2)}, u32[]{:S(2)}) %all-to-all-start.1) | async-done | bytes 4194336 | tf_op jit(solution)/shard_map/all_to_all | solution.py:43
  143.6 5.5 %copy.49 = bf16[128,8,16,128]{3,2,1,0:T(8,128)(2,1)} copy(bf16[128,8,16,128]{3,1,2,0:T(8,128)(2,1)} %bitcast.26) | data formatting | bytes 8388608
  149.1 6.9 %reshape.86 = bf16[64,128,2,128]{3,2,1,0:T(2,128)(2,1)} reshape(bf16[8192,256]{1,0:T(8,128)(2,1)} %all-gather.3.cloned.1.call-done) | data formatting | bytes 8388608 | tf_op jit(solution)/shard_map/reshape | solution.py:58
  156.0 6.9 %reshape.88 = bf16[64,128,2,128]{3,2,1,0:T(2,128)(2,1)} reshape(bf16[8192,256]{1,0:T(8,128)(2,1)} %all-gather.5.cloned.1.call-done) | data formatting | bytes 8388608 | tf_op jit(solution)/shard_map/reshape | solution.py:59
  163.0 186.8 %while.13 = (s32[]{:T(128)}, bf16[8,128,2,8,128]{4,3,2,1,0:T(8,128)(2,1)}, s32[8]{0:T(128)S(1)}, s32[]{:T(128)}, s32[8,8]{1,0:T(8,128)}, /*index=5*/bf16[64,128,...) while((s32[]{:T(128)}, ...), condition=%wide.region_6.8_spmd.clone.clone, body=%wide.region_0.7_spmd.clone.clone.sunk | while | flops 1101986048 | bytes 37861424 | solution.py:77
  166.7 3.8 gather_fusion
  170.5 3.8 gather_fusion.1
  181.7 3.2 fusion.35
  190.1 3.8 gather_fusion
  193.9 3.8 gather_fusion.1
  205.0 3.2 fusion.35
  213.4 3.8 gather_fusion
  217.2 3.8 gather_fusion.1
  228.4 3.2 fusion.35
  236.8 3.8 gather_fusion
  240.6 3.8 gather_fusion.1
  260.1 3.8 gather_fusion
  263.9 3.8 gather_fusion.1
  283.5 3.8 gather_fusion
  287.3 3.8 gather_fusion.1
  306.8 3.8 gather_fusion
  310.6 3.8 gather_fusion.1
  330.2 3.8 gather_fusion
  334.0 3.8 gather_fusion.1
  349.8 7.3 %all_to_all.65 = bf16[4,256,2048]{2,1,0:T(8,128)(2,1)} reshape(bf16[8,128,2,8,128]{4,3,2,1,0:T(8,128)(2,1)} %get-tuple-element.83) | data formatting | bytes 8388608 | tf_op jit(solution)/shard_map/all_to_all | solution.py:79
  357.1 99.0 %all_to_all.75 = bf16[4,256,2048]{2,1,0:T(8,128)(2,1)} all-to-all(bf16[4,256,2048]{2,1,0:T(8,128)(2,1)} %all_to_all.65), channel_id=1, replica_groups=mesh['kv'=2,'pb'=4,'head'=4] {'head'}, dimensions={0} | all-to-all | bytes 8388608 | tf_op jit(solution)/shard_map/all_to_all | solution.py:79
  456.0 6.2 %copy.35 = bf16[4,256,2048]{1,2,0:T(8,128)(2,1)} copy(bf16[4,256,2048]{2,1,0:T(8,128)(2,1)} %all_to_all.75) | data formatting | bytes 8388608 | tf_op jit(solution)/shard_map/all_to_all | solution.py:79
  462.2 6.3 %copy.36 = bf16[256,8192]{1,0:T(8,128)(2,1)} copy(bf16[256,8192]{0,1:T(8,128)(2,1)} %bitcast.80) | data formatting | bytes 8388608 | tf_op jit(solution)/shard_map/all_to_all | solution.py:79
  (145 shorter events, 99.4 us)
Async XLA Ops:
  6.5 142.6 %all-gather.3.cloned.1.call-start = ((), (), s32[]{:S(2)}) async-start(), calls=%async_computation.4 | async-start | bytes 4718592 | tf_op jit(solution)/shard_map/all_gather | solution.py:55
  24.1 131.9 %all-gather.5.cloned.1.call-start = ((), (), s32[]{:S(2)}) async-start(), calls=%async_computation.5 | async-start | bytes 4718592 | tf_op jit(solution)/shard_map/all_gather | solution.py:56
  46.8 96.7 %all-to-all-start.1 = ((bf16[256,4,2048]{2,0,1:T(8,128)(2,1)}), bf16[256,4,2048]{2,0,1:T(8,128)(2,1)}, u32[]{:S(2)}, u32[]{:S(2)}) async-start(bf16[256,4,2048]{2,0,1:T(8,128)(2,1)} %bitcast.79), calls=%async_computation.1 | async-start | bytes 8388608 | tf_op jit(solution)/shard_map/all_to_all | solution.py:43
Sparse Core Ops, SparseCore 0:
  24.2 39.2 all-gather.2
  65.4 36.7 all-gather.4
where the time goes:
time: 483 us; the launch traced here: 475 us
  blocking collectives  132 us (27%)
  local copies, waits for them, and re-layouts  131 us (27%)
  waiting for transfers between devices  89.7 us (19%)
  other arithmetic  44.4 us (9%)
  matrix products  38 us (8%)
  loops' own time  20.1 us (4%)
  between operations  13.4 us (3%)
  starting transfers between devices  7.13 us (1%)
    all_to_all x1, blocking collectives, per_device(): lax.all_to_all(result, 'head', split_axis=0, concat_axis=1, tiled=True)  99 us
    all_to_all x1, waiting for transfers between devices, per_device(): lax.all_to_all(queries, 'head', split_axis=1, concat_axis=0, tiled=True)  89.6 us
    gather x8, local copies, waits for them, and re-layouts, one_tile(): value_tiles = jnp.take(value_grid, listed, axis=0)  30.3 us
    gather x8, local copies, waits for them, and re-layouts, one_tile(): key_tiles = jnp.take(key_grid, listed, axis=0)  30.3 us
    dot_general x8, matrix products, tile_partial(): jnp.einsum('tkgjs,jskd->tkgjd', rounded, value_tiles, preferred_element_t...  25.7 us
    reduce_sum x8, other arithmetic, tile_partial(): tile_sum = jnp.sum(weights, axis=-1)  20.8 us
    another operation x1, loops' own time, per_device(): result = lax.map(one_tile, jnp.arange(tiles_here, dtype=jnp.int32))  20.1 us
    all_to_all x3, local copies, waits for them, and re-layouts, per_device(): lax.all_to_all(result, 'head', split_axis=0, concat_axis=1, tiled=True)  19.8 us
  transfers between devices with their start and end apart: 3, of which 1 were waited for; matrix products, arithmetic and copies ran while one was open for 4% of the time, Pallas kernels for 0%

commit v1 on v0

v1 whole, which is shorter than its diff:
```python
import functools

import jax
import jax.numpy as jnp
from jax import lax
from jax.experimental import pallas as pl
from jax.experimental.pallas import tpu as pltpu
from jax.sharding import PartitionSpec as P

HEADS = 64
KV_HEADS = 8
HEAD_DIM = 128
TILE = 128
SLOTS = 8

NEG = -1e30
GROUPS = HEADS // KV_HEADS
WIDE = GROUPS * HEAD_DIM
AXES = ("kv", "pb", "head")
LOG2 = HEAD_DIM ** (-0.5) * 1.4426950408889634


def attend_tile(masked, live, tile, loc_ref, q_buf, kv_buf, out_buf):
    listed = [kv_buf[loc_ref[tile * SLOTS + j]] for j in range(SLOTS)]
    keys = jnp.concatenate([block[:, :HEAD_DIM] for block in listed], axis=0)
    values = jnp.concatenate([block[:, HEAD_DIM:] for block in listed], axis=0)
    values = jnp.concatenate([values, jnp.ones_like(values)], axis=1)
    row = lax.broadcasted_iota(jnp.int32, (TILE, TILE), 0)
    column = lax.broadcasted_iota(jnp.int32, (TILE, TILE), 1)
    diagonal = jnp.where(column <= row, 0.0, NEG)
    for g in range(GROUPS):
        columns = slice(g * HEAD_DIM, (g + 1) * HEAD_DIM)
        scores = lax.dot_general(
            q_buf[tile, :, columns], keys, (((1,), (1,)), ((), ())),
            preferred_element_type=jnp.float32,
        )
        parts = [scores[:, :TILE] + diagonal]
        if masked:
            for j in range(1, SLOTS):
                part = scores[:, j * TILE:(j + 1) * TILE]
                parts.append(part + jnp.where(j < live, 0.0, NEG))
        else:
            parts.append(scores[:, TILE:])
        scores = jnp.concatenate(parts, axis=1)
        top = jnp.max(scores, axis=1, keepdims=True)
        weights = jnp.exp2((scores - top) * LOG2).astype(jnp.bfloat16)
        total = jnp.dot(weights, values, preferred_element_type=jnp.float32)
        out_buf[tile, :, columns] = (total[:, :HEAD_DIM] / total[:, HEAD_DIM:]).astype(jnp.bfloat16)


def attend_kernel(blocks, tiles, sources, loc_ref, tid_ref, z_ref, *refs):
    q_refs, refs = refs[:blocks], refs[blocks:]
    kv_refs, refs = refs[:len(sources)], refs[len(sources):]
    out_refs, (q_buf, kv_buf, out_buf, q_sem, kv_sem, out_sem) = refs[:blocks], refs[blocks:]
    z = z_ref[0]

    def kv_copies(act):
        for i, (at, low, high) in enumerate(sources):
            rows = kv_refs[i].shape[0]
            start = at(z) * rows if at is not None else 0

            def one(i=i, start=start, rows=rows):
                copy = pltpu.make_async_copy(
                    kv_refs[i], kv_buf.at[pl.ds(start, rows)], kv_sem.at[i]
                )
                getattr(copy, act)()

            if low is None:
                one()
            else:
                pl.when(jnp.logical_and(z >= low, z <= high))(one)

    q_copies = [
        pltpu.make_async_copy(q_refs[i], q_buf.at[pl.ds(i * tiles, tiles)], q_sem.at[i])
        for i in range(blocks)
    ]
    for copy in q_copies:
        copy.start()
    kv_copies("start")
    for copy in q_copies:
        copy.wait()
    kv_copies("wait")

    def one_tile(tile, _):
        live = jnp.minimum(tid_ref[tile] + 1, SLOTS)

        @pl.when(live < SLOTS)
        def _():
            attend_tile(True, live, tile, loc_ref, q_buf, kv_buf, out_buf)

        @pl.when(live == SLOTS)
        def _():
            attend_tile(False, live, tile, loc_ref, q_buf, kv_buf, out_buf)

        return 0

    out_copies = [
        pltpu.make_async_copy(out_buf.at[pl.ds(i * tiles, tiles)], out_refs[i], out_sem.at[i])
        for i in range(blocks)
    ]
    for i in range(blocks):
        lax.fori_loop(i * tiles, (i + 1) * tiles, one_tile, 0)
        out_copies[i].start()
    for copy in out_copies:
        copy.wait()


def attend(q_blocks, kv_bufs, sources, kv_tiles, loc, tid, z):
    blocks = len(q_blocks)
    tiles = q_blocks[0].shape[0] // TILE
    q_blocks = [q.reshape(tiles, TILE, WIDE) for q in q_blocks]
    kv_bufs = [kv.reshape(-1, TILE, 2 * HEAD_DIM) for kv in kv_bufs]
    smem = pl.BlockSpec(memory_space=pltpu.SMEM)
    hbm = pl.BlockSpec(memory_space=pl.ANY)
    units = blocks * tiles
    out = pl.pallas_call(
        functools.partial(attend_kernel, blocks, tiles, sources),
        out_shape=[jax.ShapeDtypeStruct((tiles, TILE, WIDE), jnp.bfloat16)] * blocks,
        in_specs=[smem] * 3 + [hbm] * (blocks + len(kv_bufs)),
        out_specs=[hbm] * blocks,
        scratch_shapes=[
            pltpu.VMEM((units, TILE, WIDE), jnp.bfloat16),
            pltpu.VMEM((kv_tiles, TILE, 2 * HEAD_DIM), jnp.bfloat16),
            pltpu.VMEM((units, TILE, WIDE), jnp.bfloat16),
            pltpu.SemaphoreType.DMA((blocks,)),
            pltpu.SemaphoreType.DMA((len(kv_bufs),)),
            pltpu.SemaphoreType.DMA((blocks,)),
        ],
        compiler_params=pltpu.CompilerParams(vmem_limit_bytes=48 * 2**20),
        cost_estimate=pl.CostEstimate(
            flops=units * 4 * GROUPS * TILE * TILE * SLOTS * HEAD_DIM * 2,
            bytes_accessed=kv_tiles * TILE * 4 * HEAD_DIM + units * TILE * WIDE * 4,
            transcendentals=units * GROUPS * TILE * TILE * SLOTS,
        ),
    )(loc.reshape(-1), tid, z.reshape(1), *q_blocks, *kv_bufs)
    return [o.reshape(tiles * TILE, WIDE) for o in out]


def per_device(sizes, queries, key_rows, value_rows, tile_lists):
    kv_size, pb_size, z_size = sizes
    planes = kv_size * pb_size
    tokens = queries.shape[0]
    tiles = tokens // TILE
    z = lax.axis_index("head")
    pb = lax.axis_index("pb")
    kv = lax.axis_index("kv")
    b = kv * pb_size + pb

    def move(x, pairs):
        return lax.ppermute(x, AXES, pairs)

    def swap(x, offset, low=0, high=z_size - 1):
        return move(x, [
            (i * z_size + h, (i ^ offset) * z_size + h)
            for i in range(planes) for h in range(low, high + 1)
        ])

    lists = lax.all_gather(tile_lists, ("kv", "pb"), axis=0, tiled=True)

    relay = kv_size == 2 and pb_size == 4 and z_size <= 4
    sides = (2, 4) if relay else (2, 2)

    def head_of(half, offset):
        side = sides[half]
        mine = (b & 1) + 2 * ((b & side) // side)
        return 4 * half + (mine ^ ((offset & 1) + 2 * ((offset & side) // side)))

    def near(half):
        return (0, 1, sides[half], sides[half] + 1)

    kv_bufs, kv_sources = [], []
    for half in range(2):
        blocks = []
        for offset in near(half):
            at = head_of(half, offset) * HEAD_DIM
            piece = jnp.concatenate(
                [lax.dynamic_slice_in_dim(a, at, HEAD_DIM, axis=1) for a in (key_rows, value_rows)],
                axis=1,
            )
            blocks.append(swap(piece, offset) if offset else piece)
        own = jnp.concatenate(blocks, axis=0)
        if relay:
            across = 6 - sides[half]
            bufs, sources = [own, swap(own, across)], [(lambda z: z * 2, None, None), (lambda z: z * 2 + 1, None, None)]
            up = down = own
            for step in range(1, z_size):
                up = move(up, [
                    (i * z_size + h, i * z_size + h + 1)
                    for i in range(planes) for h in range(step - 1, z_size - 1)
                ])
                down = move(down, [
                    (i * z_size + h, i * z_size + h - 1)
                    for i in range(planes) for h in range(1, z_size - step + 1)
                ])
                for buf, shift, low, high in ((up, -step, step, z_size - 1), (down, step, 0, z_size - 1 - step)):
                    bufs += [buf, swap(buf, across, low, high)]
                    sources += [
                        (lambda z, shift=shift: (z + shift) * 2, low, high),
                        (lambda z, shift=shift: (z + shift) * 2 + 1, low, high),
                    ]
        else:
            bufs = [lax.all_gather(own, ("kv", "head"), axis=0, tiled=True)]
            sources = [(None, None, None)]
        kv_bufs.append(bufs)
        kv_sources.append(sources)

    def place(half, tile):
        device, within = tile // tiles, tile % tiles
        where, z_from = device // z_size, device % z_size
        differ = where ^ b
        side = sides[half]
        slot = (differ & 1) + 2 * ((differ & side) // side)
        if relay:
            across = 6 - side
            block = (z_from * 2 + (differ & across) // across) * 4 + slot
        else:
            block = ((where // pb_size) * z_size + z_from) * 4 + slot
        return block * tiles + within

    q_blocks = []
    for half in range(2):
        blocks = {}
        for offset in near(half):
            at = head_of(half, offset) * WIDE
            piece = lax.dynamic_slice_in_dim(queries, at, WIDE, axis=1)
            blocks[offset] = swap(piece, offset) if offset else piece
        q_blocks.append(blocks)

    result = jnp.zeros((tokens, HEADS * HEAD_DIM), jnp.bfloat16)
    for far in (True, False):
        for half in range(2):
            side = sides[half]
            offsets = (side + 1, side) if far else (1, 0)
            tid = jnp.concatenate([
                ((b ^ offset) * z_size + z) * tiles + jnp.arange(tiles, dtype=jnp.int32)
                for offset in offsets
            ])
            loc = place(half, jnp.take(lists, tid, axis=0))
            outs = attend(
                [q_blocks[half][offset] for offset in offsets],
                kv_bufs[half], kv_sources[half], planes * z_size * tiles, loc, tid, z,
            )
            for offset, out in zip(offsets, outs):
                back = swap(out, offset) if offset else out
                result = lax.dynamic_update_slice_in_dim(result, back, head_of(half, offset) * WIDE, axis=1)
    return result


def solution(mesh):
    in_specs = (P(AXES, None), P(AXES, None), P(AXES, None), P(("kv", "pb"), None))
    sizes = tuple(mesh.shape[axis] for axis in AXES)
    return jax.shard_map(
        functools.partial(per_device, sizes),
        mesh=mesh, in_specs=in_specs, out_specs=P(AXES, None), check_vma=False,
    )
```

time: 483 us -> 197 us (0.41)
  the two profiles are of different devices: /device:TPU:17 before, /device:TPU:0 now
where the time goes in v1:
time: 197 us; the launch traced here: 196 us
  starting transfers between devices  67 us (34%)
  waiting for transfers between devices  51.8 us (26%)
  Pallas kernels  37.5 us (19%)
  blocking collectives  22.1 us (11%)
  local copies, waits for them, and re-layouts  14.4 us (7%)
  other arithmetic  2.71 us (1%)
    ppermute x44, starting transfers between devices, move(): return lax.ppermute(x, AXES, pairs)  67 us
    ppermute x44, waiting for transfers between devices, move(): return lax.ppermute(x, AXES, pairs)  51.8 us
    pallas_call x4, Pallas kernels, attend(): pl.pallas_call(functools.partial(attend_kernel, blocks, tiles, sources),...  37.5 us
    all_gather x1, blocking collectives, per_device(): lists = lax.all_gather(tile_lists, ('kv', 'pb'), axis=0, tiled=True)  22.1 us
    unnamed x26, local copies, waits for them, and re-layouts  5.48 us
    dynamic_slice x1, local copies, waits for them, and re-layouts, per_device(): piece = lax.dynamic_slice_in_dim(queries, at, WIDE, axis=1)  3.94 us
  transfers between devices with their start and end apart: 44, of which 11 were waited for; matrix products, arithmetic and copies ran while one was open for 5% of the time, Pallas kernels for 19%

profile of v1, /device:TPU:0, one launch (start us, length us, event | category | flops | bytes accessed | tf_op | source)
XLA Modules:
  0.0 196.2 jit_solution(3625994399365245610)
XLA Ops:
  1.9 2.6 %collective-permute-start.23 = (bf16[256,256]{1,0:T(8,128)(2,1)S(1)}, bf16[256,256]{1,0:T(8,128)(2,1)}, u32[]{:S(2)}, u32[]{:S(2)}) collective-permute-start(bf16[256,256]{1,0:T(8,128)(2,1)S(1)} %pad_maximum_fusion.6), channel_id=1, source_target_pairs={{0,16},{1,17},{2,18},{3,19},{4,20},{5,21},{6,22},{7,23},{8,24},{9,... | collective-permute-start | bytes 393224 | tf_op jit(solution)/shard_map/ppermute | solution.py:150
  4.5 3.9 %constant_dynamic-slice_fusion = (bf16[256,1024]{1,0:T(8,128)(2,1)S(1)}, bf16[256,1024]{1,0:T(8,128)(2,1)S(1)}, bf16[256,1024]{1,0:T(8,128)(2,1)S(1)}, bf16[256,...) fusion(bf16[256,8192]{1,0:T(8,128)(2,1)} %param.6, ...), kind=kLoop, calls=%fused_computation.13 | loop fusion | bytes 8388640 | tf_op jit(solution)/shard_map/dynamic_slice | solution.py:225
  9.4 1.7 collective-permute-start.3
  12.2 1.9 collective-permute-done.24
  14.2 2.1 %collective-permute-start.4 = (bf16[256,256]{1,0:T(8,128)(2,1)S(1)}, bf16[256,256]{1,0:T(8,128)(2,1)S(1)}, u32[]{:S(2)}, u32[]{:S(2)}) collective-permute-start(bf16[256,256]{1,0:T(8,128)(2,1)S(1)} %pad_maximum_fusion.4), channel_id=1, source_target_pairs={{0,12},{1,13},{2,14},{3,15},{4,8},{5,9},{6,10},{7,11},{8,4},{9,5},... | collective-permute-start | bytes 393224 | tf_op jit(solution)/shard_map/ppermute | solution.py:150
  17.8 1.7 collective-permute-done.4
  20.2 4.3 %collective-permute-start.26 = (bf16[1024,256]{1,0:T(8,128)(2,1)S(1)}, bf16[1024,256]{1,0:T(8,128)(2,1)}, u32[]{:S(2)}, u32[]{:S(2)}) collective-permute-start(bf16[1024,256]{1,0:T(8,128)(2,1)S(1)} %pad_maximum_fusion.1), channel_id=1, source_target_pairs={{0,1},{1,2},{2,3},{4,5},{5,6},{6,7},{8,9},{9,10},{10,11},{12,13},{... | collective-permute-start | bytes 1572872 | tf_op jit(solution)/shard_map/ppermute | solution.py:150
  24.5 22.1 %all_gather.3 = s32[64,8]{1,0:T(8,128)S(1)} all-gather(s32[8,8]{1,0:T(8,128)S(1)} %copy-done.8), channel_id=1, replica_groups=mesh['kv'=2,'pb'=4,'head'=4] {'kv','pb'}, dimensions={0}, use_global_device_ids=true | all-gather | bytes 2304 | tf_op jit(solution)/shard_map/all_gather | solution.py:158
  49.5 5.4 %collective-permute-start.6 = (bf16[1024,256]{1,0:T(8,128)(2,1)S(1)}, bf16[1024,256]{1,0:T(8,128)(2,1)}, u32[]{:S(2)}, u32[]{:S(2)}) collective-permute-start(bf16[1024,256]{1,0:T(8,128)(2,1)S(1)} %pad_maximum_fusion), channel_id=1, source_target_pairs={{0,1},{1,2},{2,3},{4,5},{5,6},{6,7},{8,9},{9,10},{10,11},{12,13},{... | collective-permute-start | bytes 1572872 | tf_op jit(solution)/shard_map/ppermute | solution.py:150
  56.2 1.6 collective-permute-start.5
  57.8 5.5 %collective-permute-done.28 = bf16[1024,256]{1,0:T(8,128)(2,1)} collective-permute-done((bf16[1024,256]{1,0:T(8,128)(2,1)S(1)}, bf16[1024,256]{1,0:T(8,128)(2,1)}, u32[]{:S(2)}, u32[]{:S(2)}) %collective-permute-start.28) | collective-permute-done | bytes 524320 | tf_op jit(solution)/shard_map/ppermute | solution.py:150
  68.5 5.6 %collective-permute-done.8 = bf16[1024,256]{1,0:T(8,128)(2,1)} collective-permute-done((bf16[1024,256]{1,0:T(8,128)(2,1)S(1)}, bf16[1024,256]{1,0:T(8,128)(2,1)}, u32[]{:S(2)}, u32[]{:S(2)}) %collective-permute-start.8) | collective-permute-done | bytes 524320 | tf_op jit(solution)/shard_map/ppermute | solution.py:150
  78.2 1.5 collective-permute-start.7
  79.9 7.6 %collective-permute-done.32 = bf16[1024,256]{1,0:T(8,128)(2,1)} collective-permute-done((bf16[1024,256]{1,0:T(8,128)(2,1)}, bf16[1024,256]{1,0:T(8,128)(2,1)}, u32[]{:S(2)}, u32[]{:S(2)}) %collective-permute-start.32) | collective-permute-done | bytes 524320 | tf_op jit(solution)/shard_map/ppermute | solution.py:150
  87.5 3.4 %collective-permute-start.9 = (bf16[1024,256]{1,0:T(8,128)(2,1)}, bf16[1024,256]{1,0:T(8,128)(2,1)}, u32[]{:S(2)}, u32[]{:S(2)}) collective-permute-start(bf16[1024,256]{1,0:T(8,128)(2,1)} %collective-permute-done.8), channel_id=1, source_target_pairs={{0,16},{1,17},{2,18},{4,20},{5,21},{6,22},{8,24},{9,25},{10,26},{1... | collective-permute-start | bytes 1572872 | tf_op jit(solution)/shard_map/ppermute | solution.py:150
  93.9 2.6 %collective-permute-done.12 = bf16[1024,256]{1,0:T(8,128)(2,1)} collective-permute-done((bf16[1024,256]{1,0:T(8,128)(2,1)}, bf16[1024,256]{1,0:T(8,128)(2,1)}, u32[]{:S(2)}, u32[]{:S(2)}) %collective-permute-start.12) | collective-permute-done | bytes 524320 | tf_op jit(solution)/shard_map/ppermute | solution.py:150
  101.4 3.5 %collective-permute-start.13 = (bf16[1024,256]{1,0:T(8,128)(2,1)}, bf16[1024,256]{1,0:T(8,128)(2,1)}, u32[]{:S(2)}, u32[]{:S(2)}) collective-permute-start(bf16[1024,256]{1,0:T(8,128)(2,1)} %collective-permute-done.12), channel_id=1, source_target_pairs={{0,16},{1,17},{4,20},{5,21},{8,24},{9,25},{12,28},{13,29},{16,0},{... | collective-permute-start | bytes 1572872 | tf_op jit(solution)/shard_map/ppermute | solution.py:150
  106.4 7.1 %collective-permute-done.16 = bf16[1024,256]{1,0:T(8,128)(2,1)} collective-permute-done((bf16[1024,256]{1,0:T(8,128)(2,1)}, bf16[1024,256]{1,0:T(8,128)(2,1)}, u32[]{:S(2)}, u32[]{:S(2)}) %collective-permute-start.16) | collective-permute-done | bytes 524320 | tf_op jit(solution)/shard_map/ppermute | solution.py:150
  113.5 3.5 %collective-permute-start.17 = (bf16[1024,256]{1,0:T(8,128)(2,1)}, bf16[1024,256]{1,0:T(8,128)(2,1)}, u32[]{:S(2)}, u32[]{:S(2)}) collective-permute-start(bf16[1024,256]{1,0:T(8,128)(2,1)} %collective-permute-done.16), channel_id=1, source_target_pairs={{0,16},{4,20},{8,24},{12,28},{16,0},{20,4},{24,8},{28,12}} | collective-permute-start | bytes 1572872 | tf_op jit(solution)/shard_map/ppermute | solution.py:150
  117.6 3.9 %collective-permute-done.36 = bf16[1024,256]{1,0:T(8,128)(2,1)} collective-permute-done((bf16[1024,256]{1,0:T(8,128)(2,1)}, bf16[1024,256]{1,0:T(8,128)(2,1)}, u32[]{:S(2)}, u32[]{:S(2)}) %collective-permute-start.36) | collective-permute-done | bytes 524320 | tf_op jit(solution)/shard_map/ppermute | solution.py:150
  121.6 3.3 %collective-permute-start.29 = (bf16[1024,256]{1,0:T(8,128)(2,1)}, bf16[1024,256]{1,0:T(8,128)(2,1)}, u32[]{:S(2)}, u32[]{:S(2)}) collective-permute-start(bf16[1024,256]{1,0:T(8,128)(2,1)} %collective-permute-done.28), channel_id=1, source_target_pairs={{0,8},{1,9},{2,10},{4,12},{5,13},{6,14},{8,0},{9,1},{10,2},{12,4},... | collective-permute-start | bytes 1572872 | tf_op jit(solution)/shard_map/ppermute | solution.py:150
  125.7 2.6 %collective-permute-start.33 = (bf16[1024,256]{1,0:T(8,128)(2,1)}, bf16[1024,256]{1,0:T(8,128)(2,1)S(1)}, u32[]{:S(2)}, u32[]{:S(2)}) collective-permute-start(bf16[1024,256]{1,0:T(8,128)(2,1)} %collective-permute-done.32), channel_id=1, source_target_pairs={{0,8},{1,9},{4,12},{5,13},{8,0},{9,1},{12,4},{13,5},{16,24},{17,25... | collective-permute-start | bytes 1572872 | tf_op jit(solution)/shard_map/ppermute | solution.py:150
  129.0 3.5 %collective-permute-start.37 = (bf16[1024,256]{1,0:T(8,128)(2,1)}, bf16[1024,256]{1,0:T(8,128)(2,1)S(1)}, u32[]{:S(2)}, u32[]{:S(2)}) collective-permute-start(bf16[1024,256]{1,0:T(8,128)(2,1)} %collective-permute-done.36), channel_id=1, source_target_pairs={{0,8},{4,12},{8,0},{12,4},{16,24},{20,28},{24,16},{28,20}} | collective-permute-start | bytes 1572872 | tf_op jit(solution)/shard_map/ppermute | solution.py:150
  133.6 9.3 %shard_map.48 = (bf16[2,128,1024]{2,1,0:T(8,128)(2,1)S(1)}, bf16[2,128,1024]{2,1,0:T(8,128)(2,1)S(1)}) custom-call(s32[32]{0:T(128)S(1)} %reshape.222.loc_ref, s32[4]{0:T(128)S(1)} %get-tuple-element.23.tid_ref, s32[1]{0:T(128)} %bitcast.z_ref, bf16[2,128,1024]{2,1,0:T(8,128)(2,1)S(1)} %bitcast.54, bf16[2,128,1024]{2,1,0:T(8,128)(2,1)S(1)} %bitcast.52, ...), custom_call_target="tpu_custom_call" | custom-call | flops 4294967296 | bytes 6291456 | tf_op jit(solution)/shard_map/pallas_call | solution.py:116
  143.0 9.7 %shard_map.46 = (bf16[2,128,1024]{2,1,0:T(8,128)(2,1)S(1)}, bf16[2,128,1024]{2,1,0:T(8,128)(2,1)S(1)}) custom-call(s32[32]{0:T(128)S(1)} %reshape.183.loc_ref, s32[4]{0:T(128)S(1)} %get-tuple-element.27.tid_ref, s32[1]{0:T(128)} %bitcast.z_ref, bf16[2,128,1024]{2,1,0:T(8,128)(2,1)} %bitcast.1.refs_0_, bf16[2,128,1024]{2,1,0:T(8,128)(2,1)} %bitcast.2.refs_1_, ...), custom_call_target="tpu_custom_call" | custom-call | flops 4294967296 | bytes 6291456 | tf_op jit(solution)/shard_map/pallas_call | solution.py:116
  153.6 3.9 %collective-permute-done.37 = bf16[1024,256]{1,0:T(8,128)(2,1)S(1)} collective-permute-done((bf16[1024,256]{1,0:T(8,128)(2,1)}, bf16[1024,256]{1,0:T(8,128)(2,1)S(1)}, u32[]{:S(2)}, u32[]{:S(2)}) %collective-permute-start.37) | collective-permute-done | bytes 524320 | tf_op jit(solution)/shard_map/ppermute | solution.py:150
  158.3 9.3 %shard_map.47 = (bf16[2,128,1024]{2,1,0:T(8,128)(2,1)S(1)}, bf16[2,128,1024]{2,1,0:T(8,128)(2,1)S(1)}) custom-call(s32[32]{0:T(128)S(1)} %reshape.203.loc_ref, s32[4]{0:T(128)S(1)} %get-tuple-element.25.tid_ref, s32[1]{0:T(128)} %bitcast.z_ref, bf16[2,128,1024]{2,1,0:T(8,128)(2,1)S(1)} %bitcast.53, bf16[2,128,1024]{2,1,0:T(8,128)(2,1)} %bitcast.20.refs_1_, ...), custom_call_target="tpu_custom_call" | custom-call | flops 4294967296 | bytes 6291456 | tf_op jit(solution)/shard_map/pallas_call | solution.py:116
  167.7 1.9 collective-permute-start.19
  169.6 1.6 collective-permute-start.39
  171.2 9.3 %shard_map.49 = (bf16[2,128,1024]{2,1,0:T(8,128)(2,1)S(1)}, bf16[2,128,1024]{2,1,0:T(8,128)(2,1)S(1)}) custom-call(s32[32]{0:T(128)S(1)} %reshape.227.loc_ref, s32[4]{0:T(128)S(1)} %get-tuple-element.23.tid_ref, s32[1]{0:T(128)} %bitcast.z_ref, bf16[2,128,1024]{2,1,0:T(8,128)(2,1)S(1)} %bitcast.61, bf16[2,128,1024]{2,1,0:T(8,128)(2,1)S(1)} %bitcast.51, ...), custom_call_target="tpu_custom_call" | custom-call | flops 4294967296 | bytes 6291456 | tf_op jit(solution)/shard_map/pallas_call | solution.py:116
  181.5 11.6 %collective-permute-done.39 = bf16[256,1024]{1,0:T(8,128)(2,1)S(1)} collective-permute-done((bf16[256,1024]{1,0:T(8,128)(2,1)S(1)}, bf16[256,1024]{1,0:T(8,128)(2,1)S(1)}, u32[]{:S(2)}, u32[]{:S(2)}) %collective-permute-start.39) | collective-permute-done | bytes 524320 | tf_op jit(solution)/shard_map/ppermute | solution.py:150
  193.4 2.0 %copy-done.5 = bf16[256,8192]{1,0:T(8,128)(2,1)} copy-done((bf16[256,8192]{1,0:T(8,128)(2,1)}, bf16[256,8192]{1,0:T(8,128)(2,1)S(1)}, u32[]{:S(2)}) %copy-start.5) | copy-done | bytes 4194328
  (129 shorter events, 36.2 us)
Async XLA Ops:
  11.1 35.6 %collective-permute-start.20 = (bf16[256,1024]{1,0:T(8,128)(2,1)S(1)}, bf16[256,1024]{1,0:T(8,128)(2,1)S(1)}, u32[]{:S(2)}, u32[]{:S(2)}) collective-permute-start(bf16[256,1024]{1,0:T(8,128)(2,1)S(1)} %get-tuple-element.32), channel_id=1, source_target_pairs={{0,20},{1,21},{2,22},{3,23},{4,16},{5,17},{6,18},{7,19},{8,28},{9,... | collective-permute-start | bytes 1572872 | tf_op jit(solution)/shard_map/ppermute | solution.py:150
  17.2 31.8 %collective-permute-start.21 = (bf16[256,1024]{1,0:T(8,128)(2,1)}, bf16[256,1024]{1,0:T(8,128)(2,1)}, u32[]{:S(2)}, u32[]{:S(2)}) collective-permute-start(bf16[256,1024]{1,0:T(8,128)(2,1)} %get-tuple-element.31), channel_id=1, source_target_pairs={{0,16},{1,17},{2,18},{3,19},{4,20},{5,21},{6,22},{7,23},{8,24},{9,... | collective-permute-start | bytes 1572872 | tf_op jit(solution)/shard_map/ppermute | solution.py:150
  17.8 31.7 %collective-permute-start = (bf16[256,1024]{1,0:T(8,128)(2,1)}, bf16[256,1024]{1,0:T(8,128)(2,1)}, u32[]{:S(2)}, u32[]{:S(2)}) collective-permute-start(bf16[256,1024]{1,0:T(8,128)(2,1)} %get-tuple-element.34), channel_id=1, source_target_pairs={{0,12},{1,13},{2,14},{3,15},{4,8},{5,9},{6,10},{7,11},{8,4},{9,5},... | collective-permute-start | bytes 1572872 | tf_op jit(solution)/shard_map/ppermute | solution.py:150
  19.5 35.3 %collective-permute-start.1 = (bf16[256,1024]{1,0:T(8,128)(2,1)}, bf16[256,1024]{1,0:T(8,128)(2,1)}, u32[]{:S(2)}, u32[]{:S(2)}) collective-permute-start(bf16[256,1024]{1,0:T(8,128)(2,1)} %get-tuple-element.33), channel_id=1, source_target_pairs={{0,8},{1,9},{2,10},{3,11},{4,12},{5,13},{6,14},{7,15},{8,0},{9,1},... | collective-permute-start | bytes 1572872 | tf_op jit(solution)/shard_map/ppermute | solution.py:150
  20.2 35.9 %collective-permute-start.26 = (bf16[1024,256]{1,0:T(8,128)(2,1)S(1)}, bf16[1024,256]{1,0:T(8,128)(2,1)}, u32[]{:S(2)}, u32[]{:S(2)}) collective-permute-start(bf16[1024,256]{1,0:T(8,128)(2,1)S(1)} %pad_maximum_fusion.1), channel_id=1, source_target_pairs={{0,1},{1,2},{2,3},{4,5},{5,6},{6,7},{8,9},{9,10},{10,11},{12,13},{... | collective-permute-start | bytes 1572872 | tf_op jit(solution)/shard_map/ppermute | solution.py:150
  46.6 16.7 %collective-permute-start.28 = (bf16[1024,256]{1,0:T(8,128)(2,1)S(1)}, bf16[1024,256]{1,0:T(8,128)(2,1)}, u32[]{:S(2)}, u32[]{:S(2)}) collective-permute-start(bf16[1024,256]{1,0:T(8,128)(2,1)S(1)} %pad_maximum_fusion.1), channel_id=1, source_target_pairs={{1,0},{2,1},{3,2},{5,4},{6,5},{7,6},{9,8},{10,9},{11,10},{13,12},{... | collective-permute-start | bytes 1572872 | tf_op jit(solution)/shard_map/ppermute | solution.py:150
  49.0 15.9 %collective-permute-start.25 = (bf16[1024,256]{1,0:T(8,128)(2,1)S(1)}, bf16[1024,256]{1,0:T(8,128)(2,1)S(1)}, u32[]{:S(2)}, u32[]{:S(2)}) collective-permute-start(bf16[1024,256]{1,0:T(8,128)(2,1)S(1)} %pad_maximum_fusion.1), channel_id=1, source_target_pairs={{0,8},{1,9},{2,10},{3,11},{4,12},{5,13},{6,14},{7,15},{8,0},{9,1},... | collective-permute-start | bytes 1572872 | tf_op jit(solution)/shard_map/ppermute | solution.py:150
  49.5 17.7 %collective-permute-start.6 = (bf16[1024,256]{1,0:T(8,128)(2,1)S(1)}, bf16[1024,256]{1,0:T(8,128)(2,1)}, u32[]{:S(2)}, u32[]{:S(2)}) collective-permute-start(bf16[1024,256]{1,0:T(8,128)(2,1)S(1)} %pad_maximum_fusion), channel_id=1, source_target_pairs={{0,1},{1,2},{2,3},{4,5},{5,6},{6,7},{8,9},{9,10},{10,11},{12,13},{... | collective-permute-start | bytes 1572872 | tf_op jit(solution)/shard_map/ppermute | solution.py:150
  54.9 19.2 %collective-permute-start.8 = (bf16[1024,256]{1,0:T(8,128)(2,1)S(1)}, bf16[1024,256]{1,0:T(8,128)(2,1)}, u32[]{:S(2)}, u32[]{:S(2)}) collective-permute-start(bf16[1024,256]{1,0:T(8,128)(2,1)S(1)} %pad_maximum_fusion), channel_id=1, source_target_pairs={{1,0},{2,1},{3,2},{5,4},{6,5},{7,6},{9,8},{10,9},{11,10},{13,12},{... | collective-permute-start | bytes 1572872 | tf_op jit(solution)/shard_map/ppermute | solution.py:150
  56.2 19.3 %collective-permute-start.5 = (bf16[1024,256]{1,0:T(8,128)(2,1)S(1)}, bf16[1024,256]{1,0:T(8,128)(2,1)S(1)}, u32[]{:S(2)}, u32[]{:S(2)}) collective-permute-start(bf16[1024,256]{1,0:T(8,128)(2,1)S(1)} %pad_maximum_fusion), channel_id=1, source_target_pairs={{0,16},{1,17},{2,18},{3,19},{4,20},{5,21},{6,22},{7,23},{8,24},{9,... | collective-permute-start | bytes 1572872 | tf_op jit(solution)/shard_map/ppermute | solution.py:150
  63.4 14.8 %collective-permute-start.30 = (bf16[1024,256]{1,0:T(8,128)(2,1)}, bf16[1024,256]{1,0:T(8,128)(2,1)}, u32[]{:S(2)}, u32[]{:S(2)}) collective-permute-start(bf16[1024,256]{1,0:T(8,128)(2,1)} %collective-permute-done.26), channel_id=1, source_target_pairs={{1,2},{2,3},{5,6},{6,7},{9,10},{10,11},{13,14},{14,15},{17,18},{18... | collective-permute-start | bytes 1572872 | tf_op jit(solution)/shard_map/ppermute | solution.py:150
  65.7 25.2 %collective-permute-start.27 = (bf16[1024,256]{1,0:T(8,128)(2,1)}, bf16[1024,256]{1,0:T(8,128)(2,1)}, u32[]{:S(2)}, u32[]{:S(2)}) collective-permute-start(bf16[1024,256]{1,0:T(8,128)(2,1)} %collective-permute-done.26), channel_id=1, source_target_pairs={{1,9},{2,10},{3,11},{5,13},{6,14},{7,15},{9,1},{10,2},{11,3},{13,5... | collective-permute-start | bytes 1572872 | tf_op jit(solution)/shard_map/ppermute | solution.py:150
  67.2 20.3 %collective-permute-start.32 = (bf16[1024,256]{1,0:T(8,128)(2,1)}, bf16[1024,256]{1,0:T(8,128)(2,1)}, u32[]{:S(2)}, u32[]{:S(2)}) collective-permute-start(bf16[1024,256]{1,0:T(8,128)(2,1)} %collective-permute-done.28), channel_id=1, source_target_pairs={{1,0},{2,1},{5,4},{6,5},{9,8},{10,9},{13,12},{14,13},{17,16},{18,1... | collective-permute-start | bytes 1572872 | tf_op jit(solution)/shard_map/ppermute | solution.py:150
  74.0 18.4 %collective-permute-start.10 = (bf16[1024,256]{1,0:T(8,128)(2,1)}, bf16[1024,256]{1,0:T(8,128)(2,1)}, u32[]{:S(2)}, u32[]{:S(2)}) collective-permute-start(bf16[1024,256]{1,0:T(8,128)(2,1)} %collective-permute-done.6), channel_id=1, source_target_pairs={{1,2},{2,3},{5,6},{6,7},{9,10},{10,11},{13,14},{14,15},{17,18},{18... | collective-permute-start | bytes 1572872 | tf_op jit(solution)/shard_map/ppermute | solution.py:150
  76.3 20.2 %collective-permute-start.12 = (bf16[1024,256]{1,0:T(8,128)(2,1)}, bf16[1024,256]{1,0:T(8,128)(2,1)}, u32[]{:S(2)}, u32[]{:S(2)}) collective-permute-start(bf16[1024,256]{1,0:T(8,128)(2,1)} %collective-permute-done.8), channel_id=1, source_target_pairs={{1,0},{2,1},{5,4},{6,5},{9,8},{10,9},{13,12},{14,13},{17,16},{18,1... | collective-permute-start | bytes 1572872 | tf_op jit(solution)/shard_map/ppermute | solution.py:150
  78.2 20.4 %collective-permute-start.7 = (bf16[1024,256]{1,0:T(8,128)(2,1)}, bf16[1024,256]{1,0:T(8,128)(2,1)}, u32[]{:S(2)}, u32[]{:S(2)}) collective-permute-start(bf16[1024,256]{1,0:T(8,128)(2,1)} %collective-permute-done.6), channel_id=1, source_target_pairs={{1,17},{2,18},{3,19},{5,21},{6,22},{7,23},{9,25},{10,26},{11,27},{... | collective-permute-start | bytes 1572872 | tf_op jit(solution)/shard_map/ppermute | solution.py:150
  96.5 17.1 %collective-permute-start.16 = (bf16[1024,256]{1,0:T(8,128)(2,1)}, bf16[1024,256]{1,0:T(8,128)(2,1)}, u32[]{:S(2)}, u32[]{:S(2)}) collective-permute-start(bf16[1024,256]{1,0:T(8,128)(2,1)} %collective-permute-done.12), channel_id=1, source_target_pairs={{1,0},{5,4},{9,8},{13,12},{17,16},{21,20},{25,24},{29,28}} | collective-permute-start | bytes 1572872 | tf_op jit(solution)/shard_map/ppermute | solution.py:150
  98.5 23.0 %collective-permute-start.36 = (bf16[1024,256]{1,0:T(8,128)(2,1)}, bf16[1024,256]{1,0:T(8,128)(2,1)}, u32[]{:S(2)}, u32[]{:S(2)}) collective-permute-start(bf16[1024,256]{1,0:T(8,128)(2,1)} %collective-permute-done.32), channel_id=1, source_target_pairs={{1,0},{5,4},{9,8},{13,12},{17,16},{21,20},{25,24},{29,28}} | collective-permute-start | bytes 1572872 | tf_op jit(solution)/shard_map/ppermute | solution.py:150
  99.9 25.1 %collective-permute-start.11 = (bf16[1024,256]{1,0:T(8,128)(2,1)}, bf16[1024,256]{1,0:T(8,128)(2,1)}, u32[]{:S(2)}, u32[]{:S(2)}) collective-permute-start(bf16[1024,256]{1,0:T(8,128)(2,1)} %collective-permute-done.10), channel_id=1, source_target_pairs={{2,18},{3,19},{6,22},{7,23},{10,26},{11,27},{14,30},{15,31},{18,2}... | collective-permute-start | bytes 1572872 | tf_op jit(solution)/shard_map/ppermute | solution.py:150
  101.4 24.4 %collective-permute-start.13 = (bf16[1024,256]{1,0:T(8,128)(2,1)}, bf16[1024,256]{1,0:T(8,128)(2,1)}, u32[]{:S(2)}, u32[]{:S(2)}) collective-permute-start(bf16[1024,256]{1,0:T(8,128)(2,1)} %collective-permute-done.12), channel_id=1, source_target_pairs={{0,16},{1,17},{4,20},{5,21},{8,24},{9,25},{12,28},{13,29},{16,0},{... | collective-permute-start | bytes 1572872 | tf_op jit(solution)/shard_map/ppermute | solution.py:150
  104.9 23.4 %collective-permute-start.15 = (bf16[1024,256]{1,0:T(8,128)(2,1)}, bf16[1024,256]{1,0:T(8,128)(2,1)}, u32[]{:S(2)}, u32[]{:S(2)}) collective-permute-start(bf16[1024,256]{1,0:T(8,128)(2,1)} %collective-permute-done.14), channel_id=1, source_target_pairs={{3,19},{7,23},{11,27},{15,31},{19,3},{23,7},{27,11},{31,15}} | collective-permute-start | bytes 1572872 | tf_op jit(solution)/shard_map/ppermute | solution.py:150
  113.5 15.5 %collective-permute-start.17 = (bf16[1024,256]{1,0:T(8,128)(2,1)}, bf16[1024,256]{1,0:T(8,128)(2,1)}, u32[]{:S(2)}, u32[]{:S(2)}) collective-permute-start(bf16[1024,256]{1,0:T(8,128)(2,1)} %collective-permute-done.16), channel_id=1, source_target_pairs={{0,16},{4,20},{8,24},{12,28},{16,0},{20,4},{24,8},{28,12}} | collective-permute-start | bytes 1572872 | tf_op jit(solution)/shard_map/ppermute | solution.py:150
  121.6 21.3 %collective-permute-start.29 = (bf16[1024,256]{1,0:T(8,128)(2,1)}, bf16[1024,256]{1,0:T(8,128)(2,1)}, u32[]{:S(2)}, u32[]{:S(2)}) collective-permute-start(bf16[1024,256]{1,0:T(8,128)(2,1)} %collective-permute-done.28), channel_id=1, source_target_pairs={{0,8},{1,9},{2,10},{4,12},{5,13},{6,14},{8,0},{9,1},{10,2},{12,4},... | collective-permute-start | bytes 1572872 | tf_op jit(solution)/shard_map/ppermute | solution.py:150
  125.0 27.6 %collective-permute-start.31 = (bf16[1024,256]{1,0:T(8,128)(2,1)}, bf16[1024,256]{1,0:T(8,128)(2,1)S(1)}, u32[]{:S(2)}, u32[]{:S(2)}) collective-permute-start(bf16[1024,256]{1,0:T(8,128)(2,1)} %collective-permute-done.30), channel_id=1, source_target_pairs={{2,10},{3,11},{6,14},{7,15},{10,2},{11,3},{14,6},{15,7},{18,26},{1... | collective-permute-start | bytes 1572872 | tf_op jit(solution)/shard_map/ppermute | solution.py:150
  125.7 27.5 %collective-permute-start.33 = (bf16[1024,256]{1,0:T(8,128)(2,1)}, bf16[1024,256]{1,0:T(8,128)(2,1)S(1)}, u32[]{:S(2)}, u32[]{:S(2)}) collective-permute-start(bf16[1024,256]{1,0:T(8,128)(2,1)} %collective-permute-done.32), channel_id=1, source_target_pairs={{0,8},{1,9},{4,12},{5,13},{8,0},{9,1},{12,4},{13,5},{16,24},{17,25... | collective-permute-start | bytes 1572872 | tf_op jit(solution)/shard_map/ppermute | solution.py:150
  128.3 25.2 %collective-permute-start.35 = (bf16[1024,256]{1,0:T(8,128)(2,1)}, bf16[1024,256]{1,0:T(8,128)(2,1)S(1)}, u32[]{:S(2)}, u32[]{:S(2)}) collective-permute-start(bf16[1024,256]{1,0:T(8,128)(2,1)} %collective-permute-done.34), channel_id=1, source_target_pairs={{3,11},{7,15},{11,3},{15,7},{19,27},{23,31},{27,19},{31,23}} | collective-permute-start | bytes 1572872 | tf_op jit(solution)/shard_map/ppermute | solution.py:150
  129.0 28.4 %collective-permute-start.37 = (bf16[1024,256]{1,0:T(8,128)(2,1)}, bf16[1024,256]{1,0:T(8,128)(2,1)S(1)}, u32[]{:S(2)}, u32[]{:S(2)}) collective-permute-start(bf16[1024,256]{1,0:T(8,128)(2,1)} %collective-permute-done.36), channel_id=1, source_target_pairs={{0,8},{4,12},{8,0},{12,4},{16,24},{20,28},{24,16},{28,20}} | collective-permute-start | bytes 1572872 | tf_op jit(solution)/shard_map/ppermute | solution.py:150
  142.9 26.8 %collective-permute-start.42 = (bf16[256,1024]{1,0:T(8,128)(2,1)S(1)}, bf16[256,1024]{1,0:T(8,128)(2,1)S(1)}, u32[]{:S(2)}, u32[]{:S(2)}) collective-permute-start(bf16[256,1024]{1,0:T(8,128)(2,1)S(1)} %copy-done.6), channel_id=1, source_target_pairs={{0,4},{1,5},{2,6},{3,7},{4,0},{5,1},{6,2},{7,3},{8,12},{9,13},{10,... | collective-permute-start | bytes 1572872 | tf_op jit(solution)/shard_map/ppermute | solution.py:150
  152.7 40.5 %collective-permute-start.41 = (bf16[256,1024]{1,0:T(8,128)(2,1)S(1)}, bf16[256,1024]{1,0:T(8,128)(2,1)S(1)}, u32[]{:S(2)}, u32[]{:S(2)}) collective-permute-start(bf16[256,1024]{1,0:T(8,128)(2,1)S(1)} %bitcast.59), channel_id=1, source_target_pairs={{0,4},{1,5},{2,6},{3,7},{4,0},{5,1},{6,2},{7,3},{8,12},{9,13},{10,... | collective-permute-start | bytes 1572872 | tf_op jit(solution)/shard_map/ppermute | solution.py:150
  153.2 27.3 %collective-permute-start.18 = (bf16[256,1024]{1,0:T(8,128)(2,1)S(1)}, bf16[256,1024]{1,0:T(8,128)(2,1)S(1)}, u32[]{:S(2)}, u32[]{:S(2)}) collective-permute-start(bf16[256,1024]{1,0:T(8,128)(2,1)S(1)} %bitcast.62), channel_id=1, source_target_pairs={{0,12},{1,13},{2,14},{3,15},{4,8},{5,9},{6,10},{7,11},{8,4},{9,5},... | collective-permute-start | bytes 1572872 | tf_op jit(solution)/shard_map/ppermute | solution.py:150
  167.6 13.8 %collective-permute-start.38 = (bf16[256,1024]{1,0:T(8,128)(2,1)S(1)}, bf16[256,1024]{1,0:T(8,128)(2,1)S(1)}, u32[]{:S(2)}, u32[]{:S(2)}) collective-permute-start(bf16[256,1024]{1,0:T(8,128)(2,1)S(1)} %bitcast.65), channel_id=1, source_target_pairs={{0,20},{1,21},{2,22},{3,23},{4,16},{5,17},{6,18},{7,19},{8,28},{9,... | collective-permute-start | bytes 1572872 | tf_op jit(solution)/shard_map/ppermute | solution.py:150
  169.6 23.5 %collective-permute-start.39 = (bf16[256,1024]{1,0:T(8,128)(2,1)S(1)}, bf16[256,1024]{1,0:T(8,128)(2,1)S(1)}, u32[]{:S(2)}, u32[]{:S(2)}) collective-permute-start(bf16[256,1024]{1,0:T(8,128)(2,1)S(1)} %bitcast.63), channel_id=1, source_target_pairs={{0,16},{1,17},{2,18},{3,19},{4,20},{5,21},{6,22},{7,23},{8,24},{9,... | collective-permute-start | bytes 1572872 | tf_op jit(solution)/shard_map/ppermute | solution.py:150
  (25 other events, 191.5 us)

commit v2 on v1

--- a/solution.py
+++ b/solution.py
@@ -55,20 +55,22 @@
     z = z_ref[0]
 
     def kv_copies(act):
-        for i, (at, low, high) in enumerate(sources):
+        for i, (at, places) in enumerate(sources):
             rows = kv_refs[i].shape[0]
-            start = at(z) * rows if at is not None else 0
-
-            def one(i=i, start=start, rows=rows):
+
+            def one(i=i, at=at, rows=rows):
                 copy = pltpu.make_async_copy(
-                    kv_refs[i], kv_buf.at[pl.ds(start, rows)], kv_sem.at[i]
+                    kv_refs[i], kv_buf.at[pl.ds(at * rows, rows)], kv_sem.at[i]
                 )
                 getattr(copy, act)()
 
-            if low is None:
+            if places is None:
                 one()
             else:
-                pl.when(jnp.logical_and(z >= low, z <= high))(one)
+                here = z == places[0]
+                for place in places[1:]:
+                    here = jnp.logical_or(here, z == place)
+                pl.when(here)(one)
 
     q_copies = [
         pltpu.make_async_copy(q_refs[i], q_buf.at[pl.ds(i * tiles, tiles)], q_sem.at[i])
@@ -146,18 +148,17 @@
     kv = lax.axis_index("kv")
     b = kv * pb_size + pb
 
-    def move(x, pairs):
-        return lax.ppermute(x, AXES, pairs)
-
-    def swap(x, offset, low=0, high=z_size - 1):
-        return move(x, [
-            (i * z_size + h, (i ^ offset) * z_size + h)
-            for i in range(planes) for h in range(low, high + 1)
+    def swap(x, offset, places=tuple(range(z_size))):
+        return lax.ppermute(x, AXES, [
+            (i * z_size + h, (i ^ offset) * z_size + h) for i in range(planes) for h in places
         ])
 
-    lists = lax.all_gather(tile_lists, ("kv", "pb"), axis=0, tiled=True)
-
-    relay = kv_size == 2 and pb_size == 4 and z_size <= 4
+    def along(x, pairs):
+        return lax.ppermute(x, AXES, [
+            (i * z_size + h, i * z_size + k) for i in range(planes) for h, k in pairs
+        ])
+
+    relay = kv_size == 2 and pb_size == 4 and z_size == 4
     sides = (2, 4) if relay else (2, 2)
 
     def head_of(half, offset):
@@ -168,41 +169,51 @@
     def near(half):
         return (0, 1, sides[half], sides[half] + 1)
 
-    kv_bufs, kv_sources = [], []
+    own_lists = lax.dynamic_slice_in_dim(tile_lists, z * tiles, tiles, axis=0)
+    rider = jnp.concatenate([own_lists % 128, own_lists // 128], axis=0).astype(jnp.bfloat16)
+    rider = jnp.pad(rider, ((0, -(2 * tiles) % 16), (0, 2 * HEAD_DIM - SLOTS)))
+    own, lists = [], []
     for half in range(2):
-        blocks = []
+        blocks, riders = [], []
         for offset in near(half):
             at = head_of(half, offset) * HEAD_DIM
             piece = jnp.concatenate(
                 [lax.dynamic_slice_in_dim(a, at, HEAD_DIM, axis=1) for a in (key_rows, value_rows)],
                 axis=1,
             )
-            blocks.append(swap(piece, offset) if offset else piece)
-        own = jnp.concatenate(blocks, axis=0)
-        if relay:
-            across = 6 - sides[half]
-            bufs, sources = [own, swap(own, across)], [(lambda z: z * 2, None, None), (lambda z: z * 2 + 1, None, None)]
-            up = down = own
-            for step in range(1, z_size):
-                up = move(up, [
-                    (i * z_size + h, i * z_size + h + 1)
-                    for i in range(planes) for h in range(step - 1, z_size - 1)
-                ])
-                down = move(down, [
-                    (i * z_size + h, i * z_size + h - 1)
-                    for i in range(planes) for h in range(1, z_size - step + 1)
-                ])
-                for buf, shift, low, high in ((up, -step, step, z_size - 1), (down, step, 0, z_size - 1 - step)):
-                    bufs += [buf, swap(buf, across, low, high)]
-                    sources += [
-                        (lambda z, shift=shift: (z + shift) * 2, low, high),
-                        (lambda z, shift=shift: (z + shift) * 2 + 1, low, high),
-                    ]
-        else:
-            bufs = [lax.all_gather(own, ("kv", "head"), axis=0, tiled=True)]
-            sources = [(None, None, None)]
-        kv_bufs.append(bufs)
-        kv_sources.append(sources)
+            piece = jnp.concatenate([piece, rider], axis=0)
+            if offset:
+                piece = swap(piece, offset)
+            blocks.append(piece[:tokens])
+            parts = piece[tokens:tokens + 2 * tiles, :SLOTS].astype(jnp.int32)
+            riders.append(parts[:tiles] + 128 * parts[tiles:])
+        own.append(jnp.concatenate(blocks, axis=0))
+        lists.append(dict(zip(near(half), riders)))
+    *own, queries = lax.optimization_barrier((*own, queries))
+
+    kv_bufs, kv_sources = [[], []], [[], []]
+    if relay:
+        across = [6 - side for side in sides]
+
+        def add(half, buf, distance, places=None):
+            take = tuple(range(z_size)) if places is None else places
+            kv_bufs[half] += [buf, swap(buf, across[half], take)]
+            kv_sources[half] += [(distance * 2, places), (distance * 2 + 1, places)]
+
+        two = [along(x, ((0, 2), (1, 3), (2, 0), (3, 1))) for x in own]
+        one = [along(x, ((0, 1), (1, 0), (2, 3), (3, 2))) for x in own]
+        for half in range(2):
+            add(half, own[half], 0)
+            add(half, one[half], 1)
+            add(half, two[half], 2)
+            outer = along(two[half], ((1, 0), (2, 3)))
+            inner = along(own[half], ((1, 2), (2, 1)))
+            add(half, outer, 3, (0, 3))
+            add(half, inner, 3, (1, 2))
+    else:
+        for half in range(2):
+            kv_bufs[half].append(lax.all_gather(own[half], ("kv", "head"), axis=0, tiled=True))
+            kv_sources[half].append((0, None))
 
     def place(half, tile):
         device, within = tile // tiles, tile % tiles
@@ -211,8 +222,7 @@
         side = sides[half]
         slot = (differ & 1) + 2 * ((differ & side) // side)
         if relay:
-            across = 6 - side
-            block = (z_from * 2 + (differ & across) // across) * 4 + slot
+            block = ((z_from ^ z) * 2 + (differ & across[half]) // across[half]) * 4 + slot
         else:
             block = ((where // pb_size) * z_size + z_from) * 4 + slot
         return block * tiles + within
@@ -235,7 +245,7 @@
                 ((b ^ offset) * z_size + z) * tiles + jnp.arange(tiles, dtype=jnp.int32)
                 for offset in offsets
             ])
-            loc = place(half, jnp.take(lists, tid, axis=0))
+            loc = place(half, jnp.concatenate([lists[half][offset] for offset in offsets], axis=0))
             outs = attend(
                 [q_blocks[half][offset] for offset in offsets],
                 kv_bufs[half], kv_sources[half], planes * z_size * tiles, loc, tid, z,

time: 197 us -> 201 us (1.020)
  the two profiles are of different devices: /device:TPU:0 before, /device:TPU:17 now
where the time goes in v2:
time: 201 us; the launch traced here: 198 us
  waiting for transfers between devices  103 us (51%)
  starting transfers between devices  44.8 us (22%)
  Pallas kernels  36.6 us (18%)
  local copies, waits for them, and re-layouts  12.1 us (6%)
    ppermute x8, waiting for transfers between devices, along(): lax.ppermute(x, AXES, [(i * z_size + h, i * z_size + k) for i in range(pl...  55.5 us
    ppermute x28, waiting for transfers between devices, swap(): lax.ppermute(x, AXES, [(i * z_size + h, (i ^ offset) * z_size + h) for i...  47 us
    pallas_call x4, Pallas kernels, attend(): pl.pallas_call(functools.partial(attend_kernel, blocks, tiles, sources),...  36.6 us
    ppermute x28, starting transfers between devices, swap(): lax.ppermute(x, AXES, [(i * z_size + h, (i ^ offset) * z_size + h) for i...  29.7 us
    ppermute x8, starting transfers between devices, along(): lax.ppermute(x, AXES, [(i * z_size + h, i * z_size + k) for i in range(pl...  15.1 us
    dynamic_slice x1, local copies, waits for them, and re-layouts, per_device(): piece = lax.dynamic_slice_in_dim(queries, at, WIDE, axis=1)  4.05 us
  transfers between devices with their start and end apart: 36, of which 14 were waited for; matrix products, arithmetic and copies ran while one was open for 3% of the time, Pallas kernels for 19%

profile of v2, /device:TPU:17, one launch (start us, length us, event | category | flops | bytes accessed | tf_op | source)
XLA Modules:
  0.0 197.8 jit_solution(6523499558856512786)
XLA Ops:
  9.1 3.4 %collective-permute-done.5 = bf16[272,256]{1,0:T(8,128)(2,1)S(1)} collective-permute-done((bf16[272,256]{1,0:T(8,128)(2,1)S(1)}, bf16[272,256]{1,0:T(8,128)(2,1)S(1)}, u32[]{:S(2)}, u32[]{:S(2)}) %collective-permute-start.5) | collective-permute-done | bytes 139296 | tf_op jit(solution)/shard_map/ppermute | solution.py:152
  12.6 1.4 collective-permute-done
  14.2 1.4 collective-permute-start.22
  15.6 3.2 %collective-permute-start.28 = (bf16[1024,256]{1,0:T(8,128)(2,1)S(1)}, bf16[1024,256]{1,0:T(8,128)(2,1)S(1)}, u32[]{:S(2)}, u32[]{:S(2)}) collective-permute-start(bf16[1024,256]{1,0:T(8,128)(2,1)S(1)} %pad_maximum_fusion.1), channel_id=1, source_target_pairs={{1,2},{2,1},{5,6},{6,5},{9,10},{10,9},{13,14},{14,13},{17,18},{18,... | collective-permute-start | bytes 1572872 | tf_op jit(solution)/shard_map/ppermute | solution.py:157
  20.2 4.1 %constant_dynamic-slice_fusion = (bf16[256,1024]{1,0:T(8,128)(2,1)S(1)}, bf16[256,1024]{1,0:T(8,128)(2,1)}, bf16[256,1024]{1,0:T(8,128)(2,1)S(1)}, bf16[256,1024...) fusion(bf16[256,8192]{1,0:T(8,128)(2,1)} %param.4, ...), kind=kLoop, calls=%fused_computation.12 | loop fusion | bytes 8388640 | tf_op jit(solution)/shard_map/dynamic_slice | solution.py:235
  24.3 12.6 %collective-permute-done.24 = bf16[1024,256]{1,0:T(8,128)(2,1)S(1)} collective-permute-done((bf16[1024,256]{1,0:T(8,128)(2,1)S(1)}, bf16[1024,256]{1,0:T(8,128)(2,1)S(1)}, u32[]{:S(2)}, u32[]{:S(2)}) %collective-permute-start.24) | collective-permute-done | bytes 524320 | tf_op jit(solution)/shard_map/ppermute | solution.py:157
  36.9 4.6 %collective-permute-start.15 = (bf16[1024,256]{1,0:T(8,128)(2,1)S(1)}, bf16[1024,256]{1,0:T(8,128)(2,1)}, u32[]{:S(2)}, u32[]{:S(2)}) collective-permute-start(bf16[1024,256]{1,0:T(8,128)(2,1)S(1)} %pad_maximum_fusion), channel_id=1, source_target_pairs={{1,2},{2,1},{5,6},{6,5},{9,10},{10,9},{13,14},{14,13},{17,18},{18,... | collective-permute-start | bytes 1572872 | tf_op jit(solution)/shard_map/ppermute | solution.py:157
  41.5 1.7 collective-permute-start.9
  43.1 19.6 %collective-permute-done.28 = bf16[1024,256]{1,0:T(8,128)(2,1)S(1)} collective-permute-done((bf16[1024,256]{1,0:T(8,128)(2,1)S(1)}, bf16[1024,256]{1,0:T(8,128)(2,1)S(1)}, u32[]{:S(2)}, u32[]{:S(2)}) %collective-permute-start.28) | collective-permute-done | bytes 524320 | tf_op jit(solution)/shard_map/ppermute | solution.py:157
  66.6 4.0 %collective-permute-done.11 = bf16[1024,256]{1,0:T(8,128)(2,1)} collective-permute-done((bf16[1024,256]{1,0:T(8,128)(2,1)S(1)}, bf16[1024,256]{1,0:T(8,128)(2,1)}, u32[]{:S(2)}, u32[]{:S(2)}) %collective-permute-start.11) | collective-permute-done | bytes 524320 | tf_op jit(solution)/shard_map/ppermute | solution.py:157
  70.6 1.4 collective-permute-start.20
  72.0 13.4 %collective-permute-done.15 = bf16[1024,256]{1,0:T(8,128)(2,1)} collective-permute-done((bf16[1024,256]{1,0:T(8,128)(2,1)S(1)}, bf16[1024,256]{1,0:T(8,128)(2,1)}, u32[]{:S(2)}, u32[]{:S(2)}) %collective-permute-start.15) | collective-permute-done | bytes 524320 | tf_op jit(solution)/shard_map/ppermute | solution.py:157
  85.3 1.5 collective-permute-start.6
  86.8 2.1 %collective-permute-start.13 = (bf16[1024,256]{1,0:T(8,128)(2,1)}, bf16[1024,256]{1,0:T(8,128)(2,1)}, u32[]{:S(2)}, u32[]{:S(2)}) collective-permute-start(bf16[1024,256]{1,0:T(8,128)(2,1)} %collective-permute-done.11), channel_id=1, source_target_pairs={{1,0},{2,3},{5,4},{6,7},{9,8},{10,11},{13,12},{14,15},{17,16},{18,... | collective-permute-start | bytes 1572872 | tf_op jit(solution)/shard_map/ppermute | solution.py:157
  89.1 2.1 %collective-permute-start.26 = (bf16[1024,256]{1,0:T(8,128)(2,1)S(1)}, bf16[1024,256]{1,0:T(8,128)(2,1)}, u32[]{:S(2)}, u32[]{:S(2)}) collective-permute-start(bf16[1024,256]{1,0:T(8,128)(2,1)S(1)} %collective-permute-done.24), channel_id=1, source_target_pairs={{1,0},{2,3},{5,4},{6,7},{9,8},{10,11},{13,12},{14,15},{17,16},{18,... | collective-permute-start | bytes 1572872 | tf_op jit(solution)/shard_map/ppermute | solution.py:157
  91.2 1.3 collective-permute-start.12
  92.5 7.4 %collective-permute-done.20 = bf16[256,1024]{1,0:T(8,128)(2,1)} collective-permute-done((bf16[256,1024]{1,0:T(8,128)(2,1)}, bf16[256,1024]{1,0:T(8,128)(2,1)}, u32[]{:S(2)}, u32[]{:S(2)}) %collective-permute-start.20) | collective-permute-done | bytes 524320 | tf_op jit(solution)/shard_map/ppermute | solution.py:152
  100.0 3.1 %collective-permute-start.16 = (bf16[1024,256]{1,0:T(8,128)(2,1)}, bf16[1024,256]{1,0:T(8,128)(2,1)}, u32[]{:S(2)}, u32[]{:S(2)}) collective-permute-start(bf16[1024,256]{1,0:T(8,128)(2,1)} %collective-permute-done.15), channel_id=1, source_target_pairs={{1,17},{2,18},{5,21},{6,22},{9,25},{10,26},{13,29},{14,30},{17,1},... | collective-permute-start | bytes 1572872 | tf_op jit(solution)/shard_map/ppermute | solution.py:152
  103.4 1.5 collective-permute-start.14
  105.1 6.0 %collective-permute-done.26 = bf16[1024,256]{1,0:T(8,128)(2,1)} collective-permute-done((bf16[1024,256]{1,0:T(8,128)(2,1)S(1)}, bf16[1024,256]{1,0:T(8,128)(2,1)}, u32[]{:S(2)}, u32[]{:S(2)}) %collective-permute-start.26) | collective-permute-done | bytes 524320 | tf_op jit(solution)/shard_map/ppermute | solution.py:157
  111.3 11.1 %collective-permute-done.16 = bf16[1024,256]{1,0:T(8,128)(2,1)} collective-permute-done((bf16[1024,256]{1,0:T(8,128)(2,1)}, bf16[1024,256]{1,0:T(8,128)(2,1)}, u32[]{:S(2)}, u32[]{:S(2)}) %collective-permute-start.16) | collective-permute-done | bytes 524320 | tf_op jit(solution)/shard_map/ppermute | solution.py:152
  123.6 10.0 %collective-permute-done.10 = bf16[1024,256]{1,0:T(8,128)(2,1)} collective-permute-done((bf16[1024,256]{1,0:T(8,128)(2,1)}, bf16[1024,256]{1,0:T(8,128)(2,1)}, u32[]{:S(2)}, u32[]{:S(2)}) %collective-permute-start.10) | collective-permute-done | bytes 524320 | tf_op jit(solution)/shard_map/ppermute | solution.py:152
  134.9 2.2 %collective-permute-start.29 = (bf16[1024,256]{1,0:T(8,128)(2,1)}, bf16[1024,256]{1,0:T(8,128)(2,1)S(1)}, u32[]{:S(2)}, u32[]{:S(2)}) collective-permute-start(bf16[1024,256]{1,0:T(8,128)(2,1)} %copy-done.4), channel_id=1, source_target_pairs={{1,9},{2,10},{5,13},{6,14},{9,1},{10,2},{13,5},{14,6},{17,25},{18,... | collective-permute-start | bytes 1572872 | tf_op jit(solution)/shard_map/ppermute | solution.py:152
  137.9 9.4 %shard_map.48 = (bf16[2,128,1024]{2,1,0:T(8,128)(2,1)S(1)}, bf16[2,128,1024]{2,1,0:T(8,128)(2,1)S(1)}) custom-call(s32[32]{0:T(128)S(1)} %fusion.11.loc_ref, s32[4]{0:T(128)S(1)} %pad_add_fusion.6.tid_ref, s32[1]{0:T(128)} %bitcast.z_ref, bf16[2,128,1024]{2,1,0:T(8,128)(2,1)} %bitcast.29.refs_0_, bf16[2,128,1024]{2,1,0:T(8,128)(2,1)S(1)} %bitcast.44, ...), custom_call_target="tpu_custom_call" | custom-call | flops 4294967296 | bytes 6291456 | tf_op jit(solution)/shard_map/pallas_call | solution.py:118
  147.4 1.6 collective-permute-start.34
  149.0 9.6 %shard_map.46 = (bf16[2,128,1024]{2,1,0:T(8,128)(2,1)S(1)}, bf16[2,128,1024]{2,1,0:T(8,128)(2,1)S(1)}) custom-call(s32[32]{0:T(128)S(1)} %fusion.9.loc_ref, s32[4]{0:T(128)S(1)} %pad_add_fusion.4.tid_ref, s32[1]{0:T(128)} %bitcast.z_ref, bf16[2,128,1024]{2,1,0:T(8,128)(2,1)} %bitcast.1.refs_0_, bf16[2,128,1024]{2,1,0:T(8,128)(2,1)S(1)} %bitcast.62, ...), custom_call_target="tpu_custom_call" | custom-call | flops 4294967296 | bytes 6291456 | tf_op jit(solution)/shard_map/pallas_call | solution.py:118
  158.7 1.6 collective-permute-start.17
  161.3 8.8 %shard_map.47 = (bf16[2,128,1024]{2,1,0:T(8,128)(2,1)S(1)}, bf16[2,128,1024]{2,1,0:T(8,128)(2,1)S(1)}) custom-call(s32[32]{0:T(128)S(1)} %fusion.10.loc_ref, s32[4]{0:T(128)S(1)} %pad_add_fusion.5.tid_ref, s32[1]{0:T(128)} %bitcast.z_ref, bf16[2,128,1024]{2,1,0:T(8,128)(2,1)} %bitcast.15.refs_0_, bf16[2,128,1024]{2,1,0:T(8,128)(2,1)} %bitcast.16.refs_1_, ...), custom_call_target="tpu_custom_call" | custom-call | flops 4294967296 | bytes 6291456 | tf_op jit(solution)/shard_map/pallas_call | solution.py:118
  171.8 8.8 %shard_map.49 = (bf16[2,128,1024]{2,1,0:T(8,128)(2,1)S(1)}, bf16[2,128,1024]{2,1,0:T(8,128)(2,1)S(1)}) custom-call(s32[32]{0:T(128)S(1)} %fusion.12.loc_ref, s32[4]{0:T(128)S(1)} %pad_add_fusion.6.tid_ref, s32[1]{0:T(128)} %bitcast.z_ref, bf16[2,128,1024]{2,1,0:T(8,128)(2,1)S(1)} %bitcast.57, bf16[2,128,1024]{2,1,0:T(8,128)(2,1)S(1)} %bitcast.43, ...), custom_call_target="tpu_custom_call" | custom-call | flops 4294967296 | bytes 6291456 | tf_op jit(solution)/shard_map/pallas_call | solution.py:118
  182.2 2.2 %collective-permute-done.18 = bf16[256,1024]{1,0:T(8,128)(2,1)S(1)} collective-permute-done((bf16[256,1024]{1,0:T(8,128)(2,1)S(1)}, bf16[256,1024]{1,0:T(8,128)(2,1)S(1)}, u32[]{:S(2)}, u32[]{:S(2)}) %collective-permute-start.18) | collective-permute-done | bytes 524320 | tf_op jit(solution)/shard_map/ppermute | solution.py:152
  184.7 10.1 %collective-permute-done.31 = bf16[256,1024]{1,0:T(8,128)(2,1)S(1)} collective-permute-done((bf16[256,1024]{1,0:T(8,128)(2,1)S(1)}, bf16[256,1024]{1,0:T(8,128)(2,1)S(1)}, u32[]{:S(2)}, u32[]{:S(2)}) %collective-permute-start.31) | collective-permute-done | bytes 524320 | tf_op jit(solution)/shard_map/ppermute | solution.py:152
  195.0 2.0 %copy-done.2 = bf16[256,8192]{1,0:T(8,128)(2,1)} copy-done((bf16[256,8192]{1,0:T(8,128)(2,1)}, bf16[256,8192]{1,0:T(8,128)(2,1)S(1)}, u32[]{:S(2)}) %copy-start.2) | copy-done | bytes 4194328
  (110 shorter events, 24.4 us)
Async XLA Ops:
  5.1 7.4 %collective-permute-start.5 = (bf16[272,256]{1,0:T(8,128)(2,1)S(1)}, bf16[272,256]{1,0:T(8,128)(2,1)S(1)}, u32[]{:S(2)}, u32[]{:S(2)}) collective-permute-start(bf16[272,256]{1,0:T(8,128)(2,1)S(1)} %get-tuple-element.62), channel_id=1, source_target_pairs={{0,20},{1,21},{2,22},{3,23},{4,16},{5,17},{6,18},{7,19},{8,28},{9,... | collective-permute-start | bytes 417800 | tf_op jit(solution)/shard_map/ppermute | solution.py:152
  5.5 7.0 %collective-permute-start.2 = (bf16[272,256]{1,0:T(8,128)(2,1)S(1)}, bf16[272,256]{1,0:T(8,128)(2,1)S(1)}, u32[]{:S(2)}, u32[]{:S(2)}) collective-permute-start(bf16[272,256]{1,0:T(8,128)(2,1)S(1)} %get-tuple-element.59), channel_id=1, source_target_pairs={{0,4},{1,5},{2,6},{3,7},{4,0},{5,1},{6,2},{7,3},{8,12},{9,13},{10,... | collective-permute-start | bytes 417800 | tf_op jit(solution)/shard_map/ppermute | solution.py:152
  7.1 7.0 %collective-permute-start = (bf16[272,256]{1,0:T(8,128)(2,1)S(1)}, bf16[272,256]{1,0:T(8,128)(2,1)S(1)}, u32[]{:S(2)}, u32[]{:S(2)}) collective-permute-start(bf16[272,256]{1,0:T(8,128)(2,1)S(1)} %get-tuple-element.61), channel_id=1, source_target_pairs={{0,12},{1,13},{2,14},{3,15},{4,8},{5,9},{6,10},{7,11},{8,4},{9,5},... | collective-permute-start | bytes 417800 | tf_op jit(solution)/shard_map/ppermute | solution.py:152
  14.2 22.7 %collective-permute-start.24 = (bf16[1024,256]{1,0:T(8,128)(2,1)S(1)}, bf16[1024,256]{1,0:T(8,128)(2,1)S(1)}, u32[]{:S(2)}, u32[]{:S(2)}) collective-permute-start(bf16[1024,256]{1,0:T(8,128)(2,1)S(1)} %pad_maximum_fusion.1), channel_id=1, source_target_pairs={{0,2},{1,3},{2,0},{3,1},{4,6},{5,7},{6,4},{7,5},{8,10},{9,11},{10,... | collective-permute-start | bytes 1572872 | tf_op jit(solution)/shard_map/ppermute | solution.py:157
  14.2 27.2 %collective-permute-start.22 = (bf16[1024,256]{1,0:T(8,128)(2,1)S(1)}, bf16[1024,256]{1,0:T(8,128)(2,1)S(1)}, u32[]{:S(2)}, u32[]{:S(2)}) collective-permute-start(bf16[1024,256]{1,0:T(8,128)(2,1)S(1)} %pad_maximum_fusion.1), channel_id=1, source_target_pairs={{0,1},{1,0},{2,3},{3,2},{4,5},{5,4},{6,7},{7,6},{8,9},{9,8},{10,11... | collective-permute-start | bytes 1572872 | tf_op jit(solution)/shard_map/ppermute | solution.py:157
  15.6 47.1 %collective-permute-start.28 = (bf16[1024,256]{1,0:T(8,128)(2,1)S(1)}, bf16[1024,256]{1,0:T(8,128)(2,1)S(1)}, u32[]{:S(2)}, u32[]{:S(2)}) collective-permute-start(bf16[1024,256]{1,0:T(8,128)(2,1)S(1)} %pad_maximum_fusion.1), channel_id=1, source_target_pairs={{1,2},{2,1},{5,6},{6,5},{9,10},{10,9},{13,14},{14,13},{17,18},{18,... | collective-permute-start | bytes 1572872 | tf_op jit(solution)/shard_map/ppermute | solution.py:157
  18.8 44.4 %collective-permute-start.21 = (bf16[1024,256]{1,0:T(8,128)(2,1)S(1)}, bf16[1024,256]{1,0:T(8,128)(2,1)S(1)}, u32[]{:S(2)}, u32[]{:S(2)}) collective-permute-start(bf16[1024,256]{1,0:T(8,128)(2,1)S(1)} %pad_maximum_fusion.1), channel_id=1, source_target_pairs={{0,8},{1,9},{2,10},{3,11},{4,12},{5,13},{6,14},{7,15},{8,0},{9,1},... | collective-permute-start | bytes 1572872 | tf_op jit(solution)/shard_map/ppermute | solution.py:152
  20.1 50.4 %collective-permute-start.11 = (bf16[1024,256]{1,0:T(8,128)(2,1)S(1)}, bf16[1024,256]{1,0:T(8,128)(2,1)}, u32[]{:S(2)}, u32[]{:S(2)}) collective-permute-start(bf16[1024,256]{1,0:T(8,128)(2,1)S(1)} %pad_maximum_fusion), channel_id=1, source_target_pairs={{0,2},{1,3},{2,0},{3,1},{4,6},{5,7},{6,4},{7,5},{8,10},{9,11},{10,... | collective-permute-start | bytes 1572872 | tf_op jit(solution)/shard_map/ppermute | solution.py:157
  36.9 48.4 %collective-permute-start.15 = (bf16[1024,256]{1,0:T(8,128)(2,1)S(1)}, bf16[1024,256]{1,0:T(8,128)(2,1)}, u32[]{:S(2)}, u32[]{:S(2)}) collective-permute-start(bf16[1024,256]{1,0:T(8,128)(2,1)S(1)} %pad_maximum_fusion), channel_id=1, source_target_pairs={{1,2},{2,1},{5,6},{6,5},{9,10},{10,9},{13,14},{14,13},{17,18},{18,... | collective-permute-start | bytes 1572872 | tf_op jit(solution)/shard_map/ppermute | solution.py:157
  41.5 45.4 %collective-permute-start.9 = (bf16[1024,256]{1,0:T(8,128)(2,1)S(1)}, bf16[1024,256]{1,0:T(8,128)(2,1)}, u32[]{:S(2)}, u32[]{:S(2)}) collective-permute-start(bf16[1024,256]{1,0:T(8,128)(2,1)S(1)} %pad_maximum_fusion), channel_id=1, source_target_pairs={{0,1},{1,0},{2,3},{3,2},{4,5},{5,4},{6,7},{7,6},{8,9},{9,8},{10,11... | collective-permute-start | bytes 1572872 | tf_op jit(solution)/shard_map/ppermute | solution.py:157
  64.0 25.1 %collective-permute-start.8 = (bf16[1024,256]{1,0:T(8,128)(2,1)S(1)}, bf16[1024,256]{1,0:T(8,128)(2,1)}, u32[]{:S(2)}, u32[]{:S(2)}) collective-permute-start(bf16[1024,256]{1,0:T(8,128)(2,1)S(1)} %pad_maximum_fusion), channel_id=1, source_target_pairs={{0,16},{1,17},{2,18},{3,19},{4,20},{5,21},{6,22},{7,23},{8,24},{9,... | collective-permute-start | bytes 1572872 | tf_op jit(solution)/shard_map/ppermute | solution.py:152
  65.4 25.9 %collective-permute-start.19 = (bf16[256,1024]{1,0:T(8,128)(2,1)}, bf16[256,1024]{1,0:T(8,128)(2,1)}, u32[]{:S(2)}, u32[]{:S(2)}) collective-permute-start(bf16[256,1024]{1,0:T(8,128)(2,1)} %get-tuple-element.32), channel_id=1, source_target_pairs={{0,20},{1,21},{2,22},{3,23},{4,16},{5,17},{6,18},{7,19},{8,28},{9,... | collective-permute-start | bytes 1572872 | tf_op jit(solution)/shard_map/ppermute | solution.py:152
  70.6 29.4 %collective-permute-start.20 = (bf16[256,1024]{1,0:T(8,128)(2,1)}, bf16[256,1024]{1,0:T(8,128)(2,1)}, u32[]{:S(2)}, u32[]{:S(2)}) collective-permute-start(bf16[256,1024]{1,0:T(8,128)(2,1)} %get-tuple-element.31), channel_id=1, source_target_pairs={{0,16},{1,17},{2,18},{3,19},{4,20},{5,21},{6,22},{7,23},{8,24},{9,... | collective-permute-start | bytes 1572872 | tf_op jit(solution)/shard_map/ppermute | solution.py:152
  85.3 17.8 %collective-permute-start.6 = (bf16[256,1024]{1,0:T(8,128)(2,1)}, bf16[256,1024]{1,0:T(8,128)(2,1)}, u32[]{:S(2)}, u32[]{:S(2)}) collective-permute-start(bf16[256,1024]{1,0:T(8,128)(2,1)} %get-tuple-element.34), channel_id=1, source_target_pairs={{0,12},{1,13},{2,14},{3,15},{4,8},{5,9},{6,10},{7,11},{8,4},{9,5},... | collective-permute-start | bytes 1572872 | tf_op jit(solution)/shard_map/ppermute | solution.py:152
  86.8 16.6 %collective-permute-start.13 = (bf16[1024,256]{1,0:T(8,128)(2,1)}, bf16[1024,256]{1,0:T(8,128)(2,1)}, u32[]{:S(2)}, u32[]{:S(2)}) collective-permute-start(bf16[1024,256]{1,0:T(8,128)(2,1)} %collective-permute-done.11), channel_id=1, source_target_pairs={{1,0},{2,3},{5,4},{6,7},{9,8},{10,11},{13,12},{14,15},{17,16},{18,... | collective-permute-start | bytes 1572872 | tf_op jit(solution)/shard_map/ppermute | solution.py:157
  89.1 21.9 %collective-permute-start.26 = (bf16[1024,256]{1,0:T(8,128)(2,1)S(1)}, bf16[1024,256]{1,0:T(8,128)(2,1)}, u32[]{:S(2)}, u32[]{:S(2)}) collective-permute-start(bf16[1024,256]{1,0:T(8,128)(2,1)S(1)} %collective-permute-done.24), channel_id=1, source_target_pairs={{1,0},{2,3},{5,4},{6,7},{9,8},{10,11},{13,12},{14,15},{17,16},{18,... | collective-permute-start | bytes 1572872 | tf_op jit(solution)/shard_map/ppermute | solution.py:157
  91.2 43.6 %collective-permute-start.12 = (bf16[1024,256]{1,0:T(8,128)(2,1)}, bf16[1024,256]{1,0:T(8,128)(2,1)}, u32[]{:S(2)}, u32[]{:S(2)}) collective-permute-start(bf16[1024,256]{1,0:T(8,128)(2,1)} %collective-permute-done.11), channel_id=1, source_target_pairs={{0,16},{1,17},{2,18},{3,19},{4,20},{5,21},{6,22},{7,23},{8,24},{9,... | collective-permute-start | bytes 1572872 | tf_op jit(solution)/shard_map/ppermute | solution.py:152
  100.0 22.5 %collective-permute-start.16 = (bf16[1024,256]{1,0:T(8,128)(2,1)}, bf16[1024,256]{1,0:T(8,128)(2,1)}, u32[]{:S(2)}, u32[]{:S(2)}) collective-permute-start(bf16[1024,256]{1,0:T(8,128)(2,1)} %collective-permute-done.15), channel_id=1, source_target_pairs={{1,17},{2,18},{5,21},{6,22},{9,25},{10,26},{13,29},{14,30},{17,1},... | collective-permute-start | bytes 1572872 | tf_op jit(solution)/shard_map/ppermute | solution.py:152
  103.1 30.5 %collective-permute-start.10 = (bf16[1024,256]{1,0:T(8,128)(2,1)}, bf16[1024,256]{1,0:T(8,128)(2,1)}, u32[]{:S(2)}, u32[]{:S(2)}) collective-permute-start(bf16[1024,256]{1,0:T(8,128)(2,1)} %collective-permute-done.9), channel_id=1, source_target_pairs={{0,16},{1,17},{2,18},{3,19},{4,20},{5,21},{6,22},{7,23},{8,24},{9,... | collective-permute-start | bytes 1572872 | tf_op jit(solution)/shard_map/ppermute | solution.py:152
  103.4 33.6 %collective-permute-start.14 = (bf16[1024,256]{1,0:T(8,128)(2,1)}, bf16[1024,256]{1,0:T(8,128)(2,1)}, u32[]{:S(2)}, u32[]{:S(2)}) collective-permute-start(bf16[1024,256]{1,0:T(8,128)(2,1)} %collective-permute-done.13), channel_id=1, source_target_pairs={{0,16},{3,19},{4,20},{7,23},{8,24},{11,27},{12,28},{15,31},{16,0},... | collective-permute-start | bytes 1572872 | tf_op jit(solution)/shard_map/ppermute | solution.py:152
  111.0 36.4 %collective-permute-start.7 = (bf16[256,1024]{1,0:T(8,128)(2,1)}, bf16[256,1024]{1,0:T(8,128)(2,1)S(1)}, u32[]{:S(2)}, u32[]{:S(2)}) collective-permute-start(bf16[256,1024]{1,0:T(8,128)(2,1)} %get-tuple-element.33), channel_id=1, source_target_pairs={{0,8},{1,9},{2,10},{3,11},{4,12},{5,13},{6,14},{7,15},{8,0},{9,1},... | collective-permute-start | bytes 1572872 | tf_op jit(solution)/shard_map/ppermute | solution.py:152
  122.4 36.3 %collective-permute-start.25 = (bf16[1024,256]{1,0:T(8,128)(2,1)S(1)}, bf16[1024,256]{1,0:T(8,128)(2,1)S(1)}, u32[]{:S(2)}, u32[]{:S(2)}) collective-permute-start(bf16[1024,256]{1,0:T(8,128)(2,1)S(1)} %collective-permute-done.24), channel_id=1, source_target_pairs={{0,8},{1,9},{2,10},{3,11},{4,12},{5,13},{6,14},{7,15},{8,0},{9,1},... | collective-permute-start | bytes 1572872 | tf_op jit(solution)/shard_map/ppermute | solution.py:152
  133.7 25.0 %collective-permute-start.23 = (bf16[1024,256]{1,0:T(8,128)(2,1)S(1)}, bf16[1024,256]{1,0:T(8,128)(2,1)S(1)}, u32[]{:S(2)}, u32[]{:S(2)}) collective-permute-start(bf16[1024,256]{1,0:T(8,128)(2,1)S(1)} %collective-permute-done.22), channel_id=1, source_target_pairs={{0,8},{1,9},{2,10},{3,11},{4,12},{5,13},{6,14},{7,15},{8,0},{9,1},... | collective-permute-start | bytes 1572872 | tf_op jit(solution)/shard_map/ppermute | solution.py:152
  134.9 25.4 %collective-permute-start.29 = (bf16[1024,256]{1,0:T(8,128)(2,1)}, bf16[1024,256]{1,0:T(8,128)(2,1)S(1)}, u32[]{:S(2)}, u32[]{:S(2)}) collective-permute-start(bf16[1024,256]{1,0:T(8,128)(2,1)} %copy-done.4), channel_id=1, source_target_pairs={{1,9},{2,10},{5,13},{6,14},{9,1},{10,2},{13,5},{14,6},{17,25},{18,... | collective-permute-start | bytes 1572872 | tf_op jit(solution)/shard_map/ppermute | solution.py:152
  137.0 23.3 %collective-permute-start.27 = (bf16[1024,256]{1,0:T(8,128)(2,1)}, bf16[1024,256]{1,0:T(8,128)(2,1)S(1)}, u32[]{:S(2)}, u32[]{:S(2)}) collective-permute-start(bf16[1024,256]{1,0:T(8,128)(2,1)} %collective-permute-done.26), channel_id=1, source_target_pairs={{0,8},{3,11},{4,12},{7,15},{8,0},{11,3},{12,4},{15,7},{16,24},{19,... | collective-permute-start | bytes 1572872 | tf_op jit(solution)/shard_map/ppermute | solution.py:152
  147.4 24.2 %collective-permute-start.34 = (bf16[256,1024]{1,0:T(8,128)(2,1)S(1)}, bf16[256,1024]{1,0:T(8,128)(2,1)S(1)}, u32[]{:S(2)}, u32[]{:S(2)}) collective-permute-start(bf16[256,1024]{1,0:T(8,128)(2,1)S(1)} %copy-done.3), channel_id=1, source_target_pairs={{0,4},{1,5},{2,6},{3,7},{4,0},{5,1},{6,2},{7,3},{8,12},{9,13},{10,... | collective-permute-start | bytes 1572872 | tf_op jit(solution)/shard_map/ppermute | solution.py:152
  158.6 36.2 %collective-permute-start.33 = (bf16[256,1024]{1,0:T(8,128)(2,1)S(1)}, bf16[256,1024]{1,0:T(8,128)(2,1)S(1)}, u32[]{:S(2)}, u32[]{:S(2)}) collective-permute-start(bf16[256,1024]{1,0:T(8,128)(2,1)S(1)} %bitcast.51), channel_id=1, source_target_pairs={{0,4},{1,5},{2,6},{3,7},{4,0},{5,1},{6,2},{7,3},{8,12},{9,13},{10,... | collective-permute-start | bytes 1572872 | tf_op jit(solution)/shard_map/ppermute | solution.py:152
  158.7 21.9 %collective-permute-start.17 = (bf16[256,1024]{1,0:T(8,128)(2,1)S(1)}, bf16[256,1024]{1,0:T(8,128)(2,1)S(1)}, u32[]{:S(2)}, u32[]{:S(2)}) collective-permute-start(bf16[256,1024]{1,0:T(8,128)(2,1)S(1)} %bitcast.58), channel_id=1, source_target_pairs={{0,12},{1,13},{2,14},{3,15},{4,8},{5,9},{6,10},{7,11},{8,4},{9,5},... | collective-permute-start | bytes 1572872 | tf_op jit(solution)/shard_map/ppermute | solution.py:152
  170.1 14.5 %collective-permute-start.30 = (bf16[256,1024]{1,0:T(8,128)(2,1)S(1)}, bf16[256,1024]{1,0:T(8,128)(2,1)S(1)}, u32[]{:S(2)}, u32[]{:S(2)}) collective-permute-start(bf16[256,1024]{1,0:T(8,128)(2,1)S(1)} %bitcast.61), channel_id=1, source_target_pairs={{0,20},{1,21},{2,22},{3,23},{4,16},{5,17},{6,18},{7,19},{8,28},{9,... | collective-permute-start | bytes 1572872 | tf_op jit(solution)/shard_map/ppermute | solution.py:152
  171.4 13.1 %collective-permute-start.18 = (bf16[256,1024]{1,0:T(8,128)(2,1)S(1)}, bf16[256,1024]{1,0:T(8,128)(2,1)S(1)}, u32[]{:S(2)}, u32[]{:S(2)}) collective-permute-start(bf16[256,1024]{1,0:T(8,128)(2,1)S(1)} %bitcast.56), channel_id=1, source_target_pairs={{0,8},{1,9},{2,10},{3,11},{4,12},{5,13},{6,14},{7,15},{8,0},{9,1},... | collective-permute-start | bytes 1572872 | tf_op jit(solution)/shard_map/ppermute | solution.py:152
  171.6 23.2 %collective-permute-start.31 = (bf16[256,1024]{1,0:T(8,128)(2,1)S(1)}, bf16[256,1024]{1,0:T(8,128)(2,1)S(1)}, u32[]{:S(2)}, u32[]{:S(2)}) collective-permute-start(bf16[256,1024]{1,0:T(8,128)(2,1)S(1)} %bitcast.59), channel_id=1, source_target_pairs={{0,16},{1,17},{2,18},{3,19},{4,20},{5,21},{6,22},{7,23},{8,24},{9,... | collective-permute-start | bytes 1572872 | tf_op jit(solution)/shard_map/ppermute | solution.py:152
  180.6 14.3 %collective-permute-start.35 = (bf16[256,1024]{1,0:T(8,128)(2,1)S(1)}, bf16[256,1024]{1,0:T(8,128)(2,1)S(1)}, u32[]{:S(2)}, u32[]{:S(2)}) collective-permute-start(bf16[256,1024]{1,0:T(8,128)(2,1)S(1)} %bitcast.60), channel_id=1, source_target_pairs={{0,4},{1,5},{2,6},{3,7},{4,0},{5,1},{6,2},{7,3},{8,12},{9,13},{10,... | collective-permute-start | bytes 1572872 | tf_op jit(solution)/shard_map/ppermute | solution.py:152
  (11 other events, 47.6 us)

commit v3 on v2

--- a/solution.py
+++ b/solution.py
@@ -48,40 +48,26 @@
         out_buf[tile, :, columns] = (total[:, :HEAD_DIM] / total[:, HEAD_DIM:]).astype(jnp.bfloat16)
 
 
-def attend_kernel(blocks, tiles, sources, loc_ref, tid_ref, z_ref, *refs):
+def attend_kernel(blocks, tiles, starts, loc_ref, tid_ref, col_ref, *refs):
     q_refs, refs = refs[:blocks], refs[blocks:]
-    kv_refs, refs = refs[:len(sources)], refs[len(sources):]
+    kv_refs, refs = refs[:len(starts)], refs[len(starts):]
     out_refs, (q_buf, kv_buf, out_buf, q_sem, kv_sem, out_sem) = refs[:blocks], refs[blocks:]
-    z = z_ref[0]
-
-    def kv_copies(act):
-        for i, (at, places) in enumerate(sources):
-            rows = kv_refs[i].shape[0]
-
-            def one(i=i, at=at, rows=rows):
-                copy = pltpu.make_async_copy(
-                    kv_refs[i], kv_buf.at[pl.ds(at * rows, rows)], kv_sem.at[i]
-                )
-                getattr(copy, act)()
-
-            if places is None:
-                one()
-            else:
-                here = z == places[0]
-                for place in places[1:]:
-                    here = jnp.logical_or(here, z == place)
-                pl.when(here)(one)
-
-    q_copies = [
-        pltpu.make_async_copy(q_refs[i], q_buf.at[pl.ds(i * tiles, tiles)], q_sem.at[i])
+    copies = [
+        pltpu.make_async_copy(
+            q_refs[i].at[:, :, pl.ds(pl.multiple_of(col_ref[i], WIDE), WIDE)],
+            q_buf.at[pl.ds(i * tiles, tiles)], q_sem.at[i],
+        )
         for i in range(blocks)
+    ] + [
+        pltpu.make_async_copy(
+            kv_refs[i], kv_buf.at[pl.ds(start, kv_refs[i].shape[0])], kv_sem.at[i]
+        )
+        for i, start in enumerate(starts)
     ]
-    for copy in q_copies:
+    for copy in copies:
         copy.start()
-    kv_copies("start")
-    for copy in q_copies:
+    for copy in copies:
         copy.wait()
-    kv_copies("wait")
 
     def one_tile(tile, _):
         live = jnp.minimum(tid_ref[tile] + 1, SLOTS)
@@ -107,16 +93,20 @@
         copy.wait()
 
 
-def attend(q_blocks, kv_bufs, sources, kv_tiles, loc, tid, z):
+def attend(tiles, q_blocks, kv_bufs, loc, tid):
     blocks = len(q_blocks)
-    tiles = q_blocks[0].shape[0] // TILE
-    q_blocks = [q.reshape(tiles, TILE, WIDE) for q in q_blocks]
+    queries = [q.reshape(tiles, TILE, -1) for q, _ in q_blocks]
+    columns = jnp.stack([jnp.asarray(at, jnp.int32) for _, at in q_blocks])
     kv_bufs = [kv.reshape(-1, TILE, 2 * HEAD_DIM) for kv in kv_bufs]
+    starts, kv_tiles = [], 0
+    for kv in kv_bufs:
+        starts.append(kv_tiles)
+        kv_tiles += kv.shape[0]
     smem = pl.BlockSpec(memory_space=pltpu.SMEM)
     hbm = pl.BlockSpec(memory_space=pl.ANY)
     units = blocks * tiles
     out = pl.pallas_call(
-        functools.partial(attend_kernel, blocks, tiles, sources),
+        functools.partial(attend_kernel, blocks, tiles, starts),
         out_shape=[jax.ShapeDtypeStruct((tiles, TILE, WIDE), jnp.bfloat16)] * blocks,
         in_specs=[smem] * 3 + [hbm] * (blocks + len(kv_bufs)),
         out_specs=[hbm] * blocks,
@@ -128,13 +118,13 @@
             pltpu.SemaphoreType.DMA((len(kv_bufs),)),
             pltpu.SemaphoreType.DMA((blocks,)),
         ],
-        compiler_params=pltpu.CompilerParams(vmem_limit_bytes=48 * 2**20),
+        compiler_params=pltpu.CompilerParams(vmem_limit_bytes=32 * 2**20),
         cost_estimate=pl.CostEstimate(
             flops=units * 4 * GROUPS * TILE * TILE * SLOTS * HEAD_DIM * 2,
             bytes_accessed=kv_tiles * TILE * 4 * HEAD_DIM + units * TILE * WIDE * 4,
             transcendentals=units * GROUPS * TILE * TILE * SLOTS,
         ),
-    )(loc.reshape(-1), tid, z.reshape(1), *q_blocks, *kv_bufs)
+    )(loc.reshape(-1), tid, columns, *queries, *kv_bufs)
     return [o.reshape(tiles * TILE, WIDE) for o in out]
 
 
@@ -144,13 +134,12 @@
     tokens = queries.shape[0]
     tiles = tokens // TILE
     z = lax.axis_index("head")
-    pb = lax.axis_index("pb")
-    kv = lax.axis_index("kv")
-    b = kv * pb_size + pb
-
-    def swap(x, offset, places=tuple(range(z_size))):
+    b = lax.axis_index("kv") * pb_size + lax.axis_index("pb")
+    core = b & 1
+
+    def swap(x, offset):
         return lax.ppermute(x, AXES, [
-            (i * z_size + h, (i ^ offset) * z_size + h) for i in range(planes) for h in places
+            (i * z_size + h, (i ^ offset) * z_size + h) for i in range(planes) for h in range(z_size)
         ])
 
     def along(x, pairs):
@@ -160,10 +149,11 @@
 
     relay = kv_size == 2 and pb_size == 4 and z_size == 4
     sides = (2, 4) if relay else (2, 2)
+    halves = range(2)
 
     def head_of(half, offset):
         side = sides[half]
-        mine = (b & 1) + 2 * ((b & side) // side)
+        mine = core + 2 * ((b & side) // side)
         return 4 * half + (mine ^ ((offset & 1) + 2 * ((offset & side) // side)))
 
     def near(half):
@@ -173,7 +163,7 @@
     rider = jnp.concatenate([own_lists % 128, own_lists // 128], axis=0).astype(jnp.bfloat16)
     rider = jnp.pad(rider, ((0, -(2 * tiles) % 16), (0, 2 * HEAD_DIM - SLOTS)))
     own, lists = [], []
-    for half in range(2):
+    for half in halves:
         blocks, riders = [], []
         for offset in near(half):
             at = head_of(half, offset) * HEAD_DIM
@@ -191,29 +181,48 @@
         lists.append(dict(zip(near(half), riders)))
     *own, queries = lax.optimization_barrier((*own, queries))
 
-    kv_bufs, kv_sources = [[], []], [[], []]
+    def columns(array, at, count=1):
+        return lax.dynamic_slice_in_dim(array, at, count * WIDE, axis=1)
+
+    def query_pair(half):
+        return columns(queries, (head_of(half, sides[half]) - core) * WIDE, 2)
+
+    def tie(*arrays):
+        return lax.optimization_barrier(arrays)
+
     if relay:
         across = [6 - side for side in sides]
-
-        def add(half, buf, distance, places=None):
-            take = tuple(range(z_size)) if places is None else places
-            kv_bufs[half] += [buf, swap(buf, across[half], take)]
-            kv_sources[half] += [(distance * 2, places), (distance * 2 + 1, places)]
-
-        two = [along(x, ((0, 2), (1, 3), (2, 0), (3, 1))) for x in own]
-        one = [along(x, ((0, 1), (1, 0), (2, 3), (3, 2))) for x in own]
-        for half in range(2):
-            add(half, own[half], 0)
-            add(half, one[half], 1)
-            add(half, two[half], 2)
-            outer = along(two[half], ((1, 0), (2, 3)))
-            inner = along(own[half], ((1, 2), (2, 1)))
-            add(half, outer, 3, (0, 3))
-            add(half, inner, 3, (1, 2))
+        middle = jnp.logical_or(z == 1, z == 2)
+        by_two, by_one = ((0, 2), (1, 3), (2, 0), (3, 1)), ((0, 1), (1, 0), (2, 3), (3, 2))
+        outward, inward = ((1, 0), (2, 3)), ((1, 2), (2, 1))
+        own_a, own_b = own
+        rows = own_a.shape[0]
+        both = jnp.concatenate(own, axis=0)
+        two, one = along(both, by_two), along(both, by_one)
+        own_a_far, own_b_far = swap(own_a, across[0]), swap(own_b, across[1])
+        crossed_a = swap(query_pair(0), sides[0])
+        turned_b, own_a_far = tie(query_pair(1), own_a_far)
+        crossed_b = swap(turned_b, sides[1])
+        both, one, two, own_a, own_b, own_a_far, own_b_far, crossed_a, crossed_b = tie(
+            both, one, two, own_a, own_b, own_a_far, own_b_far, crossed_a, crossed_b
+        )
+        crossed = [crossed_a, crossed_b]
+        outer, inner = along(two, outward), along(both, inward)
+        pair_a = jnp.concatenate([one[:rows], two[:rows]], axis=0)
+        pair_b = jnp.concatenate([one[rows:], two[rows:]], axis=0)
+        pair_a_far, pair_b_far = swap(pair_a, across[0]), swap(pair_b, across[1])
+        outer, inner, pair_a, pair_b, pair_a_far, pair_b_far = tie(
+            outer, inner, pair_a, pair_b, pair_a_far, pair_b_far
+        )
+        three = jnp.where(middle, inner, outer)
+        three_a, three_b = three[:rows], three[rows:]
+        kv_bufs = [
+            [own_a, own_a_far, pair_a, pair_a_far, three_a, swap(three_a, across[0])],
+            [own_b, own_b_far, pair_b, pair_b_far, three_b, swap(three_b, across[1])],
+        ]
     else:
-        for half in range(2):
-            kv_bufs[half].append(lax.all_gather(own[half], ("kv", "head"), axis=0, tiled=True))
-            kv_sources[half].append((0, None))
+        kv_bufs = [[lax.all_gather(x, ("kv", "head"), axis=0, tiled=True)] for x in own]
+        crossed = [swap(query_pair(half), sides[half]) for half in halves]
 
     def place(half, tile):
         device, within = tile // tiles, tile % tiles
@@ -222,34 +231,36 @@
         side = sides[half]
         slot = (differ & 1) + 2 * ((differ & side) // side)
         if relay:
-            block = ((z_from ^ z) * 2 + (differ & across[half]) // across[half]) * 4 + slot
+            distance, far = z_from ^ z, (differ & across[half]) // across[half]
+            block = jnp.where(
+                distance == 0, far, jnp.where(distance == 3, 6 + far, 1 + distance + 2 * far)
+            )
         else:
-            block = ((where // pb_size) * z_size + z_from) * 4 + slot
-        return block * tiles + within
-
-    q_blocks = []
-    for half in range(2):
-        blocks = {}
-        for offset in near(half):
-            at = head_of(half, offset) * WIDE
-            piece = lax.dynamic_slice_in_dim(queries, at, WIDE, axis=1)
-            blocks[offset] = swap(piece, offset) if offset else piece
-        q_blocks.append(blocks)
+            block = (where // pb_size) * z_size + z_from
+        return (block * 4 + slot) * tiles + within
+
+    other = 1 - core
+    by_core = swap(jnp.concatenate([
+        part for half in halves
+        for part in (columns(queries, head_of(half, 1) * WIDE), columns(crossed[half], other * WIDE))
+    ], axis=1), 1)
 
     result = jnp.zeros((tokens, HEADS * HEAD_DIM), jnp.bfloat16)
     for far in (True, False):
-        for half in range(2):
+        for half in halves:
             side = sides[half]
-            offsets = (side + 1, side) if far else (1, 0)
+            if far:
+                offsets = (side + 1, side)
+                q_blocks = [(by_core, (2 * half + 1) * WIDE), (crossed[half], core * WIDE)]
+            else:
+                offsets = (1, 0)
+                q_blocks = [(by_core, 2 * half * WIDE), (queries, head_of(half, 0) * WIDE)]
             tid = jnp.concatenate([
                 ((b ^ offset) * z_size + z) * tiles + jnp.arange(tiles, dtype=jnp.int32)
                 for offset in offsets
             ])
             loc = place(half, jnp.concatenate([lists[half][offset] for offset in offsets], axis=0))
-            outs = attend(
-                [q_blocks[half][offset] for offset in offsets],
-                kv_bufs[half], kv_sources[half], planes * z_size * tiles, loc, tid, z,
-            )
+            outs = attend(tiles, q_blocks, kv_bufs[half], loc, tid)
             for offset, out in zip(offsets, outs):
                 back = swap(out, offset) if offset else out
                 result = lax.dynamic_update_slice_in_dim(result, back, head_of(half, offset) * WIDE, axis=1)

time: 201 us -> 166 us (0.83); the launches traced: 198 us -> 166 us
  waiting for transfers between devices: 103 us -> 77.7 us
  starting transfers between devices: 44.8 us -> 29.8 us
  local copies, waits for them, and re-layouts: 12.1 us -> 16.6 us
  other arithmetic: 1.36 us -> 5.19 us
    ppermute x28 -> x21, waiting for transfers between devices: 47 us -> 31 us  [swap(): lax.ppermute(x, AXES, [(i * z_size + h, (i ^ offset) * z_size + h) for i...]
    ppermute x28 -> x21, starting transfers between devices: 29.7 us -> 20.7 us  [swap(): lax.ppermute(x, AXES, [(i * z_size + h, (i ^ offset) * z_size + h) for i...]
    ppermute x8 -> x4, waiting for transfers between devices: 55.5 us -> 46.7 us  [along(): lax.ppermute(x, AXES, [(i * z_size + h, i * z_size + k) for i in range(pl...]
    ppermute x8 -> x4, starting transfers between devices: 15.1 us -> 9.08 us  [along(): lax.ppermute(x, AXES, [(i * z_size + h, i * z_size + k) for i in range(pl...]
    slice x0 -> x2, local copies, waits for them, and re-layouts: none -> 2.76 us  [the longest x1 1.65 us: per_device(): pair_b = jnp.concatenate([one[rows:], two[rows:]], axis=0)]
    unnamed x14 -> x25, local copies, waits for them, and re-layouts: 3.76 us -> 4.92 us
    dynamic_slice x1 -> x3, local copies, waits for them, and re-layouts: 4.05 us -> 3.9 us  [columns(): return lax.dynamic_slice_in_dim(array, at, count * WIDE, axis=1)]
  transfers between devices with their start and end apart: 36 -> 25, of which waited for: 14 -> 14; matrix products, arithmetic and copies ran while one was open for 3% -> 8% of each run, Pallas kernels for 19% -> 22%
where the time goes in v3:
time: 166 us
  waiting for transfers between devices  77.7 us (47%)
  Pallas kernels  36 us (22%)
  starting transfers between devices  29.8 us (18%)
  local copies, waits for them, and re-layouts  16.6 us (10%)
  other arithmetic  5.19 us (3%)
    ppermute x4, waiting for transfers between devices, along(): lax.ppermute(x, AXES, [(i * z_size + h, i * z_size + k) for i in range(pl...  46.7 us
    pallas_call x4, Pallas kernels, attend(): pl.pallas_call(functools.partial(attend_kernel, blocks, tiles, starts), o...  36 us
    ppermute x21, waiting for transfers between devices, swap(): lax.ppermute(x, AXES, [(i * z_size + h, (i ^ offset) * z_size + h) for i...  31 us
    ppermute x21, starting transfers between devices, swap(): lax.ppermute(x, AXES, [(i * z_size + h, (i ^ offset) * z_size + h) for i...  20.7 us
    ppermute x4, starting transfers between devices, along(): lax.ppermute(x, AXES, [(i * z_size + h, i * z_size + k) for i in range(pl...  9.08 us
    unnamed x25, local copies, waits for them, and re-layouts  4.92 us
    dynamic_slice x3, local copies, waits for them, and re-layouts, columns(): return lax.dynamic_slice_in_dim(array, at, count * WIDE, axis=1)  3.9 us
  transfers between devices with their start and end apart: 25, of which 14 were waited for; matrix products, arithmetic and copies ran while one was open for 8% of the time, Pallas kernels for 22%

profile of v3, /device:TPU:17, one launch (start us, length us, event | category | flops | bytes accessed | tf_op | source)
XLA Modules:
  0.0 165.8 jit_solution(3891927980071822177)
XLA Ops:
  5.4 1.2 collective-permute-start.4
  7.8 1.2 collective-permute-done.1
  9.1 1.4 collective-permute-done.4
  10.5 2.1 %collective-permute-done = bf16[272,256]{1,0:T(8,128)(2,1)S(1)} collective-permute-done((bf16[272,256]{1,0:T(8,128)(2,1)S(1)}, bf16[272,256]{1,0:T(8,128)(2,1)S(1)}, u32[]{:S(2)}, u32[]{:S(2)}) %collective-permute-start) | collective-permute-done | bytes 139296 | tf_op jit(solution)/shard_map/ppermute | solution.py:141
  13.9 1.3 collective-permute-start.8
  17.2 1.3 collective-permute-start.6
  19.2 1.5 constant_dynamic-slice_fusion.3
  20.7 1.3 collective-permute-start.10
  22.0 5.5 %collective-permute-done.8 = bf16[1024,256]{1,0:T(8,128)(2,1)S(1)} collective-permute-done((bf16[1024,256]{1,0:T(8,128)(2,1)S(1)}, bf16[1024,256]{1,0:T(8,128)(2,1)S(1)}, u32[]{:S(2)}, u32[]{:S(2)}) %collective-permute-start.8) | collective-permute-done | bytes 524320 | tf_op jit(solution)/shard_map/ppermute | solution.py:141
  28.3 1.2 collective-permute-start.11
  29.8 1.3 constant_dynamic-slice_fusion.5
  31.1 30.8 %collective-permute-done.7 = bf16[2048,256]{1,0:T(8,128)(2,1)} collective-permute-done((bf16[2048,256]{1,0:T(8,128)(2,1)}, bf16[2048,256]{1,0:T(8,128)(2,1)}, u32[]{:S(2)}, u32[]{:S(2)}) %collective-permute-start.7) | collective-permute-done | bytes 1048608 | tf_op jit(solution)/shard_map/ppermute | solution.py:146
  61.9 2.1 %collective-permute-done.6 = bf16[2048,256]{1,0:T(8,128)(2,1)} collective-permute-done((bf16[2048,256]{1,0:T(8,128)(2,1)}, bf16[2048,256]{1,0:T(8,128)(2,1)}, u32[]{:S(2)}, u32[]{:S(2)}) %collective-permute-start.6) | collective-permute-done | bytes 1048608 | tf_op jit(solution)/shard_map/ppermute | solution.py:146
  64.0 3.2 %collective-permute-start.14 = (bf16[2048,256]{1,0:T(8,128)(2,1)}, bf16[2048,256]{1,0:T(8,128)(2,1)}, u32[]{:S(2)}, u32[]{:S(2)}) collective-permute-start(bf16[2048,256]{1,0:T(8,128)(2,1)} %constant_dynamic-update-slice_fusion.8), channel_id=1, source_target_pairs={{1,2},{2,1},{5,6},{6,5},{9,10},{10,9},{13,14},{14,13},{17,18},{18,... | collective-permute-start | bytes 3145736 | tf_op jit(solution)/shard_map/ppermute | solution.py:146
  67.2 4.6 %collective-permute-start.13 = (bf16[2048,256]{1,0:T(8,128)(2,1)}, bf16[2048,256]{1,0:T(8,128)(2,1)}, u32[]{:S(2)}, u32[]{:S(2)}) collective-permute-start(bf16[2048,256]{1,0:T(8,128)(2,1)} %collective-permute-done.7), channel_id=1, source_target_pairs={{1,0},{2,3},{5,4},{6,7},{9,8},{10,11},{13,12},{14,15},{17,16},{18,... | collective-permute-start | bytes 3145736 | tf_op jit(solution)/shard_map/ppermute | solution.py:146
  71.7 1.7 fusion.27
  76.3 1.5 pad_maximum_fusion
  77.8 1.3 collective-permute-start.12
  79.2 10.2 %collective-permute-done.14 = bf16[2048,256]{1,0:T(8,128)(2,1)} collective-permute-done((bf16[2048,256]{1,0:T(8,128)(2,1)}, bf16[2048,256]{1,0:T(8,128)(2,1)}, u32[]{:S(2)}, u32[]{:S(2)}) %collective-permute-start.14) | collective-permute-done | bytes 1048608 | tf_op jit(solution)/shard_map/ppermute | solution.py:146
  89.4 3.7 %collective-permute-done.13 = bf16[2048,256]{1,0:T(8,128)(2,1)} collective-permute-done((bf16[2048,256]{1,0:T(8,128)(2,1)}, bf16[2048,256]{1,0:T(8,128)(2,1)}, u32[]{:S(2)}, u32[]{:S(2)}) %collective-permute-start.13) | collective-permute-done | bytes 1048608 | tf_op jit(solution)/shard_map/ppermute | solution.py:146
  93.1 4.5 %collective-permute-done.15 = bf16[2048,256]{1,0:T(8,128)(2,1)} collective-permute-done((bf16[2048,256]{1,0:T(8,128)(2,1)S(1)}, bf16[2048,256]{1,0:T(8,128)(2,1)}, u32[]{:S(2)}, u32[]{:S(2)}) %collective-permute-start.15) | collective-permute-done | bytes 1048608 | tf_op jit(solution)/shard_map/ppermute | solution.py:141
  97.7 1.3 broadcast_select_fusion
  101.4 1.3 collective-permute-start.17
  102.7 9.2 %collective-permute-done.20 = bf16[1024,256]{1,0:T(8,128)(2,1)} collective-permute-done((bf16[1024,256]{1,0:T(8,128)(2,1)}, bf16[1024,256]{1,0:T(8,128)(2,1)}, u32[]{:S(2)}, u32[]{:S(2)}) %collective-permute-start.20) | collective-permute-done | bytes 524320 | tf_op jit(solution)/shard_map/ppermute | solution.py:141
  113.2 9.1 %shard_map.47 = (bf16[2,128,1024]{2,1,0:T(8,128)(2,1)S(1)}, bf16[2,128,1024]{2,1,0:T(8,128)(2,1)S(1)}) custom-call(s32[32]{0:T(128)S(1)} %fusion.10.loc_ref, s32[4]{0:T(128)S(1)} %pad_add_fusion.6.tid_ref, s32[2]{0:T(128)S(1)} %get-tuple-element.102.col_ref, bf16[2,128,4096]{2,1,0:T(8,128)(2,1)} %bitcast.1.refs_0_, bf16[2,128,2048]{2,1,0:T(8,128)(2,1)S(1)} %bitcast.42, ...), custom_call_target="tpu_custom_call" | custom-call | flops 4294967296 | bytes 6291456 | tf_op jit(solution)/shard_map/pallas_call | solution.py:108
  122.3 1.2 collective-permute-start.22
  123.5 3.4 %collective-permute-start.21 = (bf16[256,1024]{1,0:T(8,128)(2,1)S(1)}, bf16[256,1024]{1,0:T(8,128)(2,1)S(1)}, u32[]{:S(2)}, u32[]{:S(2)}) collective-permute-start(bf16[256,1024]{1,0:T(8,128)(2,1)S(1)} %bitcast.46), channel_id=1, source_target_pairs={{0,20},{1,21},{2,22},{3,23},{4,16},{5,17},{6,18},{7,19},{8,28},{9,... | collective-permute-start | bytes 1572872 | tf_op jit(solution)/shard_map/ppermute | solution.py:141
  126.9 9.1 %shard_map.46 = (bf16[2,128,1024]{2,1,0:T(8,128)(2,1)S(1)}, bf16[2,128,1024]{2,1,0:T(8,128)(2,1)S(1)}) custom-call(s32[32]{0:T(128)S(1)} %fusion.9.loc_ref, s32[4]{0:T(128)S(1)} %pad_add_fusion.4.tid_ref, s32[2]{0:T(128)S(1)} %get-tuple-element.100.col_ref, bf16[2,128,4096]{2,1,0:T(8,128)(2,1)} %bitcast.1.refs_0_, bf16[2,128,2048]{2,1,0:T(8,128)(2,1)S(1)} %bitcast.41, ...), custom_call_target="tpu_custom_call" | custom-call | flops 4294967296 | bytes 6291456 | tf_op jit(solution)/shard_map/pallas_call | solution.py:108
  137.6 8.7 %shard_map.48 = (bf16[2,128,1024]{2,1,0:T(8,128)(2,1)S(1)}, bf16[2,128,1024]{2,1,0:T(8,128)(2,1)S(1)}) custom-call(s32[32]{0:T(128)S(1)} %fusion.11.loc_ref, s32[4]{0:T(128)S(1)} %pad_add_fusion.8.tid_ref, s32[2]{0:T(128)S(1)} %get-tuple-element.101.col_ref, bf16[2,128,4096]{2,1,0:T(8,128)(2,1)} %bitcast.1.refs_0_, bf16[2,128,8192]{2,1,0:T(8,128)(2,1)S(1)} %bitcast.27, ...), custom_call_target="tpu_custom_call" | custom-call | flops 4294967296 | bytes 6291456 | tf_op jit(solution)/shard_map/pallas_call | solution.py:108
  146.8 9.1 %shard_map.49 = (bf16[2,128,1024]{2,1,0:T(8,128)(2,1)S(1)}, bf16[2,128,1024]{2,1,0:T(8,128)(2,1)S(1)}) custom-call(s32[32]{0:T(128)S(1)} %fusion.12.loc_ref, s32[4]{0:T(128)S(1)} %pad_add_fusion.8.tid_ref, s32[2]{0:T(128)S(1)} %get-tuple-element.103.col_ref, bf16[2,128,4096]{2,1,0:T(8,128)(2,1)} %bitcast.1.refs_0_, bf16[2,128,8192]{2,1,0:T(8,128)(2,1)S(1)} %bitcast.28, ...), custom_call_target="tpu_custom_call" | custom-call | flops 4294967296 | bytes 6291456 | tf_op jit(solution)/shard_map/pallas_call | solution.py:108
  155.9 5.1 %collective-permute-done.18 = bf16[256,1024]{1,0:T(8,128)(2,1)S(1)} collective-permute-done((bf16[256,1024]{1,0:T(8,128)(2,1)S(1)}, bf16[256,1024]{1,0:T(8,128)(2,1)S(1)}, u32[]{:S(2)}, u32[]{:S(2)}) %collective-permute-start.18) | collective-permute-done | bytes 524320 | tf_op jit(solution)/shard_map/ppermute | solution.py:141
  163.0 2.0 %copy-done.10 = bf16[256,8192]{1,0:T(8,128)(2,1)} copy-done((bf16[256,8192]{1,0:T(8,128)(2,1)}, bf16[256,8192]{1,0:T(8,128)(2,1)S(1)}, u32[]{:S(2)}) %copy-start.10) | copy-done | bytes 4194328
  (110 shorter events, 23.0 us)
Async XLA Ops:
  3.1 4.5 %collective-permute-start.3 = (bf16[272,256]{1,0:T(8,128)(2,1)S(1)}, bf16[272,256]{1,0:T(8,128)(2,1)S(1)}, u32[]{:S(2)}, u32[]{:S(2)}) collective-permute-start(bf16[272,256]{1,0:T(8,128)(2,1)S(1)} %get-tuple-element.93), channel_id=1, source_target_pairs={{0,4},{1,5},{2,6},{3,7},{4,0},{5,1},{6,2},{7,3},{8,12},{9,13},{10,... | collective-permute-start | bytes 417800 | tf_op jit(solution)/shard_map/ppermute | solution.py:141
  3.8 5.3 %collective-permute-start.1 = (bf16[272,256]{1,0:T(8,128)(2,1)S(1)}, bf16[272,256]{1,0:T(8,128)(2,1)S(1)}, u32[]{:S(2)}, u32[]{:S(2)}) collective-permute-start(bf16[272,256]{1,0:T(8,128)(2,1)S(1)} %get-tuple-element.94), channel_id=1, source_target_pairs={{0,8},{1,9},{2,10},{3,11},{4,12},{5,13},{6,14},{7,15},{8,0},{9,1},... | collective-permute-start | bytes 417800 | tf_op jit(solution)/shard_map/ppermute | solution.py:141
  5.1 4.0 %collective-permute-start.2 = (bf16[272,256]{1,0:T(8,128)(2,1)S(1)}, bf16[272,256]{1,0:T(8,128)(2,1)S(1)}, u32[]{:S(2)}, u32[]{:S(2)}) collective-permute-start(bf16[272,256]{1,0:T(8,128)(2,1)S(1)} %get-tuple-element.95), channel_id=1, source_target_pairs={{0,4},{1,5},{2,6},{3,7},{4,0},{5,1},{6,2},{7,3},{8,12},{9,13},{10,... | collective-permute-start | bytes 417800 | tf_op jit(solution)/shard_map/ppermute | solution.py:141
  5.4 5.1 %collective-permute-start.4 = (bf16[272,256]{1,0:T(8,128)(2,1)S(1)}, bf16[272,256]{1,0:T(8,128)(2,1)S(1)}, u32[]{:S(2)}, u32[]{:S(2)}) collective-permute-start(bf16[272,256]{1,0:T(8,128)(2,1)S(1)} %get-tuple-element.96), channel_id=1, source_target_pairs={{0,16},{1,17},{2,18},{3,19},{4,20},{5,21},{6,22},{7,23},{8,24},{9,... | collective-permute-start | bytes 417800 | tf_op jit(solution)/shard_map/ppermute | solution.py:141
  6.6 6.0 %collective-permute-start = (bf16[272,256]{1,0:T(8,128)(2,1)S(1)}, bf16[272,256]{1,0:T(8,128)(2,1)S(1)}, u32[]{:S(2)}, u32[]{:S(2)}) collective-permute-start(bf16[272,256]{1,0:T(8,128)(2,1)S(1)} %get-tuple-element.97), channel_id=1, source_target_pairs={{0,12},{1,13},{2,14},{3,15},{4,8},{5,9},{6,10},{7,11},{8,4},{9,5},... | collective-permute-start | bytes 417800 | tf_op jit(solution)/shard_map/ppermute | solution.py:141
  7.6 6.2 %collective-permute-start.5 = (bf16[272,256]{1,0:T(8,128)(2,1)S(1)}, bf16[272,256]{1,0:T(8,128)(2,1)S(1)}, u32[]{:S(2)}, u32[]{:S(2)}) collective-permute-start(bf16[272,256]{1,0:T(8,128)(2,1)S(1)} %get-tuple-element.98), channel_id=1, source_target_pairs={{0,20},{1,21},{2,22},{3,23},{4,16},{5,17},{6,18},{7,19},{8,28},{9,... | collective-permute-start | bytes 417800 | tf_op jit(solution)/shard_map/ppermute | solution.py:141
  7.8 11.4 %copy-start = (bf16[256,8192]{1,0:T(8,128)(2,1)S(1)}, bf16[256,8192]{1,0:T(8,128)(2,1)}, u32[]{:S(2)}) copy-start(bf16[256,8192]{1,0:T(8,128)(2,1)} %param.4) | copy-start | bytes 12582916
  13.9 13.7 %collective-permute-start.8 = (bf16[1024,256]{1,0:T(8,128)(2,1)S(1)}, bf16[1024,256]{1,0:T(8,128)(2,1)S(1)}, u32[]{:S(2)}, u32[]{:S(2)}) collective-permute-start(bf16[1024,256]{1,0:T(8,128)(2,1)S(1)} %pad_maximum_fusion.3), channel_id=1, source_target_pairs={{0,16},{1,17},{2,18},{3,19},{4,20},{5,21},{6,22},{7,23},{8,24},{9,... | collective-permute-start | bytes 1572872 | tf_op jit(solution)/shard_map/ppermute | solution.py:141
  16.1 15.0 %collective-permute-start.9 = (bf16[1024,256]{1,0:T(8,128)(2,1)S(1)}, bf16[1024,256]{1,0:T(8,128)(2,1)}, u32[]{:S(2)}, u32[]{:S(2)}) collective-permute-start(bf16[1024,256]{1,0:T(8,128)(2,1)S(1)} %pad_maximum_fusion.4), channel_id=1, source_target_pairs={{0,8},{1,9},{2,10},{3,11},{4,12},{5,13},{6,14},{7,15},{8,0},{9,1},... | collective-permute-start | bytes 1572872 | tf_op jit(solution)/shard_map/ppermute | solution.py:141
  17.1 44.8 %collective-permute-start.7 = (bf16[2048,256]{1,0:T(8,128)(2,1)}, bf16[2048,256]{1,0:T(8,128)(2,1)}, u32[]{:S(2)}, u32[]{:S(2)}) collective-permute-start(bf16[2048,256]{1,0:T(8,128)(2,1)} %constant_dynamic-update-slice_fusion.8), channel_id=1, source_target_pairs={{0,2},{1,3},{2,0},{3,1},{4,6},{5,7},{6,4},{7,5},{8,10},{9,11},{10,... | collective-permute-start | bytes 3145736 | tf_op jit(solution)/shard_map/ppermute | solution.py:146
  17.2 46.8 %collective-permute-start.6 = (bf16[2048,256]{1,0:T(8,128)(2,1)}, bf16[2048,256]{1,0:T(8,128)(2,1)}, u32[]{:S(2)}, u32[]{:S(2)}) collective-permute-start(bf16[2048,256]{1,0:T(8,128)(2,1)} %constant_dynamic-update-slice_fusion.8), channel_id=1, source_target_pairs={{0,1},{1,0},{2,3},{3,2},{4,5},{5,4},{6,7},{7,6},{8,9},{9,8},{10,11... | collective-permute-start | bytes 3145736 | tf_op jit(solution)/shard_map/ppermute | solution.py:146
  20.7 43.3 %collective-permute-start.10 = (bf16[256,2048]{1,0:T(8,128)(2,1)}, bf16[256,2048]{1,0:T(8,128)(2,1)S(1)}, u32[]{:S(2)}, u32[]{:S(2)}) collective-permute-start(bf16[256,2048]{1,0:T(8,128)(2,1)} %get-tuple-element.63), channel_id=1, source_target_pairs={{0,8},{1,9},{2,10},{3,11},{4,12},{5,13},{6,14},{7,15},{8,0},{9,1},... | collective-permute-start | bytes 3145736 | tf_op jit(solution)/shard_map/ppermute | solution.py:141
  28.3 35.7 %collective-permute-start.11 = (bf16[256,2048]{1,0:T(8,128)(2,1)}, bf16[256,2048]{1,0:T(8,128)(2,1)S(1)}, u32[]{:S(2)}, u32[]{:S(2)}) collective-permute-start(bf16[256,2048]{1,0:T(8,128)(2,1)} %get-tuple-element.37), channel_id=1, source_target_pairs={{0,16},{1,17},{2,18},{3,19},{4,20},{5,21},{6,22},{7,23},{8,24},{9,... | collective-permute-start | bytes 3145736 | tf_op jit(solution)/shard_map/ppermute | solution.py:141
  64.0 9.9 %copy-start.3 = (bf16[256,2048]{1,0:T(8,128)(2,1)}, bf16[256,2048]{1,0:T(8,128)(2,1)S(1)}, u32[]{:S(2)}) copy-start(bf16[256,2048]{1,0:T(8,128)(2,1)S(1)} %collective-permute-done.10) | copy-start | bytes 3145732
  64.0 9.4 %copy-start.5 = (bf16[256,2048]{1,0:T(8,128)(2,1)}, bf16[256,2048]{1,0:T(8,128)(2,1)S(1)}, u32[]{:S(2)}) copy-start(bf16[256,2048]{1,0:T(8,128)(2,1)S(1)} %collective-permute-done.11) | copy-start | bytes 3145732
  64.0 25.4 %collective-permute-start.14 = (bf16[2048,256]{1,0:T(8,128)(2,1)}, bf16[2048,256]{1,0:T(8,128)(2,1)}, u32[]{:S(2)}, u32[]{:S(2)}) collective-permute-start(bf16[2048,256]{1,0:T(8,128)(2,1)} %constant_dynamic-update-slice_fusion.8), channel_id=1, source_target_pairs={{1,2},{2,1},{5,6},{6,5},{9,10},{10,9},{13,14},{14,13},{17,18},{18,... | collective-permute-start | bytes 3145736 | tf_op jit(solution)/shard_map/ppermute | solution.py:146
  67.2 25.9 %collective-permute-start.13 = (bf16[2048,256]{1,0:T(8,128)(2,1)}, bf16[2048,256]{1,0:T(8,128)(2,1)}, u32[]{:S(2)}, u32[]{:S(2)}) collective-permute-start(bf16[2048,256]{1,0:T(8,128)(2,1)} %collective-permute-done.7), channel_id=1, source_target_pairs={{1,0},{2,3},{5,4},{6,7},{9,8},{10,11},{13,12},{14,15},{17,16},{18,... | collective-permute-start | bytes 3145736 | tf_op jit(solution)/shard_map/ppermute | solution.py:146
  73.5 24.1 %collective-permute-start.15 = (bf16[2048,256]{1,0:T(8,128)(2,1)S(1)}, bf16[2048,256]{1,0:T(8,128)(2,1)}, u32[]{:S(2)}, u32[]{:S(2)}) collective-permute-start(bf16[2048,256]{1,0:T(8,128)(2,1)S(1)} %pad_maximum_fusion.1), channel_id=1, source_target_pairs={{0,16},{1,17},{2,18},{3,19},{4,20},{5,21},{6,22},{7,23},{8,24},{9,... | collective-permute-start | bytes 3145736 | tf_op jit(solution)/shard_map/ppermute | solution.py:141
  74.0 23.8 %collective-permute-start.16 = (bf16[2048,256]{1,0:T(8,128)(2,1)S(1)}, bf16[2048,256]{1,0:T(8,128)(2,1)}, u32[]{:S(2)}, u32[]{:S(2)}) collective-permute-start(bf16[2048,256]{1,0:T(8,128)(2,1)S(1)} %pad_maximum_fusion.2), channel_id=1, source_target_pairs={{0,8},{1,9},{2,10},{3,11},{4,12},{5,13},{6,14},{7,15},{8,0},{9,1},... | collective-permute-start | bytes 3145736 | tf_op jit(solution)/shard_map/ppermute | solution.py:141
  77.8 34.2 %collective-permute-start.12 = (bf16[256,4096]{1,0:T(8,128)(2,1)}, bf16[256,4096]{1,0:T(8,128)(2,1)}, u32[]{:S(2)}, u32[]{:S(2)}) collective-permute-start(bf16[256,4096]{1,0:T(8,128)(2,1)} %pad_maximum_fusion), channel_id=1, source_target_pairs={{0,4},{1,5},{2,6},{3,7},{4,0},{5,1},{6,2},{7,3},{8,12},{9,13},{10,... | collective-permute-start | bytes 6291464 | tf_op jit(solution)/shard_map/ppermute | solution.py:141
  100.2 11.8 %collective-permute-start.20 = (bf16[1024,256]{1,0:T(8,128)(2,1)}, bf16[1024,256]{1,0:T(8,128)(2,1)}, u32[]{:S(2)}, u32[]{:S(2)}) collective-permute-start(bf16[1024,256]{1,0:T(8,128)(2,1)} %get-tuple-element.65), channel_id=1, source_target_pairs={{0,8},{1,9},{2,10},{3,11},{4,12},{5,13},{6,14},{7,15},{8,0},{9,1},... | collective-permute-start | bytes 1572872 | tf_op jit(solution)/shard_map/ppermute | solution.py:141
  101.4 25.5 %collective-permute-start.17 = (bf16[1024,256]{1,0:T(8,128)(2,1)}, bf16[1024,256]{1,0:T(8,128)(2,1)S(1)}, u32[]{:S(2)}, u32[]{:S(2)}) collective-permute-start(bf16[1024,256]{1,0:T(8,128)(2,1)} %get-tuple-element.66), channel_id=1, source_target_pairs={{0,16},{1,17},{2,18},{3,19},{4,20},{5,21},{6,22},{7,23},{8,24},{9,... | collective-permute-start | bytes 1572872 | tf_op jit(solution)/shard_map/ppermute | solution.py:141
  113.2 13.7 %copy-start.2 = (bf16[1024,256]{1,0:T(8,128)(2,1)S(1)}, bf16[1024,256]{1,0:T(8,128)(2,1)}, u32[]{:S(2)}) copy-start(bf16[1024,256]{1,0:T(8,128)(2,1)} %get-tuple-element.66) | copy-start | bytes 1572868
  113.2 13.7 %copy-start.4 = (bf16[256,2048]{1,0:T(8,128)(2,1)S(1)}, bf16[256,2048]{1,0:T(8,128)(2,1)}, u32[]{:S(2)}) copy-start(bf16[256,2048]{1,0:T(8,128)(2,1)} %copy-done.3) | copy-start | bytes 3145732
  113.2 13.7 %copy-start.9 = (bf16[1024,256]{1,0:T(8,128)(2,1)S(1)}, bf16[1024,256]{1,0:T(8,128)(2,1)}, u32[]{:S(2)}) copy-start(bf16[1024,256]{1,0:T(8,128)(2,1)} %copy-done.8) | copy-start | bytes 1572868
  122.3 39.7 %collective-permute-start.22 = (bf16[256,1024]{1,0:T(8,128)(2,1)S(1)}, bf16[256,1024]{1,0:T(8,128)(2,1)S(1)}, u32[]{:S(2)}, u32[]{:S(2)}) collective-permute-start(bf16[256,1024]{1,0:T(8,128)(2,1)S(1)} %bitcast.45), channel_id=1, source_target_pairs={{0,16},{1,17},{2,18},{3,19},{4,20},{5,21},{6,22},{7,23},{8,24},{9,... | collective-permute-start | bytes 1572872 | tf_op jit(solution)/shard_map/ppermute | solution.py:141
  123.5 38.4 %collective-permute-start.21 = (bf16[256,1024]{1,0:T(8,128)(2,1)S(1)}, bf16[256,1024]{1,0:T(8,128)(2,1)S(1)}, u32[]{:S(2)}, u32[]{:S(2)}) collective-permute-start(bf16[256,1024]{1,0:T(8,128)(2,1)S(1)} %bitcast.46), channel_id=1, source_target_pairs={{0,20},{1,21},{2,22},{3,23},{4,16},{5,17},{6,18},{7,19},{8,28},{9,... | collective-permute-start | bytes 1572872 | tf_op jit(solution)/shard_map/ppermute | solution.py:141
  126.9 10.6 %copy-start.1 = (bf16[256,8192]{1,0:T(8,128)(2,1)S(1)}, bf16[256,8192]{1,0:T(8,128)(2,1)}, u32[]{:S(2)}) copy-start(bf16[256,8192]{1,0:T(8,128)(2,1)} %param.4) | copy-start | bytes 12582916
  136.0 25.9 %collective-permute-start.19 = (bf16[256,1024]{1,0:T(8,128)(2,1)S(1)}, bf16[256,1024]{1,0:T(8,128)(2,1)S(1)}, u32[]{:S(2)}, u32[]{:S(2)}) collective-permute-start(bf16[256,1024]{1,0:T(8,128)(2,1)S(1)} %bitcast.51), channel_id=1, source_target_pairs={{0,8},{1,9},{2,10},{3,11},{4,12},{5,13},{6,14},{7,15},{8,0},{9,1},... | collective-permute-start | bytes 1572872 | tf_op jit(solution)/shard_map/ppermute | solution.py:141
  137.2 23.7 %collective-permute-start.18 = (bf16[256,1024]{1,0:T(8,128)(2,1)S(1)}, bf16[256,1024]{1,0:T(8,128)(2,1)S(1)}, u32[]{:S(2)}, u32[]{:S(2)}) collective-permute-start(bf16[256,1024]{1,0:T(8,128)(2,1)S(1)} %bitcast.52), channel_id=1, source_target_pairs={{0,12},{1,13},{2,14},{3,15},{4,8},{5,9},{6,10},{7,11},{8,4},{9,5},... | collective-permute-start | bytes 1572872 | tf_op jit(solution)/shard_map/ppermute | solution.py:141
  146.3 15.8 %collective-permute-start.23 = (bf16[256,1024]{1,0:T(8,128)(2,1)S(1)}, bf16[256,1024]{1,0:T(8,128)(2,1)S(1)}, u32[]{:S(2)}, u32[]{:S(2)}) collective-permute-start(bf16[256,1024]{1,0:T(8,128)(2,1)S(1)} %bitcast.47), channel_id=1, source_target_pairs={{0,4},{1,5},{2,6},{3,7},{4,0},{5,1},{6,2},{7,3},{8,12},{9,13},{10,... | collective-permute-start | bytes 1572872 | tf_op jit(solution)/shard_map/ppermute | solution.py:141
  161.0 1.9 %collective-permute-start.24 = (bf16[256,1024]{1,0:T(8,128)(2,1)S(1)}, bf16[256,1024]{1,0:T(8,128)(2,1)S(1)}, u32[]{:S(2)}, u32[]{:S(2)}) collective-permute-start(bf16[256,1024]{1,0:T(8,128)(2,1)S(1)} %bitcast.48), channel_id=1, source_target_pairs={{0,4},{1,5},{2,6},{3,7},{4,0},{5,1},{6,2},{7,3},{8,12},{9,13},{10,... | collective-permute-start | bytes 1572872 | tf_op jit(solution)/shard_map/ppermute | solution.py:141
  (5 other events, 12.0 us)

commit v4 on v3

v4 whole, which is shorter than its diff:
```python
import functools

import jax
import jax.numpy as jnp
from jax import lax
from jax.experimental import pallas as pl
from jax.experimental.pallas import tpu as pltpu
from jax.sharding import PartitionSpec as P

HEADS = 64
KV_HEADS = 8
HEAD_DIM = 128
TILE = 128
SLOTS = 8

NEG = -1e30
GROUPS = HEADS // KV_HEADS
WIDE = GROUPS * HEAD_DIM
VMEM_LIMIT = 60 * 2**20
AXES = ("kv", "pb", "head")
LOG2 = HEAD_DIM ** (-0.5) * 1.4426950408889634


def rows_of(tile, count=1):
    return pl.ds(pl.multiple_of(tile * TILE, TILE), count * TILE)


def attend_tiles(count, masked, first, tid_ref, q_buf, kv_buf, out_buf):
    keys, values = [], []
    for t in range(count):
        listed = rows_of((first + t) * SLOTS, SLOTS)
        keys.append(kv_buf[listed, :HEAD_DIM])
        value = kv_buf[listed, HEAD_DIM:]
        values.append(jnp.concatenate([value, jnp.ones_like(value)], axis=1))
    row = lax.broadcasted_iota(jnp.int32, (TILE, TILE), 0)
    column = lax.broadcasted_iota(jnp.int32, (TILE, TILE), 1)
    diagonal = jnp.where(column <= row, 0.0, NEG)

    def score(t, g):
        scores = lax.dot_general(
            q_buf[rows_of(first + t), g * HEAD_DIM:(g + 1) * HEAD_DIM], keys[t], (((1,), (1,)), ((), ())),
            preferred_element_type=jnp.float32,
        )
        parts = [scores[:, :TILE] + diagonal]
        if masked:
            live = tid_ref[first + t] + 1
            for j in range(1, SLOTS):
                part = scores[:, j * TILE:(j + 1) * TILE]
                parts.append(part + jnp.where(j < live, 0.0, NEG))
        else:
            parts.append(scores[:, TILE:])
        return jnp.concatenate(parts, axis=1)

    def weigh(scores):
        top = jnp.max(scores, axis=1, keepdims=True)
        return jnp.exp2((scores - top) * LOG2).astype(jnp.bfloat16)

    def finish(weights, t, g):
        total = jnp.dot(weights, values[t], preferred_element_type=jnp.float32)
        out = total[:, :HEAD_DIM] / total[:, HEAD_DIM:]
        out_buf[rows_of(first + t), g * HEAD_DIM:(g + 1) * HEAD_DIM] = out.astype(jnp.bfloat16)

    units = [(t, g) for t in range(count) for g in range(GROUPS)]
    ahead = 0 if masked else 3
    scores, weights = {}, {}
    for step in range(len(units) + ahead + 1):
        if step < len(units):
            scores[step] = score(*units[step])
        if 0 <= step - ahead < len(units):
            weights[step - ahead] = weigh(scores.pop(step - ahead))
        if step - ahead >= 1:
            finish(weights.pop(step - ahead - 1), *units[step - ahead - 1])


def attend_kernel(blocks, tiles, starts, direct, shared, pieces, turn_ref, loc_ref, tid_ref, col_ref, *refs):
    q_refs, refs = refs[:blocks], refs[blocks:]
    kv_refs, refs = refs[:len(starts)], refs[len(starts):]
    piece_refs, refs = refs[:pieces], refs[pieces:]
    out_refs, (next_ref, q_buf, kv_buf, out_buf, piece_buf, *sems) = refs[:-9], refs[-9:]
    q_sem, kv_sem, out_sem, piece_sem = sems
    next_ref[0] = turn_ref[0] + 1

    def wide(i):
        return pl.ds(pl.multiple_of(col_ref[i], WIDE), WIDE)

    q_copies = [
        pltpu.make_async_copy(
            q_refs[i].at[:, wide(i)], q_buf.at[rows_of(i * tiles, tiles)], q_sem.at[i]
        )
        for i in range(blocks)
    ]

    def fetch(slot, sem):
        at = loc_ref[slot]
        for ref, start in zip(kv_refs, starts):
            here = at - start

            @pl.when(jnp.logical_and(here >= 0, here < ref.shape[0] // TILE))
            def _(ref=ref, here=here):
                pltpu.make_async_copy(ref.at[rows_of(here)], kv_buf.at[rows_of(slot)], sem).start()

    def fetch_block(i):
        slots = tiles * SLOTS
        for k, copy in enumerate(q_copies):
            pl.when(i == k)(copy.start)

        def one_slot(slot, _):
            fetch(slot, kv_sem.at[i])
            return 0

        lax.fori_loop(i * slots, (i + 1) * slots, one_slot, 0)

    fetch_block(0)
    piece_ins, piece_outs = [], []
    for i in range(pieces):
        buf = piece_buf.at[rows_of(i * tiles, tiles)]
        piece_ins.append(pltpu.make_async_copy(piece_refs[i], buf, piece_sem.at[i]))
        piece_outs.append(
            pltpu.make_async_copy(buf, out_refs[0].at[:, wide(2 * blocks + i)], out_sem.at[blocks + i])
        )
        piece_ins[-1].start()

    out_copies = []
    for i in range(blocks):
        alone = blocks - shared
        if direct:
            target = out_refs[0].at[:, wide(blocks + i)]
        elif i < alone:
            target = out_refs[i]
        else:
            target = out_refs[alone].at[rows_of((i - alone) * tiles, tiles)]
        out_copies.append(
            pltpu.make_async_copy(out_buf.at[rows_of(i * tiles, tiles)], target, out_sem.at[i])
        )

    def one_block(i, _):
        first = i * tiles
        pl.when(i + 1 < blocks)(lambda: fetch_block(i + 1))
        rows = q_buf.at[rows_of(first, tiles)]
        pltpu.make_async_copy(rows, rows, q_sem.at[i]).wait()
        listed = kv_buf.at[rows_of(first * SLOTS, tiles * SLOTS)]
        pltpu.make_async_copy(listed, listed, kv_sem.at[i]).wait()
        early = tid_ref[first] + 1 < SLOTS

        @pl.when(early)
        def _():
            def one_tile(tile, _):
                attend_tiles(1, True, tile, tid_ref, q_buf, kv_buf, out_buf)
                return 0

            lax.fori_loop(first, first + tiles, one_tile, 0)

        @pl.when(jnp.logical_not(early))
        def _():
            count = 2 if tiles % 2 == 0 else 1

            def some_tiles(step, _):
                attend_tiles(count, False, first + step * count, tid_ref, q_buf, kv_buf, out_buf)
                return 0

            lax.fori_loop(0, tiles // count, some_tiles, 0)

        for k, copy in enumerate(out_copies):
            pl.when(i == k)(copy.start)
        return 0

    lax.fori_loop(0, blocks, one_block, 0)
    for copy_in, copy in zip(piece_ins, piece_outs):
        copy_in.wait()
        copy.start()
    for copy in piece_outs + out_copies:
        copy.wait()


def attend(turn, tiles, q_blocks, kv_bufs, loc, tid, out_at=None, shared=0, pieces=()):
    blocks, direct = len(q_blocks), out_at is not None
    queries = [q for q, _ in q_blocks]
    columns = [at for _, at in q_blocks] + list(out_at if direct else [])
    columns += [at for _, at in pieces]
    columns = jnp.stack([jnp.asarray(at, jnp.int32) for at in columns])
    starts, kv_tiles = [], 0
    for kv in kv_bufs:
        starts.append(kv_tiles)
        kv_tiles += kv.shape[0] // TILE
    smem = pl.BlockSpec(memory_space=pltpu.SMEM)
    hbm = pl.BlockSpec(memory_space=pl.ANY)
    units = blocks * tiles
    rows = tiles * TILE
    if direct:
        shapes = [(rows, HEADS * HEAD_DIM)]
    else:
        shapes = [(rows, WIDE)] * (blocks - shared) + [(shared * rows, WIDE)] * (shared > 0)
    out = pl.pallas_call(
        functools.partial(attend_kernel, blocks, tiles, starts, direct, shared, len(pieces)),
        out_shape=[jax.ShapeDtypeStruct(shape, jnp.bfloat16) for shape in shapes] + [jax.ShapeDtypeStruct((1,), jnp.int32)],
        in_specs=[smem] * 4 + [hbm] * (blocks + len(kv_bufs) + len(pieces)),
        out_specs=[hbm] * len(shapes) + [smem],
        scratch_shapes=[
            pltpu.VMEM((blocks * rows, WIDE), jnp.bfloat16),
            pltpu.VMEM((units * SLOTS * TILE, 2 * HEAD_DIM), jnp.bfloat16),
            pltpu.VMEM((blocks * rows, WIDE), jnp.bfloat16),
            pltpu.VMEM((max(len(pieces), 1) * rows, WIDE), jnp.bfloat16),
            pltpu.SemaphoreType.DMA((blocks,)),
            pltpu.SemaphoreType.DMA((blocks,)),
            pltpu.SemaphoreType.DMA((blocks + len(pieces),)),
            pltpu.SemaphoreType.DMA((max(len(pieces), 1),)),
        ],
        compiler_params=pltpu.CompilerParams(vmem_limit_bytes=VMEM_LIMIT),
        cost_estimate=pl.CostEstimate(flops=units * 10**10, bytes_accessed=10**6, transcendentals=0),
    )(turn, loc.reshape(-1), tid, columns, *queries, *kv_bufs, *[piece for piece, _ in pieces])
    return out


def deliver_kernel(sources, rows, col_ref, *refs):
    count, arrays = len(sources), len(refs) - 5
    out_ref, piece_buf, in_sem, out_sem = refs[arrays + 1:]
    ins = [
        pltpu.make_async_copy(refs[array].at[pl.ds(at * rows, rows)], piece_buf.at[i], in_sem.at[i])
        for i, (array, at) in enumerate(sources)
    ]
    outs = [
        pltpu.make_async_copy(
            piece_buf.at[i], out_ref.at[:, pl.ds(pl.multiple_of(col_ref[i], WIDE), WIDE)], out_sem.at[i]
        )
        for i in range(count)
    ]
    for copy in ins:
        copy.start()
    for copy_in, copy in zip(ins, outs):
        copy_in.wait()
        copy.start()
    for copy in outs:
        copy.wait()


def deliver(result, arrays, columns):
    rows = result.shape[0]
    sources = [(i, at) for i, array in enumerate(arrays) for at in range(array.shape[0] // rows)]
    count = len(sources)
    hbm = pl.BlockSpec(memory_space=pl.ANY)
    return pl.pallas_call(
        functools.partial(deliver_kernel, sources, rows),
        out_shape=jax.ShapeDtypeStruct(result.shape, result.dtype),
        in_specs=[pl.BlockSpec(memory_space=pltpu.SMEM)] + [hbm] * (len(arrays) + 1),
        out_specs=hbm,
        scratch_shapes=[
            pltpu.VMEM((count, rows, WIDE), jnp.bfloat16),
            pltpu.SemaphoreType.DMA((count,)),
            pltpu.SemaphoreType.DMA((count,)),
        ],
        input_output_aliases={len(arrays) + 1: 0},
        compiler_params=pltpu.CompilerParams(vmem_limit_bytes=VMEM_LIMIT),
    )(jnp.stack([jnp.asarray(at, jnp.int32) for at in columns]), *arrays, result)


def per_device(sizes, queries, key_rows, value_rows, tile_lists):
    kv_size, pb_size, z_size = sizes
    planes = kv_size * pb_size
    tokens = queries.shape[0]
    tiles = tokens // TILE
    z = lax.axis_index("head")
    b = lax.axis_index("kv") * pb_size + lax.axis_index("pb")
    core = b & 1

    def swap(x, offset):
        return lax.ppermute(x, AXES, [
            (i * z_size + h, (i ^ offset) * z_size + h) for i in range(planes) for h in range(z_size)
        ])

    def along(x, pairs):
        return lax.ppermute(x, AXES, [
            (i * z_size + h, i * z_size + k) for i in range(planes) for h, k in pairs
        ])

    relay = kv_size == 2 and pb_size == 4 and z_size == 4
    sides = (2, 4) if relay else (2, 2)
    halves = range(2)

    def head_of(half, offset):
        side = sides[half]
        mine = core + 2 * ((b & side) // side)
        return 4 * half + (mine ^ ((offset & 1) + 2 * ((offset & side) // side)))

    def near(half):
        return (0, 1, sides[half], sides[half] + 1)

    own_lists = lax.dynamic_slice_in_dim(tile_lists, z * tiles, tiles, axis=0)
    rider = jnp.concatenate([own_lists % 128, own_lists // 128], axis=0).astype(jnp.bfloat16)
    rider = jnp.pad(rider, ((0, -(2 * tiles) % 16), (0, 2 * HEAD_DIM - SLOTS)))
    own, lists = [], []
    for half in halves:
        blocks, riders = [], []
        for offset in near(half):
            at = head_of(half, offset) * HEAD_DIM
            piece = jnp.concatenate(
                [lax.dynamic_slice_in_dim(a, at, HEAD_DIM, axis=1) for a in (key_rows, value_rows)],
                axis=1,
            )
            piece = jnp.concatenate([piece, rider], axis=0)
            if offset:
                piece = swap(piece, offset)
            blocks.append(piece[:tokens])
            parts = piece[tokens:tokens + 2 * tiles, :SLOTS].astype(jnp.int32)
            riders.append(parts[:tiles] + 128 * parts[tiles:])
        own.append(jnp.concatenate(blocks, axis=0))
        lists.append(dict(zip(near(half), riders)))
    *own, queries = lax.optimization_barrier((*own, queries))

    def heads(array, at, count=1):
        return lax.dynamic_slice_in_dim(array, at, count * WIDE, axis=1)

    def query_pair(half):
        return heads(queries, (head_of(half, sides[half]) - core) * WIDE, 2)

    def tie(*arrays):
        return lax.optimization_barrier(arrays)

    def core_pairs(crossed):
        return jnp.concatenate([
            part for half in halves
            for part in (heads(queries, head_of(half, 1) * WIDE), heads(crossed[half], (1 - core) * WIDE))
        ], axis=1)

    if relay:
        across = [6 - side for side in sides]
        middle = jnp.logical_or(z == 1, z == 2)
        by_two, by_one = ((0, 2), (1, 3), (2, 0), (3, 1)), ((0, 1), (1, 0), (2, 3), (3, 2))
        outward, inward = ((1, 0), (2, 3)), ((1, 2), (2, 1))
        own_a, own_b = own
        rows = own_a.shape[0]
        both = jnp.concatenate(own, axis=0)
        two, one = along(both, by_two), along(both, by_one)
        own_a_far, own_b_far = swap(own_a, across[0]), swap(own_b, across[1])
        crossed_a = swap(query_pair(0), sides[0])
        turned_b, own_a_far = tie(query_pair(1), own_a_far)
        crossed_b = swap(turned_b, sides[1])
        both, one, two, own_a, own_b, own_a_far, own_b_far, crossed_a, crossed_b = tie(
            both, one, two, own_a, own_b, own_a_far, own_b_far, crossed_a, crossed_b
        )
        crossed = [crossed_a, crossed_b]
        outer, inner = along(two, outward), along(both, inward)
        pair_a = jnp.concatenate([one[:rows], two[:rows]], axis=0)
        pair_b = jnp.concatenate([one[rows:], two[rows:]], axis=0)
        pair_a_far, pair_b_far = swap(pair_a, across[0]), swap(pair_b, across[1])
        outer, inner, pair_a, pair_b, pair_a_far, pair_b_far, turned = tie(
            outer, inner, pair_a, pair_b, pair_a_far, pair_b_far, core_pairs(crossed)
        )
        by_core = swap(turned, 1)
        three = jnp.where(middle, inner, outer)
        three_a, three_b = three[:rows], three[rows:]
        kv_bufs = [
            [own_a, own_a_far, pair_a, pair_a_far, three_a, swap(three_a, across[0])],
            [own_b, own_b_far, pair_b, pair_b_far, three_b, swap(three_b, across[1])],
        ]
    else:
        kv_bufs = [[lax.all_gather(x, ("kv", "head"), axis=0, tiled=True)] for x in own]
        crossed = [swap(query_pair(half), sides[half]) for half in halves]
        by_core = swap(core_pairs(crossed), 1)

    def place(half, tile):
        device, within = tile // tiles, tile % tiles
        where, z_from = device // z_size, device % z_size
        differ = where ^ b
        side = sides[half]
        slot = (differ & 1) + 2 * ((differ & side) // side)
        if relay:
            distance, far = z_from ^ z, (differ & across[half]) // across[half]
            block = jnp.where(
                distance == 0, far, jnp.where(distance == 3, 6 + far, 1 + distance + 2 * far)
            )
        else:
            block = (where // pb_size) * z_size + z_from
        return (block * 4 + slot) * tiles + within

    kv_tiles = planes * z_size * tiles

    def operands(blocks):
        tids, locs, seen = [], [], []
        for half, offset in blocks:
            if half not in seen:
                seen.append(half)
            tids.append(((b ^ offset) * z_size + z) * tiles + jnp.arange(tiles, dtype=jnp.int32))
            locs.append(place(half, lists[half][offset]) + seen.index(half) * kv_tiles)
        q_blocks = []
        for half, offset in blocks:
            if offset == 0:
                q_blocks.append((queries, head_of(half, 0) * WIDE))
            elif offset == 1:
                q_blocks.append((by_core, 2 * half * WIDE))
            elif offset == sides[half]:
                q_blocks.append((crossed[half], core * WIDE))
            else:
                q_blocks.append((by_core, (2 * half + 1) * WIDE))
        bufs = [buf for half in seen for buf in kv_bufs[half]]
        return q_blocks, bufs, jnp.concatenate(locs, axis=0), jnp.concatenate(tids)

    diagonal = [(half, sides[half] + 1) for half in halves]
    straight, beside = [(half, sides[half]) for half in halves], [(half, 1) for half in halves]
    *outs, turn = attend(jnp.zeros((1,), jnp.int32), tiles, *operands(diagonal))
    *more, turn = attend(turn, tiles, *operands(straight + beside), shared=len(beside))
    sent = diagonal + straight + beside
    arrays = [swap(out, offset) for out, (_, offset) in zip(outs + more, sent)]
    columns = [head_of(half, offset) * WIDE for half, offset in sent]
    early = len(diagonal)
    result, _ = attend(
        turn, tiles, *operands([(half, 0) for half in halves]), [head_of(half, 0) * WIDE for half in halves],
        pieces=list(zip(arrays, columns))[:early],
    )
    return deliver(result, arrays[early:], columns[early:])


def solution(mesh):
    in_specs = (P(AXES, None), P(AXES, None), P(AXES, None), P(("kv", "pb"), None))
    sizes = tuple(mesh.shape[axis] for axis in AXES)
    return jax.shard_map(
        functools.partial(per_device, sizes),
        mesh=mesh, in_specs=in_specs, out_specs=P(AXES, None), check_vma=False,
    )
```

time: 166 us -> 161 us (0.970)
  local copies, waits for them, and re-layouts: 16.6 us -> 7.71 us
  starting transfers between devices: 29.8 us -> 26.4 us
  waiting for transfers between devices: 77.7 us -> 80.8 us
  Pallas kernels: 36 us -> 38.9 us
    ppermute x21 -> x20, waiting for transfers between devices: 31 us -> 44.6 us  [swap(): lax.ppermute(x, AXES, [(i * z_size + h, (i ^ offset) * z_size + h) for i...]
    ppermute x4, waiting for transfers between devices: 46.7 us -> 36.2 us  [along(): lax.ppermute(x, AXES, [(i * z_size + h, i * z_size + k) for i in range(pl...]
    ppermute x21 -> x20, starting transfers between devices: 20.7 us -> 16.9 us  [swap(): lax.ppermute(x, AXES, [(i * z_size + h, (i ^ offset) * z_size + h) for i...]
    dynamic_slice x3 -> x4, local copies, waits for them, and re-layouts: 3.9 us -> 0.35 us  [heads(): return lax.dynamic_slice_in_dim(array, at, count * WIDE, axis=1)]
    pallas_call x4, Pallas kernels: 36 us -> 38.9 us  [the longest x3 35.9 us: attend(): pl.pallas_call(functools.partial(attend_kernel, blocks, tiles, starts, di...]
    unnamed x25 -> x37, local copies, waits for them, and re-layouts: 4.92 us -> 2.41 us
    reshape x0 -> x3, local copies, waits for them, and re-layouts: none -> 1.85 us  [attend(): loc.reshape(-1)]
  transfers between devices with their start and end apart: 25 -> 24, of which waited for: 14 -> 11; matrix products, arithmetic and copies ran while one was open for 8% -> 5% of each run, Pallas kernels for 22% -> 17%
where the time goes in v4:
time: 161 us; the launch traced here: 160 us
  waiting for transfers between devices  80.8 us (50%)
  Pallas kernels  38.9 us (24%)
  starting transfers between devices  26.4 us (16%)
  local copies, waits for them, and re-layouts  7.71 us (5%)
  other arithmetic  5.47 us (3%)
    ppermute x20, waiting for transfers between devices, swap(): lax.ppermute(x, AXES, [(i * z_size + h, (i ^ offset) * z_size + h) for i...  44.6 us
    ppermute x4, waiting for transfers between devices, along(): lax.ppermute(x, AXES, [(i * z_size + h, i * z_size + k) for i in range(pl...  36.2 us
    pallas_call x3, Pallas kernels, attend(): pl.pallas_call(functools.partial(attend_kernel, blocks, tiles, starts, di...  35.9 us
    ppermute x20, starting transfers between devices, swap(): lax.ppermute(x, AXES, [(i * z_size + h, (i ^ offset) * z_size + h) for i...  16.9 us
    ppermute x4, starting transfers between devices, along(): lax.ppermute(x, AXES, [(i * z_size + h, i * z_size + k) for i in range(pl...  9.57 us
  transfers between devices with their start and end apart: 24, of which 11 were waited for; matrix products, arithmetic and copies ran while one was open for 5% of the time, Pallas kernels for 17%

profile of v4, /device:TPU:17, one launch (start us, length us, event | category | flops | bytes accessed | tf_op | source)
XLA Modules:
  0.0 160.0 jit_solution(14024376079646318054)
XLA Ops:
  0.0 0.7 fusion.41
  0.7 1.4 constant_dynamic-slice_fusion.10
  2.2 0.7 collective-permute-start.4
  2.9 1.2 collective-permute-start.1
  4.6 1.2 collective-permute-start.3
  9.2 0.7 reshape.11.loc_ref
  10.6 2.7 %collective-permute-done = bf16[272,256]{1,0:T(8,128)(2,1)S(1)} collective-permute-done((bf16[272,256]{1,0:T(8,128)(2,1)S(1)}, bf16[272,256]{1,0:T(8,128)(2,1)S(1)}, u32[]{:S(2)}, u32[]{:S(2)}) %collective-permute-start) | collective-permute-done | bytes 139296 | tf_op jit(solution)/shard_map/ppermute | solution.py:266
  13.9 1.3 collective-permute-start.9
  15.3 1.3 collective-permute-start.6
  17.3 8.8 %collective-permute-done.8.refs_3_.refs_5_ = bf16[1024,256]{1,0:T(8,128)(2,1)S(1)} collective-permute-done((bf16[1024,256]{1,0:T(8,128)(2,1)S(1)}, bf16[1024,256]{1,0:T(8,128)(2,1)S(1)}, u32[]{:S(2)}, u32[]{:S(2)}) %collective-permute-start.8) | collective-permute-done | bytes 524320 | tf_op jit(solution)/shard_map/ppermute | solution.py:266
  26.5 33.2 %collective-permute-done.7 = bf16[2048,256]{1,0:T(8,128)(2,1)S(1)} collective-permute-done((bf16[2048,256]{1,0:T(8,128)(2,1)S(1)}, bf16[2048,256]{1,0:T(8,128)(2,1)S(1)}, u32[]{:S(2)}, u32[]{:S(2)}) %collective-permute-start.7) | collective-permute-done | bytes 1048608 | tf_op jit(solution)/shard_map/ppermute | solution.py:271
  59.7 1.2 collective-permute-done.6
  61.0 6.0 %collective-permute-start.12 = (bf16[2048,256]{1,0:T(8,128)(2,1)S(1)}, bf16[2048,256]{1,0:T(8,128)(2,1)S(1)}, u32[]{:S(2)}, u32[]{:S(2)}) collective-permute-start(bf16[2048,256]{1,0:T(8,128)(2,1)S(1)} %collective-permute-done.7), channel_id=1, source_target_pairs={{1,0},{2,3},{5,4},{6,7},{9,8},{10,11},{13,12},{14,15},{17,16},{18,... | collective-permute-start | bytes 3145736 | tf_op jit(solution)/shard_map/ppermute | solution.py:271
  67.2 1.3 collective-permute-start.14
  68.9 2.1 %collective-permute-start.13 = (bf16[2048,256]{1,0:T(8,128)(2,1)S(1)}, bf16[2048,256]{1,0:T(8,128)(2,1)S(1)}, u32[]{:S(2)}, u32[]{:S(2)}) collective-permute-start(bf16[2048,256]{1,0:T(8,128)(2,1)S(1)} %constant_dynamic-update-slice_fusion), channel_id=1, source_target_pairs={{1,2},{2,1},{5,6},{6,5},{9,10},{10,9},{13,14},{14,13},{17,18},{18,... | collective-permute-start | bytes 3145736 | tf_op jit(solution)/shard_map/ppermute | solution.py:271
  71.4 19.8 %collective-permute-done.14.refs_5_.refs_7_ = bf16[2048,256]{1,0:T(8,128)(2,1)S(1)} collective-permute-done((bf16[2048,256]{1,0:T(8,128)(2,1)S(1)}, bf16[2048,256]{1,0:T(8,128)(2,1)S(1)}, u32[]{:S(2)}, u32[]{:S(2)}) %collective-permute-start.14) | collective-permute-done | bytes 1048608 | tf_op jit(solution)/shard_map/ppermute | solution.py:266
  91.2 1.1 collective-permute-done.15.refs_11_.refs_13_
  92.2 1.9 %collective-permute-done.13 = bf16[2048,256]{1,0:T(8,128)(2,1)S(1)} collective-permute-done((bf16[2048,256]{1,0:T(8,128)(2,1)S(1)}, bf16[2048,256]{1,0:T(8,128)(2,1)S(1)}, u32[]{:S(2)}, u32[]{:S(2)}) %collective-permute-start.13) | collective-permute-done | bytes 1048608 | tf_op jit(solution)/shard_map/ppermute | solution.py:271
  94.1 2.3 %collective-permute-start.16 = (bf16[256,4096]{1,0:T(8,128)(2,1)S(1)}, bf16[256,4096]{1,0:T(8,128)(2,1)}, u32[]{:S(2)}, u32[]{:S(2)}) collective-permute-start(bf16[256,4096]{1,0:T(8,128)(2,1)S(1)} %pad_maximum_fusion), channel_id=1, source_target_pairs={{0,4},{1,5},{2,6},{3,7},{4,0},{5,1},{6,2},{7,3},{8,12},{9,13},{10,... | collective-permute-start | bytes 6291464 | tf_op jit(solution)/shard_map/ppermute | solution.py:266
  97.0 1.3 broadcast_select_fusion
  98.4 0.9 fusion.46
  99.3 1.2 collective-permute-start.18
  101.4 10.5 %collective-permute-done.18.refs_13_.refs_15_ = bf16[1024,256]{1,0:T(8,128)(2,1)} collective-permute-done((bf16[1024,256]{1,0:T(8,128)(2,1)S(1)}, bf16[1024,256]{1,0:T(8,128)(2,1)}, u32[]{:S(2)}, u32[]{:S(2)}) %collective-permute-start.18) | collective-permute-done | bytes 524320 | tf_op jit(solution)/shard_map/ppermute | solution.py:266
  111.9 1.1 collective-permute-done.17.refs_7_.refs_9_
  113.0 8.9 %shard_map.46 = (bf16[256,1024]{1,0:T(8,128)(2,1)}, bf16[256,1024]{1,0:T(8,128)(2,1)}, s32[1]{0:T(128)}) custom-call(s32[1]{0:T(128)} %constant.408.clone.1.turn_ref, s32[32]{0:T(128)} %reshape.9.loc_ref, s32[4]{0:T(128)} %get-tuple-element.102.tid_ref, s32[2]{0:T(128)} %constant.417.clone.1.col_ref, ...), custom_call_target="tpu_custom_call" | custom-call | flops 40000000000 | bytes 1000000 | tf_op jit(solution)/shard_map/pallas_call | solution.py:193
  121.9 2.4 %collective-permute-start.22 = (bf16[256,1024]{1,0:T(8,128)(2,1)}, bf16[256,1024]{1,0:T(8,128)(2,1)S(1)}, u32[]{:S(2)}, u32[]{:S(2)}) collective-permute-start(bf16[256,1024]{1,0:T(8,128)(2,1)} %get-tuple-element.60), channel_id=1, source_target_pairs={{0,12},{1,13},{2,14},{3,15},{4,8},{5,9},{6,10},{7,11},{8,4},{9,5},... | collective-permute-start | bytes 1572872 | tf_op jit(solution)/shard_map/ppermute | solution.py:266
  124.3 17.2 %shard_map.47 = (bf16[256,1024]{1,0:T(8,128)(2,1)}, bf16[256,1024]{1,0:T(8,128)(2,1)}, bf16[512,1024]{1,0:T(8,128)(2,1)}, s32[1]{0:T(128)}) custom-call(s32[1]{0:T(128)} %get-tuple-element.55.turn_ref, s32[64]{0:T(128)} %reshape.10.loc_ref, s32[8]{0:T(128)} %pad_add_fusion.5.tid_ref, s32[4]{0:T(128)} %get-tuple-element.103.col_ref, ...), custom_call_target="tpu_custom_call" | custom-call | flops 80000000000 | bytes 1000000 | tf_op jit(solution)/shard_map/pallas_call | solution.py:193
  141.9 2.1 %collective-permute-start.21 = (bf16[512,1024]{1,0:T(8,128)(2,1)}, bf16[512,1024]{1,0:T(8,128)(2,1)S(1)}, u32[]{:S(2)}, u32[]{:S(2)}) collective-permute-start(bf16[512,1024]{1,0:T(8,128)(2,1)} %get-tuple-element.58), channel_id=1, source_target_pairs={{0,4},{1,5},{2,6},{3,7},{4,0},{5,1},{6,2},{7,3},{8,12},{9,13},{10,... | collective-permute-start | bytes 3145736 | tf_op jit(solution)/shard_map/ppermute | solution.py:266
  144.0 0.8 copy-done.16
  145.0 9.8 %shard_map.48 = (bf16[256,8192]{1,0:T(8,128)(2,1)}, s32[1]{0:T(128)}) custom-call(s32[1]{0:T(128)} %get-tuple-element.59.turn_ref, s32[32]{0:T(128)} %reshape.11.loc_ref, s32[4]{0:T(128)} %pad_add_fusion.7.tid_ref, s32[6]{0:T(128)} %stack.50.col_ref, bf16[256,8192]{1,0:T(8,128)(2,1)} %refs_1_, bf16[256,8192]{1,0:T(8,128)(2,1)} %refs_1_, ...), custom_call_target="tpu_custom_call" | custom-call | flops 40000000000 | bytes 1000000 | tf_op jit(solution)/shard_map/pallas_call | solution.py:193
  155.4 0.8 copy-done.8
  156.7 3.1 %shard_map.49 = bf16[256,8192]{1,0:T(8,128)(2,1)} custom-call(s32[4]{0:T(128)} %pad_add_fusion.3.col_ref, bf16[256,1024]{1,0:T(8,128)(2,1)} %copy-done.8, bf16[256,1024]{1,0:T(8,128)(2,1)} %copy-done.9, bf16[512,1024]{1,0:T(8,128)(2,1)} %copy-done.6, bf16[256,8192]{1,0:T(8,128)(2,1)} %get-tuple-element.62.refs_3_), custom_call_target="tpu_custom_call", output_to_operand_aliasing={{}: (4, {})} | custom-call | tf_op jit(solution)/shard_map/pallas_call | solution.py:241
  (111 shorter events, 10.7 us)
Async XLA Ops:
  2.2 6.2 %collective-permute-start.4 = (bf16[272,256]{1,0:T(8,128)(2,1)S(1)}, bf16[272,256]{1,0:T(8,128)(2,1)S(1)}, u32[]{:S(2)}, u32[]{:S(2)}) collective-permute-start(bf16[272,256]{1,0:T(8,128)(2,1)S(1)} %get-tuple-element.96), channel_id=1, source_target_pairs={{0,4},{1,5},{2,6},{3,7},{4,0},{5,1},{6,2},{7,3},{8,12},{9,13},{10,... | collective-permute-start | bytes 417800 | tf_op jit(solution)/shard_map/ppermute | solution.py:266
  2.9 7.5 %collective-permute-start.1 = (bf16[272,256]{1,0:T(8,128)(2,1)S(1)}, bf16[272,256]{1,0:T(8,128)(2,1)S(1)}, u32[]{:S(2)}, u32[]{:S(2)}) collective-permute-start(bf16[272,256]{1,0:T(8,128)(2,1)S(1)} %get-tuple-element.97), channel_id=1, source_target_pairs={{0,20},{1,21},{2,22},{3,23},{4,16},{5,17},{6,18},{7,19},{8,28},{9,... | collective-permute-start | bytes 417800 | tf_op jit(solution)/shard_map/ppermute | solution.py:266
  4.1 6.4 %collective-permute-start.2 = (bf16[272,256]{1,0:T(8,128)(2,1)S(1)}, bf16[272,256]{1,0:T(8,128)(2,1)S(1)}, u32[]{:S(2)}, u32[]{:S(2)}) collective-permute-start(bf16[272,256]{1,0:T(8,128)(2,1)S(1)} %get-tuple-element.98), channel_id=1, source_target_pairs={{0,4},{1,5},{2,6},{3,7},{4,0},{5,1},{6,2},{7,3},{8,12},{9,13},{10,... | collective-permute-start | bytes 417800 | tf_op jit(solution)/shard_map/ppermute | solution.py:266
  4.6 5.9 %collective-permute-start.3 = (bf16[272,256]{1,0:T(8,128)(2,1)S(1)}, bf16[272,256]{1,0:T(8,128)(2,1)S(1)}, u32[]{:S(2)}, u32[]{:S(2)}) collective-permute-start(bf16[272,256]{1,0:T(8,128)(2,1)S(1)} %get-tuple-element.99), channel_id=1, source_target_pairs={{0,8},{1,9},{2,10},{3,11},{4,12},{5,13},{6,14},{7,15},{8,0},{9,1},... | collective-permute-start | bytes 417800 | tf_op jit(solution)/shard_map/ppermute | solution.py:266
  5.8 7.5 %collective-permute-start = (bf16[272,256]{1,0:T(8,128)(2,1)S(1)}, bf16[272,256]{1,0:T(8,128)(2,1)S(1)}, u32[]{:S(2)}, u32[]{:S(2)}) collective-permute-start(bf16[272,256]{1,0:T(8,128)(2,1)S(1)} %get-tuple-element.100), channel_id=1, source_target_pairs={{0,12},{1,13},{2,14},{3,15},{4,8},{5,9},{6,10},{7,11},{8,4},{9,5},... | collective-permute-start | bytes 417800 | tf_op jit(solution)/shard_map/ppermute | solution.py:266
  8.4 5.1 %collective-permute-start.5 = (bf16[272,256]{1,0:T(8,128)(2,1)S(1)}, bf16[272,256]{1,0:T(8,128)(2,1)S(1)}, u32[]{:S(2)}, u32[]{:S(2)}) collective-permute-start(bf16[272,256]{1,0:T(8,128)(2,1)S(1)} %get-tuple-element.101), channel_id=1, source_target_pairs={{0,16},{1,17},{2,18},{3,19},{4,20},{5,21},{6,22},{7,23},{8,24},{9,... | collective-permute-start | bytes 417800 | tf_op jit(solution)/shard_map/ppermute | solution.py:266
  13.6 12.5 %collective-permute-start.8 = (bf16[1024,256]{1,0:T(8,128)(2,1)S(1)}, bf16[1024,256]{1,0:T(8,128)(2,1)S(1)}, u32[]{:S(2)}, u32[]{:S(2)}) collective-permute-start(bf16[1024,256]{1,0:T(8,128)(2,1)S(1)} %pad_maximum_fusion.3.refs_2_.refs_4_), channel_id=1, source_target_pairs={{0,16},{1,17},{2,18},{3,19},{4,20},{5,21},{6,22},{7,23},{8,24},{9,... | collective-permute-start | bytes 1572872 | tf_op jit(solution)/shard_map/ppermute | solution.py:266
  13.9 12.6 %collective-permute-start.9 = (bf16[1024,256]{1,0:T(8,128)(2,1)S(1)}, bf16[1024,256]{1,0:T(8,128)(2,1)S(1)}, u32[]{:S(2)}, u32[]{:S(2)}) collective-permute-start(bf16[1024,256]{1,0:T(8,128)(2,1)S(1)} %pad_maximum_fusion.4.refs_8_.refs_10_), channel_id=1, source_target_pairs={{0,8},{1,9},{2,10},{3,11},{4,12},{5,13},{6,14},{7,15},{8,0},{9,1},... | collective-permute-start | bytes 1572872 | tf_op jit(solution)/shard_map/ppermute | solution.py:266
  15.2 44.4 %collective-permute-start.7 = (bf16[2048,256]{1,0:T(8,128)(2,1)S(1)}, bf16[2048,256]{1,0:T(8,128)(2,1)S(1)}, u32[]{:S(2)}, u32[]{:S(2)}) collective-permute-start(bf16[2048,256]{1,0:T(8,128)(2,1)S(1)} %constant_dynamic-update-slice_fusion), channel_id=1, source_target_pairs={{0,2},{1,3},{2,0},{3,1},{4,6},{5,7},{6,4},{7,5},{8,10},{9,11},{10,... | collective-permute-start | bytes 3145736 | tf_op jit(solution)/shard_map/ppermute | solution.py:271
  15.3 45.5 %collective-permute-start.6 = (bf16[2048,256]{1,0:T(8,128)(2,1)S(1)}, bf16[2048,256]{1,0:T(8,128)(2,1)S(1)}, u32[]{:S(2)}, u32[]{:S(2)}) collective-permute-start(bf16[2048,256]{1,0:T(8,128)(2,1)S(1)} %constant_dynamic-update-slice_fusion), channel_id=1, source_target_pairs={{0,1},{1,0},{2,3},{3,2},{4,5},{5,4},{6,7},{7,6},{8,9},{9,8},{10,11... | collective-permute-start | bytes 3145736 | tf_op jit(solution)/shard_map/ppermute | solution.py:271
  16.9 44.0 %collective-permute-start.10 = (bf16[256,2048]{1,0:T(8,128)(2,1)S(1)}, bf16[256,2048]{1,0:T(8,128)(2,1)S(1)}, u32[]{:S(2)}, u32[]{:S(2)}) collective-permute-start(bf16[256,2048]{1,0:T(8,128)(2,1)S(1)} %get-tuple-element.68), channel_id=1, source_target_pairs={{0,8},{1,9},{2,10},{3,11},{4,12},{5,13},{6,14},{7,15},{8,0},{9,1},... | collective-permute-start | bytes 3145736 | tf_op jit(solution)/shard_map/ppermute | solution.py:266
  26.1 41.0 %copy-start.14 = (bf16[1024,256]{1,0:T(8,128)(2,1)}, bf16[1024,256]{1,0:T(8,128)(2,1)S(1)}, u32[]{:S(2)}) copy-start(bf16[1024,256]{1,0:T(8,128)(2,1)S(1)} %collective-permute-done.8.refs_3_.refs_5_) | copy-start | bytes 1572868
  26.1 34.8 %collective-permute-start.11 = (bf16[256,2048]{1,0:T(8,128)(2,1)S(1)}, bf16[256,2048]{1,0:T(8,128)(2,1)S(1)}, u32[]{:S(2)}, u32[]{:S(2)}) collective-permute-start(bf16[256,2048]{1,0:T(8,128)(2,1)S(1)} %get-tuple-element.38), channel_id=1, source_target_pairs={{0,16},{1,17},{2,18},{3,19},{4,20},{5,21},{6,22},{7,23},{8,24},{9,... | collective-permute-start | bytes 3145736 | tf_op jit(solution)/shard_map/ppermute | solution.py:266
  26.5 40.6 %copy-start.15 = (bf16[1024,256]{1,0:T(8,128)(2,1)}, bf16[1024,256]{1,0:T(8,128)(2,1)S(1)}, u32[]{:S(2)}) copy-start(bf16[1024,256]{1,0:T(8,128)(2,1)S(1)} %collective-permute-done.9.refs_9_.refs_11_) | copy-start | bytes 1572868
  60.9 10.2 %copy-start.10 = (bf16[256,2048]{1,0:T(8,128)(2,1)}, bf16[256,2048]{1,0:T(8,128)(2,1)S(1)}, u32[]{:S(2)}) copy-start(bf16[256,2048]{1,0:T(8,128)(2,1)S(1)} %collective-permute-done.10.refs_0_) | copy-start | bytes 3145732
  60.9 10.3 %copy-start.11 = (bf16[256,2048]{1,0:T(8,128)(2,1)}, bf16[256,2048]{1,0:T(8,128)(2,1)S(1)}, u32[]{:S(2)}) copy-start(bf16[256,2048]{1,0:T(8,128)(2,1)S(1)} %collective-permute-done.11.refs_1_) | copy-start | bytes 3145732
  61.0 33.1 %collective-permute-start.12 = (bf16[2048,256]{1,0:T(8,128)(2,1)S(1)}, bf16[2048,256]{1,0:T(8,128)(2,1)S(1)}, u32[]{:S(2)}, u32[]{:S(2)}) collective-permute-start(bf16[2048,256]{1,0:T(8,128)(2,1)S(1)} %collective-permute-done.7), channel_id=1, source_target_pairs={{1,0},{2,3},{5,4},{6,7},{9,8},{10,11},{13,12},{14,15},{17,16},{18,... | collective-permute-start | bytes 3145736 | tf_op jit(solution)/shard_map/ppermute | solution.py:271
  67.2 3.9 %copy-start.3 = (bf16[2048,256]{1,0:T(8,128)(2,1)}, bf16[2048,256]{1,0:T(8,128)(2,1)S(1)}, u32[]{:S(2)}) copy-start(bf16[2048,256]{1,0:T(8,128)(2,1)S(1)} %pad_maximum_fusion.1.refs_4_.refs_6_) | copy-start | bytes 3145732
  67.2 24.0 %collective-permute-start.14 = (bf16[2048,256]{1,0:T(8,128)(2,1)S(1)}, bf16[2048,256]{1,0:T(8,128)(2,1)S(1)}, u32[]{:S(2)}, u32[]{:S(2)}) collective-permute-start(bf16[2048,256]{1,0:T(8,128)(2,1)S(1)} %pad_maximum_fusion.1.refs_4_.refs_6_), channel_id=1, source_target_pairs={{0,16},{1,17},{2,18},{3,19},{4,20},{5,21},{6,22},{7,23},{8,24},{9,... | collective-permute-start | bytes 3145736 | tf_op jit(solution)/shard_map/ppermute | solution.py:266
  68.6 23.7 %collective-permute-start.15 = (bf16[2048,256]{1,0:T(8,128)(2,1)S(1)}, bf16[2048,256]{1,0:T(8,128)(2,1)S(1)}, u32[]{:S(2)}, u32[]{:S(2)}) collective-permute-start(bf16[2048,256]{1,0:T(8,128)(2,1)S(1)} %pad_maximum_fusion.2.refs_10_.refs_12_), channel_id=1, source_target_pairs={{0,8},{1,9},{2,10},{3,11},{4,12},{5,13},{6,14},{7,15},{8,0},{9,1},... | collective-permute-start | bytes 3145736 | tf_op jit(solution)/shard_map/ppermute | solution.py:266
  68.9 25.2 %collective-permute-start.13 = (bf16[2048,256]{1,0:T(8,128)(2,1)S(1)}, bf16[2048,256]{1,0:T(8,128)(2,1)S(1)}, u32[]{:S(2)}, u32[]{:S(2)}) collective-permute-start(bf16[2048,256]{1,0:T(8,128)(2,1)S(1)} %constant_dynamic-update-slice_fusion), channel_id=1, source_target_pairs={{1,2},{2,1},{5,6},{6,5},{9,10},{10,9},{13,14},{14,13},{17,18},{18,... | collective-permute-start | bytes 3145736 | tf_op jit(solution)/shard_map/ppermute | solution.py:271
  91.2 5.2 %copy-start.12 = (bf16[2048,256]{1,0:T(8,128)(2,1)}, bf16[2048,256]{1,0:T(8,128)(2,1)S(1)}, u32[]{:S(2)}) copy-start(bf16[2048,256]{1,0:T(8,128)(2,1)S(1)} %collective-permute-done.14.refs_5_.refs_7_) | copy-start | bytes 3145732
  92.2 4.1 %copy-start.13 = (bf16[2048,256]{1,0:T(8,128)(2,1)}, bf16[2048,256]{1,0:T(8,128)(2,1)S(1)}, u32[]{:S(2)}) copy-start(bf16[2048,256]{1,0:T(8,128)(2,1)S(1)} %collective-permute-done.15.refs_11_.refs_13_) | copy-start | bytes 3145732
  94.1 18.9 %collective-permute-start.16 = (bf16[256,4096]{1,0:T(8,128)(2,1)S(1)}, bf16[256,4096]{1,0:T(8,128)(2,1)}, u32[]{:S(2)}, u32[]{:S(2)}) collective-permute-start(bf16[256,4096]{1,0:T(8,128)(2,1)S(1)} %pad_maximum_fusion), channel_id=1, source_target_pairs={{0,4},{1,5},{2,6},{3,7},{4,0},{5,1},{6,2},{7,3},{8,12},{9,13},{10,... | collective-permute-start | bytes 6291464 | tf_op jit(solution)/shard_map/ppermute | solution.py:266
  99.3 13.7 %copy-start.7 = (bf16[1024,256]{1,0:T(8,128)(2,1)}, bf16[1024,256]{1,0:T(8,128)(2,1)S(1)}, u32[]{:S(2)}) copy-start(bf16[1024,256]{1,0:T(8,128)(2,1)S(1)} %get-tuple-element.70.refs_12_.refs_14_) | copy-start | bytes 1572868
  99.3 12.6 %collective-permute-start.18 = (bf16[1024,256]{1,0:T(8,128)(2,1)S(1)}, bf16[1024,256]{1,0:T(8,128)(2,1)}, u32[]{:S(2)}, u32[]{:S(2)}) collective-permute-start(bf16[1024,256]{1,0:T(8,128)(2,1)S(1)} %get-tuple-element.70.refs_12_.refs_14_), channel_id=1, source_target_pairs={{0,8},{1,9},{2,10},{3,11},{4,12},{5,13},{6,14},{7,15},{8,0},{9,1},... | collective-permute-start | bytes 1572872 | tf_op jit(solution)/shard_map/ppermute | solution.py:266
  100.5 12.5 %collective-permute-start.17 = (bf16[1024,256]{1,0:T(8,128)(2,1)}, bf16[1024,256]{1,0:T(8,128)(2,1)}, u32[]{:S(2)}, u32[]{:S(2)}) collective-permute-start(bf16[1024,256]{1,0:T(8,128)(2,1)} %get-tuple-element.71.refs_6_.refs_8_), channel_id=1, source_target_pairs={{0,16},{1,17},{2,18},{3,19},{4,20},{5,21},{6,22},{7,23},{8,24},{9,... | collective-permute-start | bytes 1572872 | tf_op jit(solution)/shard_map/ppermute | solution.py:266
  121.9 22.1 %collective-permute-start.22 = (bf16[256,1024]{1,0:T(8,128)(2,1)}, bf16[256,1024]{1,0:T(8,128)(2,1)S(1)}, u32[]{:S(2)}, u32[]{:S(2)}) collective-permute-start(bf16[256,1024]{1,0:T(8,128)(2,1)} %get-tuple-element.60), channel_id=1, source_target_pairs={{0,12},{1,13},{2,14},{3,15},{4,8},{5,9},{6,10},{7,11},{8,4},{9,5},... | collective-permute-start | bytes 1572872 | tf_op jit(solution)/shard_map/ppermute | solution.py:266
  124.2 19.8 %collective-permute-start.23 = (bf16[256,1024]{1,0:T(8,128)(2,1)}, bf16[256,1024]{1,0:T(8,128)(2,1)S(1)}, u32[]{:S(2)}, u32[]{:S(2)}) collective-permute-start(bf16[256,1024]{1,0:T(8,128)(2,1)} %get-tuple-element.61), channel_id=1, source_target_pairs={{0,20},{1,21},{2,22},{3,23},{4,16},{5,17},{6,18},{7,19},{8,28},{9,... | collective-permute-start | bytes 1572872 | tf_op jit(solution)/shard_map/ppermute | solution.py:266
  141.5 13.9 %collective-permute-start.19 = (bf16[256,1024]{1,0:T(8,128)(2,1)}, bf16[256,1024]{1,0:T(8,128)(2,1)S(1)}, u32[]{:S(2)}, u32[]{:S(2)}) collective-permute-start(bf16[256,1024]{1,0:T(8,128)(2,1)} %get-tuple-element.56), channel_id=1, source_target_pairs={{0,8},{1,9},{2,10},{3,11},{4,12},{5,13},{6,14},{7,15},{8,0},{9,1},... | collective-permute-start | bytes 1572872 | tf_op jit(solution)/shard_map/ppermute | solution.py:266
  141.6 13.8 %collective-permute-start.20 = (bf16[256,1024]{1,0:T(8,128)(2,1)}, bf16[256,1024]{1,0:T(8,128)(2,1)S(1)}, u32[]{:S(2)}, u32[]{:S(2)}) collective-permute-start(bf16[256,1024]{1,0:T(8,128)(2,1)} %get-tuple-element.57), channel_id=1, source_target_pairs={{0,16},{1,17},{2,18},{3,19},{4,20},{5,21},{6,22},{7,23},{8,24},{9,... | collective-permute-start | bytes 1572872 | tf_op jit(solution)/shard_map/ppermute | solution.py:266
  141.9 13.4 %collective-permute-start.21 = (bf16[512,1024]{1,0:T(8,128)(2,1)}, bf16[512,1024]{1,0:T(8,128)(2,1)S(1)}, u32[]{:S(2)}, u32[]{:S(2)}) collective-permute-start(bf16[512,1024]{1,0:T(8,128)(2,1)} %get-tuple-element.58), channel_id=1, source_target_pairs={{0,4},{1,5},{2,6},{3,7},{4,0},{5,1},{6,2},{7,3},{8,12},{9,13},{10,... | collective-permute-start | bytes 3145736 | tf_op jit(solution)/shard_map/ppermute | solution.py:266
  (10 other events, 20.0 us)

commit v5 on v4

--- a/solution.py
+++ b/solution.py
@@ -16,7 +16,7 @@
 NEG = -1e30
 GROUPS = HEADS // KV_HEADS
 WIDE = GROUPS * HEAD_DIM
-VMEM_LIMIT = 60 * 2**20
+VMEM_LIMIT, DELIVER_LIMIT = 60 * 2**20, 8 * 2**20
 AXES = ("kv", "pb", "head")
 LOG2 = HEAD_DIM ** (-0.5) * 1.4426950408889634
 
@@ -90,14 +90,17 @@
         for i in range(blocks)
     ]
 
-    def fetch(slot, sem):
-        at = loc_ref[slot]
-        for ref, start in zip(kv_refs, starts):
-            here = at - start
-
-            @pl.when(jnp.logical_and(here >= 0, here < ref.shape[0] // TILE))
-            def _(ref=ref, here=here):
-                pltpu.make_async_copy(ref.at[rows_of(here)], kv_buf.at[rows_of(slot)], sem).start()
+    def fetch_from(first, last, at, slot, sem):
+        if last - first == 1:
+            source = kv_refs[first].at[rows_of(at - starts[first])]
+            pltpu.make_async_copy(source, kv_buf.at[rows_of(slot)], sem).start()
+            return 0
+        cut = (first + last) // 2
+        return lax.cond(
+            at < starts[cut],
+            lambda: fetch_from(first, cut, at, slot, sem),
+            lambda: fetch_from(cut, last, at, slot, sem),
+        )
 
     def fetch_block(i):
         slots = tiles * SLOTS
@@ -105,12 +108,11 @@
             pl.when(i == k)(copy.start)
 
         def one_slot(slot, _):
-            fetch(slot, kv_sem.at[i])
-            return 0
-
-        lax.fori_loop(i * slots, (i + 1) * slots, one_slot, 0)
-
-    fetch_block(0)
+            return fetch_from(0, len(kv_refs), loc_ref[slot], slot, kv_sem.at[i])
+
+        return lax.fori_loop(i * slots, (i + 1) * slots, one_slot, 0)
+
+    lax.fori_loop(0, blocks, lambda i, _: fetch_block(i), 0)
     piece_ins, piece_outs = [], []
     for i in range(pieces):
         buf = piece_buf.at[rows_of(i * tiles, tiles)]
@@ -135,7 +137,6 @@
 
     def one_block(i, _):
         first = i * tiles
-        pl.when(i + 1 < blocks)(lambda: fetch_block(i + 1))
         rows = q_buf.at[rows_of(first, tiles)]
         pltpu.make_async_copy(rows, rows, q_sem.at[i]).wait()
         listed = kv_buf.at[rows_of(first * SLOTS, tiles * SLOTS)]
@@ -212,44 +213,33 @@
 
 
 def deliver_kernel(sources, rows, col_ref, *refs):
-    count, arrays = len(sources), len(refs) - 5
-    out_ref, piece_buf, in_sem, out_sem = refs[arrays + 1:]
-    ins = [
-        pltpu.make_async_copy(refs[array].at[pl.ds(at * rows, rows)], piece_buf.at[i], in_sem.at[i])
+    out_ref, sem = refs[-2:]
+    copies = [
+        pltpu.make_async_copy(
+            refs[array].at[pl.ds(at * rows, rows)],
+            out_ref.at[:, pl.ds(pl.multiple_of(col_ref[i], WIDE), WIDE)], sem.at[i],
+        )
         for i, (array, at) in enumerate(sources)
     ]
-    outs = [
-        pltpu.make_async_copy(
-            piece_buf.at[i], out_ref.at[:, pl.ds(pl.multiple_of(col_ref[i], WIDE), WIDE)], out_sem.at[i]
-        )
-        for i in range(count)
-    ]
-    for copy in ins:
+    for copy in copies:
         copy.start()
-    for copy_in, copy in zip(ins, outs):
-        copy_in.wait()
-        copy.start()
-    for copy in outs:
+    for copy in copies:
         copy.wait()
 
 
 def deliver(result, arrays, columns):
     rows = result.shape[0]
     sources = [(i, at) for i, array in enumerate(arrays) for at in range(array.shape[0] // rows)]
-    count = len(sources)
     hbm = pl.BlockSpec(memory_space=pl.ANY)
     return pl.pallas_call(
         functools.partial(deliver_kernel, sources, rows),
         out_shape=jax.ShapeDtypeStruct(result.shape, result.dtype),
-        in_specs=[pl.BlockSpec(memory_space=pltpu.SMEM)] + [hbm] * (len(arrays) + 1),
+        in_specs=[pl.BlockSpec(memory_space=pltpu.SMEM)]
+        + [pl.BlockSpec(memory_space=pltpu.VMEM)] * len(arrays) + [hbm],
         out_specs=hbm,
-        scratch_shapes=[
-            pltpu.VMEM((count, rows, WIDE), jnp.bfloat16),
-            pltpu.SemaphoreType.DMA((count,)),
-            pltpu.SemaphoreType.DMA((count,)),
-        ],
+        scratch_shapes=[pltpu.SemaphoreType.DMA((len(sources),))],
         input_output_aliases={len(arrays) + 1: 0},
-        compiler_params=pltpu.CompilerParams(vmem_limit_bytes=VMEM_LIMIT),
+        compiler_params=pltpu.CompilerParams(vmem_limit_bytes=DELIVER_LIMIT),
     )(jnp.stack([jnp.asarray(at, jnp.int32) for at in columns]), *arrays, result)
 
 
@@ -287,23 +277,26 @@
     own_lists = lax.dynamic_slice_in_dim(tile_lists, z * tiles, tiles, axis=0)
     rider = jnp.concatenate([own_lists % 128, own_lists // 128], axis=0).astype(jnp.bfloat16)
     rider = jnp.pad(rider, ((0, -(2 * tiles) % 16), (0, 2 * HEAD_DIM - SLOTS)))
-    own, lists = [], []
-    for half in halves:
-        blocks, riders = [], []
-        for offset in near(half):
-            at = head_of(half, offset) * HEAD_DIM
-            piece = jnp.concatenate(
-                [lax.dynamic_slice_in_dim(a, at, HEAD_DIM, axis=1) for a in (key_rows, value_rows)],
-                axis=1,
-            )
-            piece = jnp.concatenate([piece, rider], axis=0)
-            if offset:
-                piece = swap(piece, offset)
-            blocks.append(piece[:tokens])
-            parts = piece[tokens:tokens + 2 * tiles, :SLOTS].astype(jnp.int32)
-            riders.append(parts[:tiles] + 128 * parts[tiles:])
-        own.append(jnp.concatenate(blocks, axis=0))
-        lists.append(dict(zip(near(half), riders)))
+
+    def key_block(half, offset):
+        at = head_of(half, offset) * HEAD_DIM
+        return jnp.concatenate(
+            [lax.dynamic_slice_in_dim(a, at, HEAD_DIM, axis=1) for a in (key_rows, value_rows)], axis=1
+        )
+
+    blocks = {(half, 0): key_block(half, 0) for half in halves}
+    riders = {0: rider}
+    for group in [[(0, 1), (1, 1)]] + [[(half, sides[half] + c)] for half in halves for c in (0, 1)]:
+        offset = group[0][1]
+        came = swap(jnp.concatenate([key_block(*block) for block in group] + [rider], axis=0), offset)
+        for i, block in enumerate(group):
+            blocks[block] = came[i * tokens:(i + 1) * tokens]
+        riders[offset] = came[len(group) * tokens:]
+    own = [jnp.concatenate([blocks[half, offset] for offset in near(half)], axis=0) for half in halves]
+    lists = {}
+    for offset, came in riders.items():
+        parts = came[:2 * tiles, :SLOTS].astype(jnp.int32)
+        lists[offset] = parts[:tiles] + 128 * parts[tiles:]
     *own, queries = lax.optimization_barrier((*own, queries))
 
     def heads(array, at, count=1):
@@ -380,7 +373,7 @@
             if half not in seen:
                 seen.append(half)
             tids.append(((b ^ offset) * z_size + z) * tiles + jnp.arange(tiles, dtype=jnp.int32))
-            locs.append(place(half, lists[half][offset]) + seen.index(half) * kv_tiles)
+            locs.append(place(half, lists[offset]) + seen.index(half) * kv_tiles)
         q_blocks = []
         for half, offset in blocks:
             if offset == 0:

time: 161 us -> 157 us (0.975)
  waiting for transfers between devices: 80.8 us -> 77.7 us
    ppermute x4, waiting for transfers between devices: 36.2 us -> 12.8 us  [along(): lax.ppermute(x, AXES, [(i * z_size + h, i * z_size + k) for i in range(pl...]
    ppermute x20 -> x19, waiting for transfers between devices: 44.6 us -> 64.9 us  [swap(): lax.ppermute(x, AXES, [(i * z_size + h, (i ^ offset) * z_size + h) for i...]
    ppermute x20 -> x19, starting transfers between devices: 16.9 us -> 19.2 us  [swap(): lax.ppermute(x, AXES, [(i * z_size + h, (i ^ offset) * z_size + h) for i...]
  transfers between devices with their start and end apart: 24 -> 23, of which waited for: 11 -> 10; matrix products, arithmetic and copies ran while one was open for 5% -> 5% of each run, Pallas kernels for 17% -> 18%
where the time goes in v5:
time: 157 us; the launch traced here: 156 us
  waiting for transfers between devices  77.7 us (49%)
  Pallas kernels  38.6 us (25%)
  starting transfers between devices  27.9 us (18%)
  local copies, waits for them, and re-layouts  6.69 us (4%)
  other arithmetic  4.91 us (3%)
    ppermute x19, waiting for transfers between devices, swap(): lax.ppermute(x, AXES, [(i * z_size + h, (i ^ offset) * z_size + h) for i...  64.9 us
    pallas_call x3, Pallas kernels, attend(): pl.pallas_call(functools.partial(attend_kernel, blocks, tiles, starts, di...  36.7 us
    ppermute x19, starting transfers between devices, swap(): lax.ppermute(x, AXES, [(i * z_size + h, (i ^ offset) * z_size + h) for i...  19.2 us
    ppermute x4, waiting for transfers between devices, along(): lax.ppermute(x, AXES, [(i * z_size + h, i * z_size + k) for i in range(pl...  12.8 us
    ppermute x4, starting transfers between devices, along(): lax.ppermute(x, AXES, [(i * z_size + h, i * z_size + k) for i in range(pl...  8.67 us
  transfers between devices with their start and end apart: 23, of which 10 were waited for; matrix products, arithmetic and copies ran while one was open for 5% of the time, Pallas kernels for 18%

profile of v5, /device:TPU:17, one launch (start us, length us, event | category | flops | bytes accessed | tf_op | source)
XLA Modules:
  0.0 156.4 jit_solution(16491420537575619118)
XLA Ops:
  0.7 1.4 constant_dynamic-slice_fusion.8
  2.2 1.3 collective-permute-start.4
  3.5 1.1 collective-permute-start.1
  4.6 1.2 collective-permute-start.3
  9.9 1.0 collective-permute-done.1
  11.0 2.0 %collective-permute-done = bf16[272,256]{1,0:T(8,128)(2,1)S(1)} collective-permute-done((bf16[272,256]{1,0:T(8,128)(2,1)S(1)}, bf16[272,256]{1,0:T(8,128)(2,1)S(1)}, u32[]{:S(2)}, u32[]{:S(2)}) %collective-permute-start) | collective-permute-done | bytes 139296 | tf_op jit(solution)/shard_map/ppermute | solution.py:256
  13.2 1.5 collective-permute-start.7
  14.9 1.3 collective-permute-start.5
  16.5 1.3 collective-permute-start.9
  17.8 8.6 %collective-permute-done.7.refs_3_.refs_5_ = bf16[1024,256]{1,0:T(8,128)(2,1)S(1)} collective-permute-done((bf16[1024,256]{1,0:T(8,128)(2,1)S(1)}, bf16[1024,256]{1,0:T(8,128)(2,1)S(1)}, u32[]{:S(2)}, u32[]{:S(2)}) %collective-permute-start.7) | collective-permute-done | bytes 524320 | tf_op jit(solution)/shard_map/ppermute | solution.py:256
  26.4 1.4 collective-permute-start.10
  27.8 1.3 collective-permute-start.8
  29.2 22.0 %collective-permute-done.8.refs_9_.refs_11_ = bf16[1024,256]{1,0:T(8,128)(2,1)S(1)} collective-permute-done((bf16[1024,256]{1,0:T(8,128)(2,1)S(1)}, bf16[1024,256]{1,0:T(8,128)(2,1)S(1)}, u32[]{:S(2)}, u32[]{:S(2)}) %collective-permute-start.8) | collective-permute-done | bytes 524320 | tf_op jit(solution)/shard_map/ppermute | solution.py:256
  51.2 8.0 %collective-permute-done.6 = bf16[2048,256]{1,0:T(8,128)(2,1)S(1)} collective-permute-done((bf16[2048,256]{1,0:T(8,128)(2,1)S(1)}, bf16[2048,256]{1,0:T(8,128)(2,1)S(1)}, u32[]{:S(2)}, u32[]{:S(2)}) %collective-permute-start.6) | collective-permute-done | bytes 1048608 | tf_op jit(solution)/shard_map/ppermute | solution.py:261
  59.3 2.1 %collective-permute-done.5 = bf16[2048,256]{1,0:T(8,128)(2,1)S(1)} collective-permute-done((bf16[2048,256]{1,0:T(8,128)(2,1)S(1)}, bf16[2048,256]{1,0:T(8,128)(2,1)S(1)}, u32[]{:S(2)}, u32[]{:S(2)}) %collective-permute-start.5) | collective-permute-done | bytes 1048608 | tf_op jit(solution)/shard_map/ppermute | solution.py:261
  61.4 5.1 %collective-permute-start.11 = (bf16[2048,256]{1,0:T(8,128)(2,1)S(1)}, bf16[2048,256]{1,0:T(8,128)(2,1)S(1)}, u32[]{:S(2)}, u32[]{:S(2)}) collective-permute-start(bf16[2048,256]{1,0:T(8,128)(2,1)S(1)} %collective-permute-done.6), channel_id=1, source_target_pairs={{1,0},{2,3},{5,4},{6,7},{9,8},{10,11},{13,12},{14,15},{17,16},{18,... | collective-permute-start | bytes 3145736 | tf_op jit(solution)/shard_map/ppermute | solution.py:261
  66.9 1.3 collective-permute-start.14
  68.2 2.1 %collective-permute-start.12 = (bf16[2048,256]{1,0:T(8,128)(2,1)S(1)}, bf16[2048,256]{1,0:T(8,128)(2,1)S(1)}, u32[]{:S(2)}, u32[]{:S(2)}) collective-permute-start(bf16[2048,256]{1,0:T(8,128)(2,1)S(1)} %constant_dynamic-update-slice_fusion), channel_id=1, source_target_pairs={{1,2},{2,1},{5,6},{6,5},{9,10},{10,9},{13,14},{14,13},{17,18},{18,... | collective-permute-start | bytes 3145736 | tf_op jit(solution)/shard_map/ppermute | solution.py:261
  70.6 1.5 pad_maximum_fusion
  72.1 18.6 %collective-permute-done.13.refs_5_.refs_7_ = bf16[2048,256]{1,0:T(8,128)(2,1)S(1)} collective-permute-done((bf16[2048,256]{1,0:T(8,128)(2,1)S(1)}, bf16[2048,256]{1,0:T(8,128)(2,1)S(1)}, u32[]{:S(2)}, u32[]{:S(2)}) %collective-permute-start.13) | collective-permute-done | bytes 1048608 | tf_op jit(solution)/shard_map/ppermute | solution.py:256
  90.8 2.7 %collective-permute-done.12 = bf16[2048,256]{1,0:T(8,128)(2,1)S(1)} collective-permute-done((bf16[2048,256]{1,0:T(8,128)(2,1)S(1)}, bf16[2048,256]{1,0:T(8,128)(2,1)S(1)}, u32[]{:S(2)}, u32[]{:S(2)}) %collective-permute-start.12) | collective-permute-done | bytes 1048608 | tf_op jit(solution)/shard_map/ppermute | solution.py:261
  93.5 2.3 %collective-permute-start.15 = (bf16[256,4096]{1,0:T(8,128)(2,1)}, bf16[256,4096]{1,0:T(8,128)(2,1)}, u32[]{:S(2)}, u32[]{:S(2)}) collective-permute-start(bf16[256,4096]{1,0:T(8,128)(2,1)} %pad_maximum_fusion), channel_id=1, source_target_pairs={{0,4},{1,5},{2,6},{3,7},{4,0},{5,1},{6,2},{7,3},{8,12},{9,13},{10,... | collective-permute-start | bytes 6291464 | tf_op jit(solution)/shard_map/ppermute | solution.py:256
  97.0 1.4 collective-permute-start.16
  99.1 11.2 %collective-permute-done.17.refs_13_.refs_15_ = bf16[1024,256]{1,0:T(8,128)(2,1)S(1)} collective-permute-done((bf16[1024,256]{1,0:T(8,128)(2,1)S(1)}, bf16[1024,256]{1,0:T(8,128)(2,1)S(1)}, u32[]{:S(2)}, u32[]{:S(2)}) %collective-permute-start.17) | collective-permute-done | bytes 524320 | tf_op jit(solution)/shard_map/ppermute | solution.py:256
  111.2 9.0 %shard_map.46 = (bf16[256,1024]{1,0:T(8,128)(2,1)}, bf16[256,1024]{1,0:T(8,128)(2,1)}, s32[1]{0:T(128)}) custom-call(s32[1]{0:T(128)} %constant.384.clone.1.turn_ref, s32[32]{0:T(128)} %reshape.9.loc_ref, s32[4]{0:T(128)} %get-tuple-element.105.tid_ref, s32[2]{0:T(128)} %constant.393.clone.1.col_ref, ...), custom_call_target="tpu_custom_call" | custom-call | flops 40000000000 | bytes 1000000 | tf_op jit(solution)/shard_map/pallas_call | solution.py:194
  120.2 2.1 %collective-permute-start.21 = (bf16[256,1024]{1,0:T(8,128)(2,1)}, bf16[256,1024]{1,0:T(8,128)(2,1)S(1)}, u32[]{:S(2)}, u32[]{:S(2)}) collective-permute-start(bf16[256,1024]{1,0:T(8,128)(2,1)} %get-tuple-element.60), channel_id=1, source_target_pairs={{0,12},{1,13},{2,14},{3,15},{4,8},{5,9},{6,10},{7,11},{8,4},{9,5},... | collective-permute-start | bytes 1572872 | tf_op jit(solution)/shard_map/ppermute | solution.py:256
  123.0 17.5 %shard_map.47 = (bf16[256,1024]{1,0:T(8,128)(2,1)}, bf16[256,1024]{1,0:T(8,128)(2,1)}, bf16[512,1024]{1,0:T(8,128)(2,1)}, s32[1]{0:T(128)}) custom-call(s32[1]{0:T(128)} %get-tuple-element.55.turn_ref, s32[64]{0:T(128)} %reshape.10.loc_ref, s32[8]{0:T(128)} %pad_add_fusion.5.tid_ref, s32[4]{0:T(128)} %get-tuple-element.106.col_ref, ...), custom_call_target="tpu_custom_call" | custom-call | flops 80000000000 | bytes 1000000 | tf_op jit(solution)/shard_map/pallas_call | solution.py:194
  140.7 1.0 collective-permute-start.20
  141.8 0.8 copy-done.15
  142.8 10.2 %shard_map.48 = (bf16[256,8192]{1,0:T(8,128)(2,1)}, s32[1]{0:T(128)}) custom-call(s32[1]{0:T(128)} %get-tuple-element.59.turn_ref, s32[32]{0:T(128)} %reshape.11.loc_ref, s32[4]{0:T(128)} %pad_add_fusion.7.tid_ref, s32[6]{0:T(128)} %stack.50.col_ref, bf16[256,8192]{1,0:T(8,128)(2,1)} %refs_1_, bf16[256,8192]{1,0:T(8,128)(2,1)} %refs_1_, ...), custom_call_target="tpu_custom_call" | custom-call | flops 40000000000 | bytes 1000000 | tf_op jit(solution)/shard_map/pallas_call | solution.py:194
  152.9 1.4 collective-permute-done.18.refs_0_
  154.3 1.9 %shard_map.49 = bf16[256,8192]{1,0:T(8,128)(2,1)} custom-call(s32[4]{0:T(128)S(1)} %pad_add_fusion.3.col_ref, bf16[256,1024]{1,0:T(8,128)(2,1)S(1)} %collective-permute-done.18.refs_0_, bf16[256,1024]{1,0:T(8,128)(2,1)S(1)} %collective-permute-done.19.refs_1_, bf16[512,1024]{1,0:T(8,128)(2,1)S(1)} %collective-permute-done.20.refs_2_, ...), custom_call_target="tpu_custom_call", output_to_operand_aliasing={{}: (4, {})} | custom-call | tf_op jit(solution)/shard_map/pallas_call | solution.py:234
  (107 shorter events, 10.0 us)
Async XLA Ops:
  2.2 7.7 %collective-permute-start.4 = (bf16[272,256]{1,0:T(8,128)(2,1)S(1)}, bf16[272,256]{1,0:T(8,128)(2,1)S(1)}, u32[]{:S(2)}, u32[]{:S(2)}) collective-permute-start(bf16[272,256]{1,0:T(8,128)(2,1)S(1)} %get-tuple-element.97), channel_id=1, source_target_pairs={{0,16},{1,17},{2,18},{3,19},{4,20},{5,21},{6,22},{7,23},{8,24},{9,... | collective-permute-start | bytes 417800 | tf_op jit(solution)/shard_map/ppermute | solution.py:256
  3.5 7.4 %collective-permute-start.1 = (bf16[272,256]{1,0:T(8,128)(2,1)S(1)}, bf16[272,256]{1,0:T(8,128)(2,1)S(1)}, u32[]{:S(2)}, u32[]{:S(2)}) collective-permute-start(bf16[272,256]{1,0:T(8,128)(2,1)S(1)} %get-tuple-element.98), channel_id=1, source_target_pairs={{0,20},{1,21},{2,22},{3,23},{4,16},{5,17},{6,18},{7,19},{8,28},{9,... | collective-permute-start | bytes 417800 | tf_op jit(solution)/shard_map/ppermute | solution.py:256
  4.6 6.4 %collective-permute-start.3 = (bf16[272,256]{1,0:T(8,128)(2,1)S(1)}, bf16[272,256]{1,0:T(8,128)(2,1)S(1)}, u32[]{:S(2)}, u32[]{:S(2)}) collective-permute-start(bf16[272,256]{1,0:T(8,128)(2,1)S(1)} %get-tuple-element.99), channel_id=1, source_target_pairs={{0,8},{1,9},{2,10},{3,11},{4,12},{5,13},{6,14},{7,15},{8,0},{9,1},... | collective-permute-start | bytes 417800 | tf_op jit(solution)/shard_map/ppermute | solution.py:256
  5.8 7.2 %collective-permute-start = (bf16[272,256]{1,0:T(8,128)(2,1)S(1)}, bf16[272,256]{1,0:T(8,128)(2,1)S(1)}, u32[]{:S(2)}, u32[]{:S(2)}) collective-permute-start(bf16[272,256]{1,0:T(8,128)(2,1)S(1)} %get-tuple-element.100), channel_id=1, source_target_pairs={{0,12},{1,13},{2,14},{3,15},{4,8},{5,9},{6,10},{7,11},{8,4},{9,5},... | collective-permute-start | bytes 417800 | tf_op jit(solution)/shard_map/ppermute | solution.py:256
  6.1 6.9 %collective-permute-start.2 = (bf16[528,256]{1,0:T(8,128)(2,1)S(1)}, bf16[528,256]{1,0:T(8,128)(2,1)S(1)}, u32[]{:S(2)}, u32[]{:S(2)}) collective-permute-start(bf16[528,256]{1,0:T(8,128)(2,1)S(1)} %pad_maximum_fusion.9), channel_id=1, source_target_pairs={{0,4},{1,5},{2,6},{3,7},{4,0},{5,1},{6,2},{7,3},{8,12},{9,13},{10,... | collective-permute-start | bytes 811016 | tf_op jit(solution)/shard_map/ppermute | solution.py:256
  13.1 14.7 %copy-start.1 = (bf16[1024,256]{1,0:T(8,128)(2,1)}, bf16[1024,256]{1,0:T(8,128)(2,1)S(1)}, u32[]{:S(2)}) copy-start(bf16[1024,256]{1,0:T(8,128)(2,1)S(1)} %pad_maximum_fusion.4.refs_8_.refs_10_) | copy-start | bytes 1572868
  13.2 13.2 %collective-permute-start.7 = (bf16[1024,256]{1,0:T(8,128)(2,1)S(1)}, bf16[1024,256]{1,0:T(8,128)(2,1)S(1)}, u32[]{:S(2)}, u32[]{:S(2)}) collective-permute-start(bf16[1024,256]{1,0:T(8,128)(2,1)S(1)} %pad_maximum_fusion.3.refs_2_.refs_4_), channel_id=1, source_target_pairs={{0,16},{1,17},{2,18},{3,19},{4,20},{5,21},{6,22},{7,23},{8,24},{9,... | collective-permute-start | bytes 1572872 | tf_op jit(solution)/shard_map/ppermute | solution.py:256
  14.8 44.5 %collective-permute-start.6 = (bf16[2048,256]{1,0:T(8,128)(2,1)S(1)}, bf16[2048,256]{1,0:T(8,128)(2,1)S(1)}, u32[]{:S(2)}, u32[]{:S(2)}) collective-permute-start(bf16[2048,256]{1,0:T(8,128)(2,1)S(1)} %constant_dynamic-update-slice_fusion), channel_id=1, source_target_pairs={{0,2},{1,3},{2,0},{3,1},{4,6},{5,7},{6,4},{7,5},{8,10},{9,11},{10,... | collective-permute-start | bytes 3145736 | tf_op jit(solution)/shard_map/ppermute | solution.py:261
  14.9 46.4 %collective-permute-start.5 = (bf16[2048,256]{1,0:T(8,128)(2,1)S(1)}, bf16[2048,256]{1,0:T(8,128)(2,1)S(1)}, u32[]{:S(2)}, u32[]{:S(2)}) collective-permute-start(bf16[2048,256]{1,0:T(8,128)(2,1)S(1)} %constant_dynamic-update-slice_fusion), channel_id=1, source_target_pairs={{0,1},{1,0},{2,3},{3,2},{4,5},{5,4},{6,7},{7,6},{8,9},{9,8},{10,11... | collective-permute-start | bytes 3145736 | tf_op jit(solution)/shard_map/ppermute | solution.py:261
  16.5 44.8 %collective-permute-start.9 = (bf16[256,2048]{1,0:T(8,128)(2,1)S(1)}, bf16[256,2048]{1,0:T(8,128)(2,1)S(1)}, u32[]{:S(2)}, u32[]{:S(2)}) collective-permute-start(bf16[256,2048]{1,0:T(8,128)(2,1)S(1)} %get-tuple-element.71), channel_id=1, source_target_pairs={{0,8},{1,9},{2,10},{3,11},{4,12},{5,13},{6,14},{7,15},{8,0},{9,1},... | collective-permute-start | bytes 3145736 | tf_op jit(solution)/shard_map/ppermute | solution.py:256
  26.4 40.3 %copy-start.11 = (bf16[1024,256]{1,0:T(8,128)(2,1)}, bf16[1024,256]{1,0:T(8,128)(2,1)S(1)}, u32[]{:S(2)}) copy-start(bf16[1024,256]{1,0:T(8,128)(2,1)S(1)} %collective-permute-done.7.refs_3_.refs_5_) | copy-start | bytes 1572868
  26.4 35.0 %collective-permute-start.10 = (bf16[256,2048]{1,0:T(8,128)(2,1)S(1)}, bf16[256,2048]{1,0:T(8,128)(2,1)S(1)}, u32[]{:S(2)}, u32[]{:S(2)}) collective-permute-start(bf16[256,2048]{1,0:T(8,128)(2,1)S(1)} %get-tuple-element.38), channel_id=1, source_target_pairs={{0,16},{1,17},{2,18},{3,19},{4,20},{5,21},{6,22},{7,23},{8,24},{9,... | collective-permute-start | bytes 3145736 | tf_op jit(solution)/shard_map/ppermute | solution.py:256
  27.8 23.4 %collective-permute-start.8 = (bf16[1024,256]{1,0:T(8,128)(2,1)S(1)}, bf16[1024,256]{1,0:T(8,128)(2,1)S(1)}, u32[]{:S(2)}, u32[]{:S(2)}) collective-permute-start(bf16[1024,256]{1,0:T(8,128)(2,1)S(1)} %pad_maximum_fusion.4.refs_8_.refs_10_), channel_id=1, source_target_pairs={{0,8},{1,9},{2,10},{3,11},{4,12},{5,13},{6,14},{7,15},{8,0},{9,1},... | collective-permute-start | bytes 1572872 | tf_op jit(solution)/shard_map/ppermute | solution.py:256
  51.2 15.4 %copy-start.12 = (bf16[1024,256]{1,0:T(8,128)(2,1)}, bf16[1024,256]{1,0:T(8,128)(2,1)S(1)}, u32[]{:S(2)}) copy-start(bf16[1024,256]{1,0:T(8,128)(2,1)S(1)} %collective-permute-done.8.refs_9_.refs_11_) | copy-start | bytes 1572868
  61.3 9.1 %copy-start.7 = (bf16[256,2048]{1,0:T(8,128)(2,1)}, bf16[256,2048]{1,0:T(8,128)(2,1)S(1)}, u32[]{:S(2)}) copy-start(bf16[256,2048]{1,0:T(8,128)(2,1)S(1)} %collective-permute-done.9.refs_0_) | copy-start | bytes 3145732
  61.4 9.2 %copy-start.8 = (bf16[256,2048]{1,0:T(8,128)(2,1)}, bf16[256,2048]{1,0:T(8,128)(2,1)S(1)}, u32[]{:S(2)}) copy-start(bf16[256,2048]{1,0:T(8,128)(2,1)S(1)} %collective-permute-done.10.refs_1_) | copy-start | bytes 3145732
  61.4 32.0 %collective-permute-start.11 = (bf16[2048,256]{1,0:T(8,128)(2,1)S(1)}, bf16[2048,256]{1,0:T(8,128)(2,1)S(1)}, u32[]{:S(2)}, u32[]{:S(2)}) collective-permute-start(bf16[2048,256]{1,0:T(8,128)(2,1)S(1)} %collective-permute-done.6), channel_id=1, source_target_pairs={{1,0},{2,3},{5,4},{6,7},{9,8},{10,11},{13,12},{14,15},{17,16},{18,... | collective-permute-start | bytes 3145736 | tf_op jit(solution)/shard_map/ppermute | solution.py:261
  66.8 3.7 %copy-start.3 = (bf16[2048,256]{1,0:T(8,128)(2,1)}, bf16[2048,256]{1,0:T(8,128)(2,1)S(1)}, u32[]{:S(2)}) copy-start(bf16[2048,256]{1,0:T(8,128)(2,1)S(1)} %pad_maximum_fusion.1.refs_4_.refs_6_) | copy-start | bytes 3145732
  66.8 24.0 %collective-permute-start.13 = (bf16[2048,256]{1,0:T(8,128)(2,1)S(1)}, bf16[2048,256]{1,0:T(8,128)(2,1)S(1)}, u32[]{:S(2)}, u32[]{:S(2)}) collective-permute-start(bf16[2048,256]{1,0:T(8,128)(2,1)S(1)} %pad_maximum_fusion.1.refs_4_.refs_6_), channel_id=1, source_target_pairs={{0,16},{1,17},{2,18},{3,19},{4,20},{5,21},{6,22},{7,23},{8,24},{9,... | collective-permute-start | bytes 3145736 | tf_op jit(solution)/shard_map/ppermute | solution.py:256
  66.9 23.8 %collective-permute-start.14 = (bf16[2048,256]{1,0:T(8,128)(2,1)S(1)}, bf16[2048,256]{1,0:T(8,128)(2,1)S(1)}, u32[]{:S(2)}, u32[]{:S(2)}) collective-permute-start(bf16[2048,256]{1,0:T(8,128)(2,1)S(1)} %pad_maximum_fusion.2.refs_10_.refs_12_), channel_id=1, source_target_pairs={{0,8},{1,9},{2,10},{3,11},{4,12},{5,13},{6,14},{7,15},{8,0},{9,1},... | collective-permute-start | bytes 3145736 | tf_op jit(solution)/shard_map/ppermute | solution.py:256
  68.2 25.2 %collective-permute-start.12 = (bf16[2048,256]{1,0:T(8,128)(2,1)S(1)}, bf16[2048,256]{1,0:T(8,128)(2,1)S(1)}, u32[]{:S(2)}, u32[]{:S(2)}) collective-permute-start(bf16[2048,256]{1,0:T(8,128)(2,1)S(1)} %constant_dynamic-update-slice_fusion), channel_id=1, source_target_pairs={{1,2},{2,1},{5,6},{6,5},{9,10},{10,9},{13,14},{14,13},{17,18},{18,... | collective-permute-start | bytes 3145736 | tf_op jit(solution)/shard_map/ppermute | solution.py:261
  90.8 5.0 %copy-start.10 = (bf16[2048,256]{1,0:T(8,128)(2,1)}, bf16[2048,256]{1,0:T(8,128)(2,1)S(1)}, u32[]{:S(2)}) copy-start(bf16[2048,256]{1,0:T(8,128)(2,1)S(1)} %collective-permute-done.14.refs_11_.refs_13_) | copy-start | bytes 3145732
  93.5 16.8 %collective-permute-start.15 = (bf16[256,4096]{1,0:T(8,128)(2,1)}, bf16[256,4096]{1,0:T(8,128)(2,1)}, u32[]{:S(2)}, u32[]{:S(2)}) collective-permute-start(bf16[256,4096]{1,0:T(8,128)(2,1)} %pad_maximum_fusion), channel_id=1, source_target_pairs={{0,4},{1,5},{2,6},{3,7},{4,0},{5,1},{6,2},{7,3},{8,12},{9,13},{10,... | collective-permute-start | bytes 6291464 | tf_op jit(solution)/shard_map/ppermute | solution.py:256
  96.6 13.6 %copy-start.5 = (bf16[1024,256]{1,0:T(8,128)(2,1)}, bf16[1024,256]{1,0:T(8,128)(2,1)S(1)}, u32[]{:S(2)}) copy-start(bf16[1024,256]{1,0:T(8,128)(2,1)S(1)} %get-tuple-element.73.refs_12_.refs_14_) | copy-start | bytes 1572868
  96.6 13.6 %copy-start.6 = (bf16[1024,256]{1,0:T(8,128)(2,1)}, bf16[1024,256]{1,0:T(8,128)(2,1)S(1)}, u32[]{:S(2)}) copy-start(bf16[1024,256]{1,0:T(8,128)(2,1)S(1)} %get-tuple-element.74.refs_6_.refs_8_) | copy-start | bytes 1572868
  96.7 13.6 %collective-permute-start.17 = (bf16[1024,256]{1,0:T(8,128)(2,1)S(1)}, bf16[1024,256]{1,0:T(8,128)(2,1)S(1)}, u32[]{:S(2)}, u32[]{:S(2)}) collective-permute-start(bf16[1024,256]{1,0:T(8,128)(2,1)S(1)} %get-tuple-element.73.refs_12_.refs_14_), channel_id=1, source_target_pairs={{0,8},{1,9},{2,10},{3,11},{4,12},{5,13},{6,14},{7,15},{8,0},{9,1},... | collective-permute-start | bytes 1572872 | tf_op jit(solution)/shard_map/ppermute | solution.py:256
  97.0 13.3 %collective-permute-start.16 = (bf16[1024,256]{1,0:T(8,128)(2,1)S(1)}, bf16[1024,256]{1,0:T(8,128)(2,1)S(1)}, u32[]{:S(2)}, u32[]{:S(2)}) collective-permute-start(bf16[1024,256]{1,0:T(8,128)(2,1)S(1)} %get-tuple-element.74.refs_6_.refs_8_), channel_id=1, source_target_pairs={{0,16},{1,17},{2,18},{3,19},{4,20},{5,21},{6,22},{7,23},{8,24},{9,... | collective-permute-start | bytes 1572872 | tf_op jit(solution)/shard_map/ppermute | solution.py:256
  120.2 21.5 %collective-permute-start.21 = (bf16[256,1024]{1,0:T(8,128)(2,1)}, bf16[256,1024]{1,0:T(8,128)(2,1)S(1)}, u32[]{:S(2)}, u32[]{:S(2)}) collective-permute-start(bf16[256,1024]{1,0:T(8,128)(2,1)} %get-tuple-element.60), channel_id=1, source_target_pairs={{0,12},{1,13},{2,14},{3,15},{4,8},{5,9},{6,10},{7,11},{8,4},{9,5},... | collective-permute-start | bytes 1572872 | tf_op jit(solution)/shard_map/ppermute | solution.py:256
  122.3 19.5 %collective-permute-start.22 = (bf16[256,1024]{1,0:T(8,128)(2,1)}, bf16[256,1024]{1,0:T(8,128)(2,1)S(1)}, u32[]{:S(2)}, u32[]{:S(2)}) collective-permute-start(bf16[256,1024]{1,0:T(8,128)(2,1)} %get-tuple-element.61), channel_id=1, source_target_pairs={{0,20},{1,21},{2,22},{3,23},{4,16},{5,17},{6,18},{7,19},{8,28},{9,... | collective-permute-start | bytes 1572872 | tf_op jit(solution)/shard_map/ppermute | solution.py:256
  140.6 13.8 %collective-permute-start.18 = (bf16[256,1024]{1,0:T(8,128)(2,1)}, bf16[256,1024]{1,0:T(8,128)(2,1)S(1)}, u32[]{:S(2)}, u32[]{:S(2)}) collective-permute-start(bf16[256,1024]{1,0:T(8,128)(2,1)} %get-tuple-element.56), channel_id=1, source_target_pairs={{0,8},{1,9},{2,10},{3,11},{4,12},{5,13},{6,14},{7,15},{8,0},{9,1},... | collective-permute-start | bytes 1572872 | tf_op jit(solution)/shard_map/ppermute | solution.py:256
  140.6 13.7 %collective-permute-start.19 = (bf16[256,1024]{1,0:T(8,128)(2,1)}, bf16[256,1024]{1,0:T(8,128)(2,1)S(1)}, u32[]{:S(2)}, u32[]{:S(2)}) collective-permute-start(bf16[256,1024]{1,0:T(8,128)(2,1)} %get-tuple-element.57), channel_id=1, source_target_pairs={{0,16},{1,17},{2,18},{3,19},{4,20},{5,21},{6,22},{7,23},{8,24},{9,... | collective-permute-start | bytes 1572872 | tf_op jit(solution)/shard_map/ppermute | solution.py:256
  140.7 13.6 %collective-permute-start.20 = (bf16[512,1024]{1,0:T(8,128)(2,1)}, bf16[512,1024]{1,0:T(8,128)(2,1)S(1)}, u32[]{:S(2)}, u32[]{:S(2)}) collective-permute-start(bf16[512,1024]{1,0:T(8,128)(2,1)} %get-tuple-element.58), channel_id=1, source_target_pairs={{0,4},{1,5},{2,6},{3,7},{4,0},{5,1},{6,2},{7,3},{8,12},{9,13},{10,... | collective-permute-start | bytes 3145736 | tf_op jit(solution)/shard_map/ppermute | solution.py:256
  (8 other events, 16.5 us)

commit v6 on v5

--- a/solution.py
+++ b/solution.py
@@ -389,12 +389,12 @@
 
     diagonal = [(half, sides[half] + 1) for half in halves]
     straight, beside = [(half, sides[half]) for half in halves], [(half, 1) for half in halves]
-    *outs, turn = attend(jnp.zeros((1,), jnp.int32), tiles, *operands(diagonal))
-    *more, turn = attend(turn, tiles, *operands(straight + beside), shared=len(beside))
-    sent = diagonal + straight + beside
+    *outs, turn = attend(jnp.zeros((1,), jnp.int32), tiles, *operands(straight))
+    *more, turn = attend(turn, tiles, *operands(diagonal + beside), shared=len(beside))
+    sent = straight + diagonal + beside
     arrays = [swap(out, offset) for out, (_, offset) in zip(outs + more, sent)]
     columns = [head_of(half, offset) * WIDE for half, offset in sent]
-    early = len(diagonal)
+    early = len(straight)
     result, _ = attend(
         turn, tiles, *operands([(half, 0) for half in halves]), [head_of(half, 0) * WIDE for half in halves],
         pieces=list(zip(arrays, columns))[:early],

time: 157 us -> 153 us (0.975)
  waiting for transfers between devices: 77.7 us -> 60.3 us
  local copies, waits for them, and re-layouts: 6.69 us -> 13.4 us
  starting transfers between devices: 27.9 us -> 32.8 us
    ppermute x19, waiting for transfers between devices: 64.9 us -> 37.6 us  [swap(): lax.ppermute(x, AXES, [(i * z_size + h, (i ^ offset) * z_size + h) for i...]
    ppermute x4, waiting for transfers between devices: 12.8 us -> 22.8 us  [along(): lax.ppermute(x, AXES, [(i * z_size + h, i * z_size + k) for i in range(pl...]
    ppermute x19, starting transfers between devices: 19.2 us -> 26.7 us  [swap(): lax.ppermute(x, AXES, [(i * z_size + h, (i ^ offset) * z_size + h) for i...]
    dynamic_slice x4, local copies, waits for them, and re-layouts: 0.41 us -> 3.57 us  [heads(): return lax.dynamic_slice_in_dim(array, at, count * WIDE, axis=1)]
    ppermute x4, starting transfers between devices: 8.67 us -> 6.09 us  [along(): lax.ppermute(x, AXES, [(i * z_size + h, i * z_size + k) for i in range(pl...]
    slice x2, local copies, waits for them, and re-layouts: 0.14 us -> 2.54 us  [per_device(): pair_b = jnp.concatenate([one[rows:], two[rows:]], axis=0)]
  transfers between devices with their start and end apart: 23 -> 23, of which waited for: 10 -> 12; matrix products, arithmetic and copies ran while one was open for 5% -> 10% of each run, Pallas kernels for 18% -> 24%
where the time goes in v6:
time: 153 us; the launch traced here: 151 us
  waiting for transfers between devices  60.3 us (39%)
  Pallas kernels  38.7 us (25%)
  starting transfers between devices  32.8 us (21%)
  local copies, waits for them, and re-layouts  13.4 us (9%)
  other arithmetic  5.67 us (4%)
    ppermute x19, waiting for transfers between devices, swap(): lax.ppermute(x, AXES, [(i * z_size + h, (i ^ offset) * z_size + h) for i...  37.6 us
    pallas_call x3, Pallas kernels, attend(): pl.pallas_call(functools.partial(attend_kernel, blocks, tiles, starts, di...  36.8 us
    ppermute x19, starting transfers between devices, swap(): lax.ppermute(x, AXES, [(i * z_size + h, (i ^ offset) * z_size + h) for i...  26.7 us
    ppermute x4, waiting for transfers between devices, along(): lax.ppermute(x, AXES, [(i * z_size + h, i * z_size + k) for i in range(pl...  22.8 us
    ppermute x4, starting transfers between devices, along(): lax.ppermute(x, AXES, [(i * z_size + h, i * z_size + k) for i in range(pl...  6.09 us
    dynamic_slice x4, local copies, waits for them, and re-layouts, heads(): return lax.dynamic_slice_in_dim(array, at, count * WIDE, axis=1)  3.57 us
  transfers between devices with their start and end apart: 23, of which 12 were waited for; matrix products, arithmetic and copies ran while one was open for 10% of the time, Pallas kernels for 24%

profile of v6, /device:TPU:17, one launch (start us, length us, event | category | flops | bytes accessed | tf_op | source)
XLA Modules:
  0.0 151.4 jit_solution(2854891341538481533)
XLA Ops:
  0.8 1.4 constant_dynamic-slice_fusion.8
  2.2 1.3 collective-permute-start.1
  3.5 1.2 collective-permute-start
  4.7 1.4 collective-permute-start.3
  14.3 1.3 collective-permute-start.5
  15.8 1.3 collective-permute-start.9
  17.0 8.6 %collective-permute-done.7.refs_3_.refs_5_ = bf16[1024,256]{1,0:T(8,128)(2,1)S(1)} collective-permute-done((bf16[1024,256]{1,0:T(8,128)(2,1)S(1)}, bf16[1024,256]{1,0:T(8,128)(2,1)S(1)}, u32[]{:S(2)}, u32[]{:S(2)}) %collective-permute-start.7) | collective-permute-done | bytes 524320 | tf_op jit(solution)/shard_map/ppermute | solution.py:256
  26.7 1.3 collective-permute-start.8
  29.3 21.4 %collective-permute-done.8.refs_9_.refs_11_ = bf16[1024,256]{1,0:T(8,128)(2,1)} collective-permute-done((bf16[1024,256]{1,0:T(8,128)(2,1)S(1)}, bf16[1024,256]{1,0:T(8,128)(2,1)}, u32[]{:S(2)}, u32[]{:S(2)}) %collective-permute-start.8) | collective-permute-done | bytes 524320 | tf_op jit(solution)/shard_map/ppermute | solution.py:256
  50.7 8.3 %collective-permute-done.5 = bf16[2048,256]{1,0:T(8,128)(2,1)} collective-permute-done((bf16[2048,256]{1,0:T(8,128)(2,1)}, bf16[2048,256]{1,0:T(8,128)(2,1)}, u32[]{:S(2)}, u32[]{:S(2)}) %collective-permute-start.5) | collective-permute-done | bytes 1048608 | tf_op jit(solution)/shard_map/ppermute | solution.py:261
  59.0 2.1 %collective-permute-done.6 = bf16[2048,256]{1,0:T(8,128)(2,1)} collective-permute-done((bf16[2048,256]{1,0:T(8,128)(2,1)}, bf16[2048,256]{1,0:T(8,128)(2,1)}, u32[]{:S(2)}, u32[]{:S(2)}) %collective-permute-start.6) | collective-permute-done | bytes 1048608 | tf_op jit(solution)/shard_map/ppermute | solution.py:261
  61.1 2.1 %collective-permute-start.11 = (bf16[2048,256]{1,0:T(8,128)(2,1)}, bf16[2048,256]{1,0:T(8,128)(2,1)S(1)}, u32[]{:S(2)}, u32[]{:S(2)}) collective-permute-start(bf16[2048,256]{1,0:T(8,128)(2,1)} %collective-permute-done.6), channel_id=1, source_target_pairs={{1,0},{2,3},{5,4},{6,7},{9,8},{10,11},{13,12},{14,15},{17,16},{18,... | collective-permute-start | bytes 3145736 | tf_op jit(solution)/shard_map/ppermute | solution.py:261
  63.2 1.3 fusion.33
  64.5 2.6 %collective-permute-start.12 = (bf16[2048,256]{1,0:T(8,128)(2,1)}, bf16[2048,256]{1,0:T(8,128)(2,1)S(1)}, u32[]{:S(2)}, u32[]{:S(2)}) collective-permute-start(bf16[2048,256]{1,0:T(8,128)(2,1)} %constant_dynamic-update-slice_fusion), channel_id=1, source_target_pairs={{1,2},{2,1},{5,6},{6,5},{9,10},{10,9},{13,14},{14,13},{17,18},{18,... | collective-permute-start | bytes 3145736 | tf_op jit(solution)/shard_map/ppermute | solution.py:261
  67.1 1.3 fusion.32
  68.5 1.3 collective-permute-start.13
  69.9 1.3 collective-permute-start.14
  71.1 1.3 constant_dynamic-slice_fusion.3
  74.8 7.3 %collective-permute-done.11 = bf16[2048,256]{1,0:T(8,128)(2,1)S(1)} collective-permute-done((bf16[2048,256]{1,0:T(8,128)(2,1)}, bf16[2048,256]{1,0:T(8,128)(2,1)S(1)}, u32[]{:S(2)}, u32[]{:S(2)}) %collective-permute-start.11) | collective-permute-done | bytes 1048608 | tf_op jit(solution)/shard_map/ppermute | solution.py:261
  82.1 5.1 %collective-permute-done.12 = bf16[2048,256]{1,0:T(8,128)(2,1)S(1)} collective-permute-done((bf16[2048,256]{1,0:T(8,128)(2,1)}, bf16[2048,256]{1,0:T(8,128)(2,1)S(1)}, u32[]{:S(2)}, u32[]{:S(2)}) %collective-permute-start.12) | collective-permute-done | bytes 1048608 | tf_op jit(solution)/shard_map/ppermute | solution.py:261
  87.1 2.0 %collective-permute-done.13.refs_5_.refs_7_ = bf16[2048,256]{1,0:T(8,128)(2,1)S(1)} collective-permute-done((bf16[2048,256]{1,0:T(8,128)(2,1)S(1)}, bf16[2048,256]{1,0:T(8,128)(2,1)S(1)}, u32[]{:S(2)}, u32[]{:S(2)}) %collective-permute-start.13) | collective-permute-done | bytes 1048608 | tf_op jit(solution)/shard_map/ppermute | solution.py:256
  89.2 1.1 collective-permute-done.14.refs_11_.refs_13_
  91.8 1.2 collective-permute-start.16
  93.7 5.9 %collective-permute-start.17 = (bf16[256,4096]{1,0:T(8,128)(2,1)S(1)}, bf16[256,4096]{1,0:T(8,128)(2,1)}, u32[]{:S(2)}, u32[]{:S(2)}) collective-permute-start(bf16[256,4096]{1,0:T(8,128)(2,1)S(1)} %pad_maximum_fusion), channel_id=1, source_target_pairs={{0,4},{1,5},{2,6},{3,7},{4,0},{5,1},{6,2},{7,3},{8,12},{9,13},{10,... | collective-permute-start | bytes 6291464 | tf_op jit(solution)/shard_map/ppermute | solution.py:256
  99.6 1.3 collective-permute-done.16.refs_13_.refs_15_
  100.9 9.0 %shard_map.46 = (bf16[256,1024]{1,0:T(8,128)(2,1)}, bf16[256,1024]{1,0:T(8,128)(2,1)}, s32[1]{0:T(128)}) custom-call(s32[1]{0:T(128)} %constant.383.clone.1.turn_ref, s32[32]{0:T(128)} %reshape.9.loc_ref, s32[4]{0:T(128)} %pad_add_fusion.4.tid_ref, s32[2]{0:T(128)} %pad_add_fusion.5.col_ref, bf16[256,2048]{1,0:T(8,128)(2,1)} %collective-permute-done.9.refs_0_, ...), custom_call_target="tpu_custom_call" | custom-call | flops 40000000000 | bytes 1000000 | tf_op jit(solution)/shard_map/pallas_call | solution.py:194
  109.9 1.3 collective-permute-start.21
  111.5 17.6 %shard_map.47 = (bf16[256,1024]{1,0:T(8,128)(2,1)}, bf16[256,1024]{1,0:T(8,128)(2,1)}, bf16[512,1024]{1,0:T(8,128)(2,1)}, s32[1]{0:T(128)}) custom-call(s32[1]{0:T(128)} %get-tuple-element.54.turn_ref, s32[64]{0:T(128)} %reshape.10.loc_ref, s32[8]{0:T(128)} %pad_add_fusion.6.tid_ref, s32[4]{0:T(128)} %constant.394.clone.1.col_ref, ...), custom_call_target="tpu_custom_call" | custom-call | flops 80000000000 | bytes 1000000 | tf_op jit(solution)/shard_map/pallas_call | solution.py:194
  129.1 7.1 %collective-permute-start.18 = (bf16[256,1024]{1,0:T(8,128)(2,1)}, bf16[256,1024]{1,0:T(8,128)(2,1)S(1)}, u32[]{:S(2)}, u32[]{:S(2)}) collective-permute-start(bf16[256,1024]{1,0:T(8,128)(2,1)} %get-tuple-element.56), channel_id=1, source_target_pairs={{0,12},{1,13},{2,14},{3,15},{4,8},{5,9},{6,10},{7,11},{8,4},{9,5},... | collective-permute-start | bytes 1572872 | tf_op jit(solution)/shard_map/ppermute | solution.py:256
  137.2 10.2 %shard_map.48 = (bf16[256,8192]{1,0:T(8,128)(2,1)}, s32[1]{0:T(128)}) custom-call(s32[1]{0:T(128)} %get-tuple-element.59.turn_ref, s32[32]{0:T(128)} %reshape.11.loc_ref, s32[4]{0:T(128)} %pad_add_fusion.7.tid_ref, s32[6]{0:T(128)} %stack.50.col_ref, bf16[256,8192]{1,0:T(8,128)(2,1)} %refs_1_, bf16[256,8192]{1,0:T(8,128)(2,1)} %refs_1_, ...), custom_call_target="tpu_custom_call" | custom-call | flops 40000000000 | bytes 1000000 | tf_op jit(solution)/shard_map/pallas_call | solution.py:194
  147.4 1.5 collective-permute-done.18.refs_0_
  149.4 1.9 %shard_map.49 = bf16[256,8192]{1,0:T(8,128)(2,1)} custom-call(s32[4]{0:T(128)S(1)} %pad_add_fusion.3.col_ref, bf16[256,1024]{1,0:T(8,128)(2,1)S(1)} %collective-permute-done.18.refs_0_, bf16[256,1024]{1,0:T(8,128)(2,1)S(1)} %collective-permute-done.19.refs_1_, bf16[512,1024]{1,0:T(8,128)(2,1)S(1)} %collective-permute-done.20.refs_2_, ...), custom_call_target="tpu_custom_call", output_to_operand_aliasing={{}: (4, {})} | custom-call | tf_op jit(solution)/shard_map/pallas_call | solution.py:234
  (99 shorter events, 17.7 us)
Async XLA Ops:
  2.2 8.7 %collective-permute-start.1 = (bf16[272,256]{1,0:T(8,128)(2,1)S(1)}, bf16[272,256]{1,0:T(8,128)(2,1)S(1)}, u32[]{:S(2)}, u32[]{:S(2)}) collective-permute-start(bf16[272,256]{1,0:T(8,128)(2,1)S(1)} %get-tuple-element.98), channel_id=1, source_target_pairs={{0,16},{1,17},{2,18},{3,19},{4,20},{5,21},{6,22},{7,23},{8,24},{9,... | collective-permute-start | bytes 417800 | tf_op jit(solution)/shard_map/ppermute | solution.py:256
  3.5 8.5 %collective-permute-start = (bf16[272,256]{1,0:T(8,128)(2,1)S(1)}, bf16[272,256]{1,0:T(8,128)(2,1)S(1)}, u32[]{:S(2)}, u32[]{:S(2)}) collective-permute-start(bf16[272,256]{1,0:T(8,128)(2,1)S(1)} %get-tuple-element.100), channel_id=1, source_target_pairs={{0,8},{1,9},{2,10},{3,11},{4,12},{5,13},{6,14},{7,15},{8,0},{9,1},... | collective-permute-start | bytes 417800 | tf_op jit(solution)/shard_map/ppermute | solution.py:256
  4.7 7.3 %collective-permute-start.3 = (bf16[272,256]{1,0:T(8,128)(2,1)S(1)}, bf16[272,256]{1,0:T(8,128)(2,1)S(1)}, u32[]{:S(2)}, u32[]{:S(2)}) collective-permute-start(bf16[272,256]{1,0:T(8,128)(2,1)S(1)} %get-tuple-element.99), channel_id=1, source_target_pairs={{0,12},{1,13},{2,14},{3,15},{4,8},{5,9},{6,10},{7,11},{8,4},{9,5},... | collective-permute-start | bytes 417800 | tf_op jit(solution)/shard_map/ppermute | solution.py:256
  6.1 6.0 %collective-permute-start.2 = (bf16[528,256]{1,0:T(8,128)(2,1)S(1)}, bf16[528,256]{1,0:T(8,128)(2,1)S(1)}, u32[]{:S(2)}, u32[]{:S(2)}) collective-permute-start(bf16[528,256]{1,0:T(8,128)(2,1)S(1)} %pad_maximum_fusion.9), channel_id=1, source_target_pairs={{0,4},{1,5},{2,6},{3,7},{4,0},{5,1},{6,2},{7,3},{8,12},{9,13},{10,... | collective-permute-start | bytes 811016 | tf_op jit(solution)/shard_map/ppermute | solution.py:256
  6.2 5.9 %collective-permute-start.4 = (bf16[272,256]{1,0:T(8,128)(2,1)S(1)}, bf16[272,256]{1,0:T(8,128)(2,1)S(1)}, u32[]{:S(2)}, u32[]{:S(2)}) collective-permute-start(bf16[272,256]{1,0:T(8,128)(2,1)S(1)} %get-tuple-element.97), channel_id=1, source_target_pairs={{0,20},{1,21},{2,22},{3,23},{4,16},{5,17},{6,18},{7,19},{8,28},{9,... | collective-permute-start | bytes 417800 | tf_op jit(solution)/shard_map/ppermute | solution.py:256
  12.1 2.2 %copy-start.8 = (bf16[272,256]{1,0:T(8,128)(2,1)}, bf16[272,256]{1,0:T(8,128)(2,1)S(1)}, u32[]{:S(2)}) copy-start(bf16[272,256]{1,0:T(8,128)(2,1)S(1)} %collective-permute-done.4) | copy-start | bytes 417796
  12.2 3.4 %copy-start = (bf16[256,8192]{1,0:T(8,128)(2,1)S(1)}, bf16[256,8192]{1,0:T(8,128)(2,1)}, u32[]{:S(2)}) copy-start(bf16[256,8192]{1,0:T(8,128)(2,1)} %refs_1_) | copy-start | bytes 12582916
  12.2 3.5 %copy-start.1 = (bf16[1024,256]{1,0:T(8,128)(2,1)}, bf16[1024,256]{1,0:T(8,128)(2,1)S(1)}, u32[]{:S(2)}) copy-start(bf16[1024,256]{1,0:T(8,128)(2,1)S(1)} %pad_maximum_fusion.3.refs_2_.refs_4_) | copy-start | bytes 1572868
  12.3 14.4 %copy-start.2 = (bf16[1024,256]{1,0:T(8,128)(2,1)}, bf16[1024,256]{1,0:T(8,128)(2,1)S(1)}, u32[]{:S(2)}) copy-start(bf16[1024,256]{1,0:T(8,128)(2,1)S(1)} %pad_maximum_fusion.4.refs_8_.refs_10_) | copy-start | bytes 1572868
  12.3 13.4 %collective-permute-start.7 = (bf16[1024,256]{1,0:T(8,128)(2,1)S(1)}, bf16[1024,256]{1,0:T(8,128)(2,1)S(1)}, u32[]{:S(2)}, u32[]{:S(2)}) collective-permute-start(bf16[1024,256]{1,0:T(8,128)(2,1)S(1)} %pad_maximum_fusion.3.refs_2_.refs_4_), channel_id=1, source_target_pairs={{0,16},{1,17},{2,18},{3,19},{4,20},{5,21},{6,22},{7,23},{8,24},{9,... | collective-permute-start | bytes 1572872 | tf_op jit(solution)/shard_map/ppermute | solution.py:256
  14.3 44.7 %collective-permute-start.5 = (bf16[2048,256]{1,0:T(8,128)(2,1)}, bf16[2048,256]{1,0:T(8,128)(2,1)}, u32[]{:S(2)}, u32[]{:S(2)}) collective-permute-start(bf16[2048,256]{1,0:T(8,128)(2,1)} %constant_dynamic-update-slice_fusion), channel_id=1, source_target_pairs={{0,1},{1,0},{2,3},{3,2},{4,5},{5,4},{6,7},{7,6},{8,9},{9,8},{10,11... | collective-permute-start | bytes 3145736 | tf_op jit(solution)/shard_map/ppermute | solution.py:261
  15.6 45.5 %collective-permute-start.6 = (bf16[2048,256]{1,0:T(8,128)(2,1)}, bf16[2048,256]{1,0:T(8,128)(2,1)}, u32[]{:S(2)}, u32[]{:S(2)}) collective-permute-start(bf16[2048,256]{1,0:T(8,128)(2,1)} %constant_dynamic-update-slice_fusion), channel_id=1, source_target_pairs={{0,2},{1,3},{2,0},{3,1},{4,6},{5,7},{6,4},{7,5},{8,10},{9,11},{10,... | collective-permute-start | bytes 3145736 | tf_op jit(solution)/shard_map/ppermute | solution.py:261
  15.8 45.3 %collective-permute-start.9 = (bf16[256,2048]{1,0:T(8,128)(2,1)S(1)}, bf16[256,2048]{1,0:T(8,128)(2,1)}, u32[]{:S(2)}, u32[]{:S(2)}) collective-permute-start(bf16[256,2048]{1,0:T(8,128)(2,1)S(1)} %get-tuple-element.71), channel_id=1, source_target_pairs={{0,8},{1,9},{2,10},{3,11},{4,12},{5,13},{6,14},{7,15},{8,0},{9,1},... | collective-permute-start | bytes 3145736 | tf_op jit(solution)/shard_map/ppermute | solution.py:256
  25.7 2.3 %copy-start.11 = (bf16[1024,256]{1,0:T(8,128)(2,1)}, bf16[1024,256]{1,0:T(8,128)(2,1)S(1)}, u32[]{:S(2)}) copy-start(bf16[1024,256]{1,0:T(8,128)(2,1)S(1)} %collective-permute-done.7.refs_3_.refs_5_) | copy-start | bytes 1572868
  25.7 35.4 %collective-permute-start.10 = (bf16[256,2048]{1,0:T(8,128)(2,1)S(1)}, bf16[256,2048]{1,0:T(8,128)(2,1)}, u32[]{:S(2)}, u32[]{:S(2)}) collective-permute-start(bf16[256,2048]{1,0:T(8,128)(2,1)S(1)} %get-tuple-element.38), channel_id=1, source_target_pairs={{0,16},{1,17},{2,18},{3,19},{4,20},{5,21},{6,22},{7,23},{8,24},{9,... | collective-permute-start | bytes 3145736 | tf_op jit(solution)/shard_map/ppermute | solution.py:256
  26.7 24.0 %collective-permute-start.8 = (bf16[1024,256]{1,0:T(8,128)(2,1)S(1)}, bf16[1024,256]{1,0:T(8,128)(2,1)}, u32[]{:S(2)}, u32[]{:S(2)}) collective-permute-start(bf16[1024,256]{1,0:T(8,128)(2,1)S(1)} %pad_maximum_fusion.4.refs_8_.refs_10_), channel_id=1, source_target_pairs={{0,8},{1,9},{2,10},{3,11},{4,12},{5,13},{6,14},{7,15},{8,0},{9,1},... | collective-permute-start | bytes 1572872 | tf_op jit(solution)/shard_map/ppermute | solution.py:256
  61.1 21.0 %collective-permute-start.11 = (bf16[2048,256]{1,0:T(8,128)(2,1)}, bf16[2048,256]{1,0:T(8,128)(2,1)S(1)}, u32[]{:S(2)}, u32[]{:S(2)}) collective-permute-start(bf16[2048,256]{1,0:T(8,128)(2,1)} %collective-permute-done.6), channel_id=1, source_target_pairs={{1,0},{2,3},{5,4},{6,7},{9,8},{10,11},{13,12},{14,15},{17,16},{18,... | collective-permute-start | bytes 3145736 | tf_op jit(solution)/shard_map/ppermute | solution.py:261
  64.5 22.7 %collective-permute-start.12 = (bf16[2048,256]{1,0:T(8,128)(2,1)}, bf16[2048,256]{1,0:T(8,128)(2,1)S(1)}, u32[]{:S(2)}, u32[]{:S(2)}) collective-permute-start(bf16[2048,256]{1,0:T(8,128)(2,1)} %constant_dynamic-update-slice_fusion), channel_id=1, source_target_pairs={{1,2},{2,1},{5,6},{6,5},{9,10},{10,9},{13,14},{14,13},{17,18},{18,... | collective-permute-start | bytes 3145736 | tf_op jit(solution)/shard_map/ppermute | solution.py:261
  68.5 3.9 %copy-start.3 = (bf16[2048,256]{1,0:T(8,128)(2,1)}, bf16[2048,256]{1,0:T(8,128)(2,1)S(1)}, u32[]{:S(2)}) copy-start(bf16[2048,256]{1,0:T(8,128)(2,1)S(1)} %pad_maximum_fusion.1.refs_4_.refs_6_) | copy-start | bytes 3145732
  68.5 20.7 %collective-permute-start.13 = (bf16[2048,256]{1,0:T(8,128)(2,1)S(1)}, bf16[2048,256]{1,0:T(8,128)(2,1)S(1)}, u32[]{:S(2)}, u32[]{:S(2)}) collective-permute-start(bf16[2048,256]{1,0:T(8,128)(2,1)S(1)} %pad_maximum_fusion.1.refs_4_.refs_6_), channel_id=1, source_target_pairs={{0,16},{1,17},{2,18},{3,19},{4,20},{5,21},{6,22},{7,23},{8,24},{9,... | collective-permute-start | bytes 3145736 | tf_op jit(solution)/shard_map/ppermute | solution.py:256
  69.8 4.8 %copy-start.4 = (bf16[2048,256]{1,0:T(8,128)(2,1)}, bf16[2048,256]{1,0:T(8,128)(2,1)S(1)}, u32[]{:S(2)}) copy-start(bf16[2048,256]{1,0:T(8,128)(2,1)S(1)} %pad_maximum_fusion.2.refs_10_.refs_12_) | copy-start | bytes 3145732
  69.9 20.4 %collective-permute-start.14 = (bf16[2048,256]{1,0:T(8,128)(2,1)S(1)}, bf16[2048,256]{1,0:T(8,128)(2,1)S(1)}, u32[]{:S(2)}, u32[]{:S(2)}) collective-permute-start(bf16[2048,256]{1,0:T(8,128)(2,1)S(1)} %pad_maximum_fusion.2.refs_10_.refs_12_), channel_id=1, source_target_pairs={{0,8},{1,9},{2,10},{3,11},{4,12},{5,13},{6,14},{7,15},{8,0},{9,1},... | collective-permute-start | bytes 3145736 | tf_op jit(solution)/shard_map/ppermute | solution.py:256
  91.3 9.6 %copy-start.5 = (bf16[1024,256]{1,0:T(8,128)(2,1)}, bf16[1024,256]{1,0:T(8,128)(2,1)S(1)}, u32[]{:S(2)}) copy-start(bf16[1024,256]{1,0:T(8,128)(2,1)S(1)} %get-tuple-element.73.refs_12_.refs_14_) | copy-start | bytes 1572868
  91.3 9.7 %copy-start.6 = (bf16[1024,256]{1,0:T(8,128)(2,1)}, bf16[1024,256]{1,0:T(8,128)(2,1)S(1)}, u32[]{:S(2)}) copy-start(bf16[1024,256]{1,0:T(8,128)(2,1)S(1)} %get-tuple-element.74.refs_6_.refs_8_) | copy-start | bytes 1572868
  91.3 8.3 %collective-permute-start.15 = (bf16[1024,256]{1,0:T(8,128)(2,1)S(1)}, bf16[1024,256]{1,0:T(8,128)(2,1)}, u32[]{:S(2)}, u32[]{:S(2)}) collective-permute-start(bf16[1024,256]{1,0:T(8,128)(2,1)S(1)} %get-tuple-element.74.refs_6_.refs_8_), channel_id=1, source_target_pairs={{0,16},{1,17},{2,18},{3,19},{4,20},{5,21},{6,22},{7,23},{8,24},{9,... | collective-permute-start | bytes 1572872 | tf_op jit(solution)/shard_map/ppermute | solution.py:256
  91.8 9.1 %collective-permute-start.16 = (bf16[1024,256]{1,0:T(8,128)(2,1)S(1)}, bf16[1024,256]{1,0:T(8,128)(2,1)}, u32[]{:S(2)}, u32[]{:S(2)}) collective-permute-start(bf16[1024,256]{1,0:T(8,128)(2,1)S(1)} %get-tuple-element.73.refs_12_.refs_14_), channel_id=1, source_target_pairs={{0,8},{1,9},{2,10},{3,11},{4,12},{5,13},{6,14},{7,15},{8,0},{9,1},... | collective-permute-start | bytes 1572872 | tf_op jit(solution)/shard_map/ppermute | solution.py:256
  93.7 17.8 %collective-permute-start.17 = (bf16[256,4096]{1,0:T(8,128)(2,1)S(1)}, bf16[256,4096]{1,0:T(8,128)(2,1)}, u32[]{:S(2)}, u32[]{:S(2)}) collective-permute-start(bf16[256,4096]{1,0:T(8,128)(2,1)S(1)} %pad_maximum_fusion), channel_id=1, source_target_pairs={{0,4},{1,5},{2,6},{3,7},{4,0},{5,1},{6,2},{7,3},{8,12},{9,13},{10,... | collective-permute-start | bytes 6291464 | tf_op jit(solution)/shard_map/ppermute | solution.py:256
  109.9 26.5 %collective-permute-start.21 = (bf16[256,1024]{1,0:T(8,128)(2,1)}, bf16[256,1024]{1,0:T(8,128)(2,1)S(1)}, u32[]{:S(2)}, u32[]{:S(2)}) collective-permute-start(bf16[256,1024]{1,0:T(8,128)(2,1)} %get-tuple-element.60), channel_id=1, source_target_pairs={{0,8},{1,9},{2,10},{3,11},{4,12},{5,13},{6,14},{7,15},{8,0},{9,1},... | collective-permute-start | bytes 1572872 | tf_op jit(solution)/shard_map/ppermute | solution.py:256
  111.2 25.2 %collective-permute-start.22 = (bf16[256,1024]{1,0:T(8,128)(2,1)}, bf16[256,1024]{1,0:T(8,128)(2,1)}, u32[]{:S(2)}, u32[]{:S(2)}) collective-permute-start(bf16[256,1024]{1,0:T(8,128)(2,1)} %get-tuple-element.61), channel_id=1, source_target_pairs={{0,16},{1,17},{2,18},{3,19},{4,20},{5,21},{6,22},{7,23},{8,24},{9,... | collective-permute-start | bytes 1572872 | tf_op jit(solution)/shard_map/ppermute | solution.py:256
  129.1 19.8 %collective-permute-start.18 = (bf16[256,1024]{1,0:T(8,128)(2,1)}, bf16[256,1024]{1,0:T(8,128)(2,1)S(1)}, u32[]{:S(2)}, u32[]{:S(2)}) collective-permute-start(bf16[256,1024]{1,0:T(8,128)(2,1)} %get-tuple-element.56), channel_id=1, source_target_pairs={{0,12},{1,13},{2,14},{3,15},{4,8},{5,9},{6,10},{7,11},{8,4},{9,5},... | collective-permute-start | bytes 1572872 | tf_op jit(solution)/shard_map/ppermute | solution.py:256
  136.2 13.2 %collective-permute-start.19 = (bf16[256,1024]{1,0:T(8,128)(2,1)}, bf16[256,1024]{1,0:T(8,128)(2,1)S(1)}, u32[]{:S(2)}, u32[]{:S(2)}) collective-permute-start(bf16[256,1024]{1,0:T(8,128)(2,1)} %get-tuple-element.57), channel_id=1, source_target_pairs={{0,20},{1,21},{2,22},{3,23},{4,16},{5,17},{6,18},{7,19},{8,28},{9,... | collective-permute-start | bytes 1572872 | tf_op jit(solution)/shard_map/ppermute | solution.py:256
  136.3 13.1 %collective-permute-start.20 = (bf16[512,1024]{1,0:T(8,128)(2,1)}, bf16[512,1024]{1,0:T(8,128)(2,1)S(1)}, u32[]{:S(2)}, u32[]{:S(2)}) collective-permute-start(bf16[512,1024]{1,0:T(8,128)(2,1)} %get-tuple-element.58), channel_id=1, source_target_pairs={{0,4},{1,5},{2,6},{3,7},{4,0},{5,1},{6,2},{7,3},{8,12},{9,13},{10,... | collective-permute-start | bytes 3145736 | tf_op jit(solution)/shard_map/ppermute | solution.py:256
  (4 other events, 4.5 us)
